TPU v7x, 32 devices: a whole 2x2x4 slice. The times are simulated.
32 devices in a mesh: replica: 16 (over z, y, core), shard: 2 (over x).
Axes of the slice: x: 2, y: 2, z: 4, core: 2. Of those that a mesh axis runs over, the one named last changes fastest.
Arguments:
- tokens: bfloat16 [16384, 1024], P(('replica', 'shard')), may hold values from -6 to 6
- positions: int32 [16384], P(('replica', 'shard')), may hold values from 0 to 1534, as said below
- cotangent: bfloat16 [16384, 1024], P(('replica', 'shard')), may hold values from -6 to 6
- norm1_gain: bfloat16 [1024], P('shard'), may hold values from 0.099609375 to 1.8984375
- w_query: bfloat16 [1024, 2048], P('shard'), may hold values from -0.1875 to 0.1875
- w_key: bfloat16 [1024, 1024], P('shard'), may hold values from -0.1875 to 0.1875
- w_value: bfloat16 [1024, 1024], P('shard'), may hold values from -0.1875 to 0.1875
- w_out: bfloat16 [2048, 1024], P('shard'), may hold values from -1 to 1
- query_gain: bfloat16 [128], P('shard'), may hold values from 0.099609375 to 1.8984375
- key_gain: bfloat16 [128], P('shard'), may hold values from 0.099609375 to 1.8984375
- norm2_gain: bfloat16 [1024], P('shard'), may hold values from 0.099609375 to 1.8984375
- w_gate: bfloat16 [1024, 3072], P('shard'), may hold values from -0.1875 to 0.1875
- w_up: bfloat16 [1024, 3072], P('shard'), may hold values from -0.1875 to 0.1875
- w_down: bfloat16 [3072, 1024], P('shard'), may hold values from -0.109375 to 0.109375
Outputs:
- result: bfloat16 [16384, 1024], P(('replica', 'shard'))
- grad_input: float32 [16384, 1024], P(('replica', 'shard'))
- grad_norm1_gain: float32 [1024], P('shard')
- grad_w_query: float32 [1024, 2048], P('shard')
- grad_w_key: float32 [1024, 1024], P('shard')
- grad_w_value: float32 [1024, 1024], P('shard')
- grad_w_out: float32 [2048, 1024], P('shard')
- grad_query_gain: float32 [128], P('shard')
- grad_key_gain: float32 [128], P('shard')
- grad_norm2_gain: float32 [1024], P('shard')
- grad_w_gate: float32 [1024, 3072], P('shard')
- grad_w_up: float32 [1024, 3072], P('shard')
- grad_w_down: float32 [3072, 1024], P('shard')
Inputs may be any that keep to these rules, and one draw needn't show every extreme that they name: Within each sequence of 1024 tokens positions start at 0 and rise by 1 or 2 from each token to the next, by 2 exactly (1023) // 2 times.
All inputs are finite; a program needn't handle non-finite values.
Results may differ from a plain program's by a relative error of at most 0.023.
Values may be sent and summed in bfloat16 or wider, within the bound.
No kernel may reach another device: no remote copies, remote signals or barrier semaphores. Data moves between devices by JAX's collectives and lax.ppermute only.
A program may use at most 448 MiB of HBM per device.

v0:
```python
from functools import partial
import math

import jax
import jax.numpy as jnp
from jax import lax
from jax.sharding import PartitionSpec as P

EPS = 1e-06
THETA = 1000000.0
NEG = -1e30


def rms_scale(values):
    return lax.rsqrt(jnp.mean(values * values, axis=-1, keepdims=True) + EPS)


def norm_back(values, gain, incoming):
    scale = rms_scale(values)
    normed = values * scale
    scaled_in = incoming * gain
    return (
        scale * (scaled_in - normed * jnp.mean(scaled_in * normed, axis=-1, keepdims=True)),
        incoming * normed,
    )


def rotation_tables(places, width):
    half_width = width // 2
    freqs = THETA ** (-jnp.arange(half_width, dtype=jnp.float32) * 2.0 / width)
    angles = places.astype(jnp.float32)[:, None, None] * freqs
    return (jnp.cos(angles), jnp.sin(angles))


def rotate(values, cosine, sine_table):
    half_width = values.shape[-1] // 2
    first_half, second_half = (values[..., :half_width], values[..., half_width:])
    return jnp.concatenate(
        [
            first_half * cosine - second_half * sine_table,
            second_half * cosine + first_half * sine_table,
        ],
        axis=-1,
    )


def unrotate(grads, cosine, sine_table):
    half_width = grads.shape[-1] // 2
    first_half, second_half = (grads[..., :half_width], grads[..., half_width:])
    return jnp.concatenate(
        [
            first_half * cosine + second_half * sine_table,
            second_half * cosine - first_half * sine_table,
        ],
        axis=-1,
    )


def inner_rows(left, right):
    return lax.dot_general(
        left, right, (((0,), (0,)), ((), ())), preferred_element_type=jnp.float32
    )


def times_t(left, right):
    return lax.dot_general(
        left, right, (((1,), (1,)), ((), ())), preferred_element_type=jnp.float32
    )


def local(
    tokens,
    positions,
    cotangent,
    norm1_gain,
    w_query,
    w_key,
    w_value,
    w_out,
    query_gain,
    key_gain,
    norm2_gain,
    w_gate,
    w_up,
    w_down,
):
    row_count = tokens.shape[0]
    blocks = lax.axis_size("shard")
    own_index = lax.axis_index("shard")
    head_dim = query_gain.shape[0] * blocks
    attn_set = (
        lax.all_gather(norm1_gain, "shard", axis=0, tiled=True),
        lax.all_gather(w_query, "shard", axis=0, tiled=True),
        lax.all_gather(w_key, "shard", axis=0, tiled=True),
        lax.all_gather(w_value, "shard", axis=0, tiled=True),
        lax.all_gather(w_out, "shard", axis=0, tiled=True),
        lax.all_gather(query_gain, "shard", axis=0, tiled=True),
        lax.all_gather(key_gain, "shard", axis=0, tiled=True),
    )
    gain_one = attn_set[0].astype(jnp.float32)
    q_gain = attn_set[5].astype(jnp.float32)
    k_gain = attn_set[6].astype(jnp.float32)
    q_heads = attn_set[1].shape[1] // head_dim
    kv_heads = attn_set[2].shape[1] // head_dim
    group = q_heads // kv_heads
    inv_scale = 1.0 / math.sqrt(head_dim)
    cosine, sine_table = rotation_tables(positions, head_dim)
    x_float = tokens.astype(jnp.float32)
    h_one = (x_float * rms_scale(x_float) * gain_one).astype(jnp.bfloat16)
    q_proj = jnp.dot(h_one, attn_set[1], preferred_element_type=jnp.float32).reshape(
        row_count, q_heads, head_dim
    )
    k_proj = jnp.dot(h_one, attn_set[2], preferred_element_type=jnp.float32).reshape(
        row_count, kv_heads, head_dim
    )
    v_low = jnp.dot(h_one, attn_set[3], preferred_element_type=jnp.float32).astype(jnp.bfloat16)
    q_low = (rotate(q_proj * rms_scale(q_proj) * q_gain, cosine, sine_table) * inv_scale).astype(
        jnp.bfloat16
    )
    q_low = q_low.reshape(row_count, kv_heads, group, head_dim)
    k_low = rotate(k_proj * rms_scale(k_proj) * k_gain, cosine, sine_table).astype(jnp.bfloat16)
    k_low = k_low.reshape(row_count, kv_heads * head_dim)
    key_full, value_full = (
        lax.all_gather(k_low, "shard", axis=0, tiled=True),
        lax.all_gather(v_low, "shard", axis=0, tiled=True),
    )
    query_place = own_index * row_count + jnp.arange(row_count)

    def block_of(full, kblock):
        return full[kblock * row_count : (kblock + 1) * row_count].reshape(
            row_count, kv_heads, head_dim
        )

    def block_scores(keys_all, kblock):
        raw = jnp.einsum(
            "sngd,tnd->ngst", q_low, block_of(keys_all, kblock), preferred_element_type=jnp.float32
        )
        key_place = kblock * row_count + jnp.arange(row_count)
        return jnp.where(key_place[None, :] <= query_place[:, None], raw, NEG)

    empty_scores = jnp.full((kv_heads, group, row_count, row_count), NEG, jnp.float32)
    zero_scores = jnp.zeros((kv_heads, group, row_count, row_count), jnp.float32)
    zero_out = jnp.zeros((row_count, kv_heads, group, head_dim), jnp.float32)
    zero_keys = jnp.zeros((row_count, kv_heads, head_dim), jnp.float32)
    score_list = [
        lax.cond(kblock <= own_index, partial(block_scores, key_full, kblock), lambda: empty_scores)
        for kblock in range(blocks)
    ]
    score_all = jnp.concatenate(score_list, axis=-1)
    peak = jnp.max(score_all, axis=-1, keepdims=True)
    log_total = peak + jnp.log(jnp.sum(jnp.exp(score_all - peak), axis=-1, keepdims=True))
    probs_low = jnp.exp(score_all - log_total).astype(jnp.bfloat16)

    def block_output(kblock):
        part_probs = probs_low[..., kblock * row_count : (kblock + 1) * row_count]
        return jnp.einsum(
            "ngst,tnd->sngd",
            part_probs,
            block_of(value_full, kblock),
            preferred_element_type=jnp.float32,
        )

    attended = zero_out
    for kblock in range(blocks):
        attended = attended + lax.cond(
            kblock <= own_index, partial(block_output, kblock), lambda: zero_out
        )
    out_low = attended.reshape(row_count, q_heads * head_dim).astype(jnp.bfloat16)
    resid_one = x_float + jnp.dot(out_low, attn_set[4], preferred_element_type=jnp.float32)
    mlp_set = (
        lax.all_gather(norm2_gain, "shard", axis=0, tiled=True),
        lax.all_gather(w_gate, "shard", axis=0, tiled=True),
        lax.all_gather(w_up, "shard", axis=0, tiled=True),
        lax.all_gather(w_down, "shard", axis=0, tiled=True),
    )
    gain_two = mlp_set[0].astype(jnp.float32)
    h_two = (resid_one * rms_scale(resid_one) * gain_two).astype(jnp.bfloat16)
    gate = jnp.dot(h_two, mlp_set[1], preferred_element_type=jnp.float32)
    up_val = jnp.dot(h_two, mlp_set[2], preferred_element_type=jnp.float32)
    sigmoid_gate = jax.nn.sigmoid(gate)
    hidden_low = (gate * sigmoid_gate * up_val).astype(jnp.bfloat16)
    result = (
        resid_one + jnp.dot(hidden_low, mlp_set[3], preferred_element_type=jnp.float32)
    ).astype(jnp.bfloat16)
    mlp_back = (
        lax.all_gather(norm2_gain, "shard", axis=0, tiled=True),
        lax.all_gather(w_gate, "shard", axis=0, tiled=True),
        lax.all_gather(w_up, "shard", axis=0, tiled=True),
        lax.all_gather(w_down, "shard", axis=0, tiled=True),
    )
    grad_hidden = times_t(cotangent, mlp_back[3])
    grad_gate_low = (
        grad_hidden * up_val * sigmoid_gate * (1.0 + gate * (1.0 - sigmoid_gate))
    ).astype(jnp.bfloat16)
    grad_up_low = (grad_hidden * gate * sigmoid_gate).astype(jnp.bfloat16)
    grad_h_two = times_t(grad_gate_low, mlp_back[1]) + times_t(grad_up_low, mlp_back[2])
    resid_part, gain_two_terms = norm_back(resid_one, gain_two, grad_h_two)
    grad_resid = cotangent.astype(jnp.float32) + resid_part
    grad_down = inner_rows(hidden_low, cotangent)
    grad_gate_w = inner_rows(h_two, grad_gate_low)
    grad_up_w = inner_rows(h_two, grad_up_low)
    mlp_shares = (
        lax.psum_scatter(
            jnp.sum(gain_two_terms, axis=0).astype(jnp.bfloat16),
            "shard",
            scatter_dimension=0,
            tiled=True,
        ).astype(jnp.float32),
        lax.psum_scatter(
            grad_gate_w.astype(jnp.bfloat16), "shard", scatter_dimension=0, tiled=True
        ).astype(jnp.float32),
        lax.psum_scatter(
            grad_up_w.astype(jnp.bfloat16), "shard", scatter_dimension=0, tiled=True
        ).astype(jnp.float32),
        lax.psum_scatter(
            grad_down.astype(jnp.bfloat16), "shard", scatter_dimension=0, tiled=True
        ).astype(jnp.float32),
    )
    attn_back = (
        lax.all_gather(norm1_gain, "shard", axis=0, tiled=True),
        lax.all_gather(w_query, "shard", axis=0, tiled=True),
        lax.all_gather(w_key, "shard", axis=0, tiled=True),
        lax.all_gather(w_value, "shard", axis=0, tiled=True),
        lax.all_gather(w_out, "shard", axis=0, tiled=True),
        lax.all_gather(query_gain, "shard", axis=0, tiled=True),
        lax.all_gather(key_gain, "shard", axis=0, tiled=True),
    )
    resid_low = grad_resid.astype(jnp.bfloat16)
    grad_att_low = (
        times_t(resid_low, attn_back[4])
        .astype(jnp.bfloat16)
        .reshape(row_count, kv_heads, group, head_dim)
    )
    key_back, value_back = (key_full, value_full)

    def first_pass(kblock):
        part_probs = jnp.exp(block_scores(key_back, kblock) - log_total)
        part_dprobs = jnp.einsum(
            "sngd,tnd->ngst",
            grad_att_low,
            block_of(value_back, kblock),
            preferred_element_type=jnp.float32,
        )
        return (part_probs, part_dprobs)

    pass_list = [
        lax.cond(
            kblock <= own_index, partial(first_pass, kblock), lambda: (zero_scores, zero_scores)
        )
        for kblock in range(blocks)
    ]
    delta_sum = jnp.zeros((kv_heads, group, row_count, 1), jnp.float32)
    for part_probs, part_dprobs in pass_list:
        delta_sum = delta_sum + jnp.sum(part_probs * part_dprobs, axis=-1, keepdims=True)

    def second_pass(kblock):
        part_probs, part_dprobs = pass_list[kblock]
        dscore_low = (part_probs * (part_dprobs - delta_sum)).astype(jnp.bfloat16)
        query_term = jnp.einsum(
            "ngst,tnd->sngd",
            dscore_low,
            block_of(key_back, kblock),
            preferred_element_type=jnp.float32,
        )
        key_term = jnp.einsum(
            "ngst,sngd->tnd", dscore_low, q_low, preferred_element_type=jnp.float32
        )
        value_term = jnp.einsum(
            "ngst,sngd->tnd",
            part_probs.astype(jnp.bfloat16),
            grad_att_low,
            preferred_element_type=jnp.float32,
        )
        return (query_term, key_term, value_term)

    grad_query = zero_out
    key_terms = []
    value_terms = []
    for kblock in range(blocks):
        query_term, key_term, value_term = lax.cond(
            kblock <= own_index,
            partial(second_pass, kblock),
            lambda: (zero_out, zero_keys, zero_keys),
        )
        grad_query = grad_query + query_term
        key_terms.append(key_term.reshape(row_count, kv_heads * head_dim))
        value_terms.append(value_term.reshape(row_count, kv_heads * head_dim))
    grad_key_local, grad_value_local = (
        lax.psum_scatter(
            jnp.concatenate(key_terms, axis=0).astype(jnp.bfloat16),
            "shard",
            scatter_dimension=0,
            tiled=True,
        ).astype(jnp.float32),
        lax.psum_scatter(
            jnp.concatenate(value_terms, axis=0).astype(jnp.bfloat16),
            "shard",
            scatter_dimension=0,
            tiled=True,
        ).astype(jnp.float32),
    )
    grad_value_low = grad_value_local.astype(jnp.bfloat16)
    key_rot = unrotate(grad_key_local.reshape(row_count, kv_heads, head_dim), cosine, sine_table)
    key_proj_grad, key_gain_terms = norm_back(k_proj, k_gain, key_rot)
    grad_key_low = key_proj_grad.reshape(row_count, kv_heads * head_dim).astype(jnp.bfloat16)
    query_rot = unrotate(
        grad_query.reshape(row_count, q_heads, head_dim) * inv_scale, cosine, sine_table
    )
    query_proj_grad, query_gain_terms = norm_back(q_proj, q_gain, query_rot)
    grad_query_low = query_proj_grad.reshape(row_count, q_heads * head_dim).astype(jnp.bfloat16)
    grad_h_one = (
        times_t(grad_query_low, attn_back[1])
        + times_t(grad_key_low, attn_back[2])
        + times_t(grad_value_low, attn_back[3])
    )
    input_part, gain_one_terms = norm_back(x_float, gain_one, grad_h_one)
    grad_input = grad_resid + input_part
    gain_one_sum = jnp.sum(gain_one_terms, axis=0)
    query_gain_sum = jnp.sum(query_gain_terms, axis=(0, 1))
    key_gain_sum = jnp.sum(key_gain_terms, axis=(0, 1))
    grad_out_w = inner_rows(out_low, resid_low)
    grad_query_w = inner_rows(h_one, grad_query_low)
    grad_key_w = inner_rows(h_one, grad_key_low)
    grad_value_w = inner_rows(h_one, grad_value_low)
    attn_shares = (
        lax.psum_scatter(
            gain_one_sum.astype(jnp.bfloat16), "shard", scatter_dimension=0, tiled=True
        ).astype(jnp.float32),
        lax.psum_scatter(
            grad_query_w.astype(jnp.bfloat16), "shard", scatter_dimension=0, tiled=True
        ).astype(jnp.float32),
        lax.psum_scatter(
            grad_key_w.astype(jnp.bfloat16), "shard", scatter_dimension=0, tiled=True
        ).astype(jnp.float32),
        lax.psum_scatter(
            grad_value_w.astype(jnp.bfloat16), "shard", scatter_dimension=0, tiled=True
        ).astype(jnp.float32),
        lax.psum_scatter(
            grad_out_w.astype(jnp.bfloat16), "shard", scatter_dimension=0, tiled=True
        ).astype(jnp.float32),
        lax.psum_scatter(
            query_gain_sum.astype(jnp.bfloat16), "shard", scatter_dimension=0, tiled=True
        ).astype(jnp.float32),
        lax.psum_scatter(
            key_gain_sum.astype(jnp.bfloat16), "shard", scatter_dimension=0, tiled=True
        ).astype(jnp.float32),
    )
    totals = (
        lax.psum(attn_shares[0].astype(jnp.bfloat16), "replica").astype(jnp.float32),
        lax.psum(attn_shares[1].astype(jnp.bfloat16), "replica").astype(jnp.float32),
        lax.psum(attn_shares[2].astype(jnp.bfloat16), "replica").astype(jnp.float32),
        lax.psum(attn_shares[3].astype(jnp.bfloat16), "replica").astype(jnp.float32),
        lax.psum(attn_shares[4].astype(jnp.bfloat16), "replica").astype(jnp.float32),
        lax.psum(attn_shares[5].astype(jnp.bfloat16), "replica").astype(jnp.float32),
        lax.psum(attn_shares[6].astype(jnp.bfloat16), "replica").astype(jnp.float32),
        lax.psum(mlp_shares[0].astype(jnp.bfloat16), "replica").astype(jnp.float32),
        lax.psum(mlp_shares[1].astype(jnp.bfloat16), "replica").astype(jnp.float32),
        lax.psum(mlp_shares[2].astype(jnp.bfloat16), "replica").astype(jnp.float32),
        lax.psum(mlp_shares[3].astype(jnp.bfloat16), "replica").astype(jnp.float32),
    )
    return (
        result,
        grad_input,
        totals[0],
        totals[1],
        totals[2],
        totals[3],
        totals[4],
        totals[5],
        totals[6],
        totals[7],
        totals[8],
        totals[9],
        totals[10],
    )


def solution(mesh):
    return jax.shard_map(
        local,
        mesh=mesh,
        in_specs=(
            P(("replica", "shard"), None),
            P(("replica", "shard")),
            P(("replica", "shard"), None),
            P("shard"),
            P("shard", None),
            P("shard", None),
            P("shard", None),
            P("shard", None),
            P("shard"),
            P("shard"),
            P("shard"),
            P("shard", None),
            P("shard", None),
            P("shard", None),
        ),
        out_specs=(
            P(("replica", "shard"), None),
            P(("replica", "shard"), None),
            P("shard"),
            P("shard", None),
            P("shard", None),
            P("shard", None),
            P("shard", None),
            P("shard"),
            P("shard"),
            P("shard"),
            P("shard", None),
            P("shard", None),
            P("shard", None),
        ),
        check_vma=False,
    )
```

profile of v0, /device:TPU:0, one launch (start us, length us, event | category | flops | bytes accessed | tf_op | source)
XLA Modules:
  0.0 1559.7 jit_solution(13807052646778097941)
XLA Ops:
  22.9 22.6 %all-gather.16.cloned.1.call-done = bf16[1024,1024]{1,0:T(8,128)(2,1)} async-done(((bf16[512,1024]{1,0:T(8,128)(2,1)}), bf16[1024,1024]{1,0:T(8,128)(2,1)}) %all-gather.16.cloned.1.call-update) | async-done | bytes 2097168 | tf_op jit(solution)/shard_map/all_gather | solution.py:94
  54.2 26.0 %all-gather.12.cloned.1.call-done = bf16[1024,1024]{1,0:T(8,128)(2,1)} async-done(((bf16[512,1024]{1,0:T(8,128)(2,1)}), bf16[1024,1024]{1,0:T(8,128)(2,1)}) %all-gather.12.cloned.1.call-update) | async-done | bytes 2097168 | tf_op jit(solution)/shard_map/all_gather | solution.py:95
  91.5 47.0 %all-gather.20.cloned.1.call-done = bf16[1024,2048]{1,0:T(8,128)(2,1)} async-done(((bf16[512,2048]{1,0:T(8,128)(2,1)}), bf16[1024,2048]{1,0:T(8,128)(2,1)}) %all-gather.20.cloned.1.call-update) | async-done | bytes 4194320 | tf_op jit(solution)/shard_map/all_gather | solution.py:93
  155.0 18.7 %all-gather.18.cloned.1.call-done = bf16[1024,1024]{0,1:T(8,128)(2,1)} async-done(((bf16[512,1024]{0,1:T(8,128)(2,1)}), bf16[1024,1024]{0,1:T(8,128)(2,1)}) %all-gather.18.cloned.1.call-update) | async-done | bytes 2097168 | tf_op jit(solution)/shard_map/all_gather | solution.py:124
  182.0 17.8 %copy.121 = f32[8,2,512,512]{3,2,1,0:T(8,128)} copy(f32[8,2,512,512]{2,3,1,0:T(8,128)} %get-tuple-element.349) | data formatting | bytes 33554432 | tf_op jit(solution)/shard_map/cond | solution.py:146
  209.5 17.9 %copy.120 = f32[8,2,512,512]{3,2,1,0:T(8,128)} copy(f32[8,2,512,512]{2,3,1,0:T(8,128)} %get-tuple-element.348) | data formatting | bytes 33554432 | tf_op jit(solution)/shard_map/cond | solution.py:146
  305.0 43.9 %all-gather.24.cloned.1.call-done = bf16[1024,3072]{1,0:T(8,128)(2,1)} async-done(((bf16[512,3072]{1,0:T(8,128)(2,1)}), bf16[1024,3072]{1,0:T(8,128)(2,1)}) %all-gather.24.cloned.1.call-update) | async-done | bytes 6291472 | tf_op jit(solution)/shard_map/all_gather | solution.py:172
  357.0 73.9 %all-gather.26.cloned.1.call-done = bf16[1024,3072]{1,0:T(8,128)(2,1)} async-done(((bf16[512,3072]{1,0:T(8,128)(2,1)}), bf16[1024,3072]{1,0:T(8,128)(2,1)}) %all-gather.26.cloned.1.call-update) | async-done | bytes 6291472 | tf_op jit(solution)/shard_map/all_gather | solution.py:173
  438.9 73.9 %all-gather.28.cloned.1.call-done = bf16[3072,1024]{1,0:T(8,128)(2,1)} async-done(((bf16[1536,1024]{1,0:T(8,128)(2,1)}), bf16[3072,1024]{1,0:T(8,128)(2,1)}) %all-gather.28.cloned.1.call-update) | async-done | bytes 6291472 | tf_op jit(solution)/shard_map/all_gather | solution.py:174
  564.6 23.2 %conditional.12 = (f32[8,2,512,512]{2,3,1,0:T(8,128)}, f32[8,2,512,512]{2,3,1,0:T(8,128)}) conditional(s32[]{:T(128)} %convert_element_type.190, () %tuple.79, (s32[512]{0:T(512)S(1)}, bf16[1024,1024]{0,1:T(8,128)(2,1)}, bf16[512,8,2,128]{3,0,2,1:T(8,128)(2,1)S(1)}, f32[8,2,512,1]{2,1,0,3:T(2,128)S(1)}, bf16[1024,1024]{1,0:T(8,128)(2,1)}, ...), branch_computations={%region_16.17_spmd, %region_17.18_spmd} | conditional | flops 2156134400 | bytes 57182252 | solution.py:247
  587.9 22.3 %multiply_reduce_fusion = (f32[8,2,512]{2,1,0:T(2,128)S(1)}, f32[8,2,512]{2,1,0:T(2,128)S(1)}) fusion(f32[8,2,512,512]{2,3,1,0:T(8,128)} %get-tuple-element.143, f32[8,2,512,512]{2,3,1,0:T(8,128)} %copy-done, f32[8,2,512,512]{2,3,1,0:T(8,128)} %get-tuple-element.141, f32[8,2,512,512]{2,3,1,0:T(8,128)} %get-tuple-element.142), kind=kLoop, calls=%fused_computation.41 | loop fusion | flops 16760832 | bytes 67174400 | tf_op jit(solution)/shard_map/reduce_sum | solution.py:254
  619.1 65.9 %conditional.14 = (f32[512,8,2,128]{3,0,2,1:T(8,128)}, bf16[512,1024]{0,1:T(8,128)(2,1)}, bf16[512,1024]{0,1:T(8,128)(2,1)}) conditional(s32[]{:T(128)} %convert_element_type.190, () %tuple.78, (f32[8,2,512,1]{2,1,0,3:T(2,128)S(1)}, f32[8,2,512,512]{2,3,1,0:T(8,128)}, f32[8,2,512,512]{2,3,1,0:T(8,128)}, bf16[1024,1024]{0,1:T(8,128)(2,1)}, ...), branch_computations={%region_22.23_spmd, %region_23.24_spmd} | conditional | flops 3239051264 | bytes 206602368 | solution.py:280
  619.2 17.5 %copy.129 = f32[8,2,512,512]{3,2,1,0:T(8,128)} copy(f32[8,2,512,512]{2,3,1,0:T(8,128)} %get-tuple-element.257) | data formatting | bytes 33554432 | tf_op jit(solution)/shard_map
  636.7 17.5 %copy.128 = f32[8,2,512,512]{3,2,1,0:T(8,128)} copy(f32[8,2,512,512]{2,3,1,0:T(8,128)} %get-tuple-element.256) | data formatting | bytes 33554432 | tf_op jit(solution)/shard_map
  722.3 61.4 %reduce-scatter.10.cloned.1.call-done = bf16[512,1024]{0,1:T(8,128)(2,1)} async-done(((bf16[1024,1024]{0,1:T(8,128)(2,1)}), bf16[512,1024]{0,1:T(8,128)(2,1)}) %reduce-scatter.10.cloned.1.call-update) | async-done | bytes 1048592 | tf_op jit(solution)/shard_map/reduce_scatter | solution.py:289
  853.1 22.5 %reduce-scatter.14.cloned.1.call-done = bf16[512,2048]{1,0:T(8,128)(2,1)} async-done(((bf16[1024,2048]{1,0:T(8,128)(2,1)}), bf16[512,2048]{1,0:T(8,128)(2,1)}) %reduce-scatter.14.cloned.1.call-update) | async-done | bytes 2097168 | tf_op jit(solution)/shard_map/reduce_scatter | solution.py:329
  875.5 34.2 %reduce-scatter.16.cloned.1.call-done = bf16[512,1024]{1,0:T(8,128)(2,1)} async-done(((bf16[1024,1024]{1,0:T(8,128)(2,1)}), bf16[512,1024]{1,0:T(8,128)(2,1)}) %reduce-scatter.16.cloned.1.call-update) | async-done | bytes 1048592 | tf_op jit(solution)/shard_map/reduce_scatter | solution.py:332
  909.8 34.0 %reduce-scatter.18.cloned.1.call-done = bf16[512,1024]{1,0:T(8,128)(2,1)} async-done(((bf16[1024,1024]{1,0:T(8,128)(2,1)}), bf16[512,1024]{1,0:T(8,128)(2,1)}) %reduce-scatter.18.cloned.1.call-update) | async-done | bytes 1048592 | tf_op jit(solution)/shard_map/reduce_scatter | solution.py:335
  943.7 57.2 %reduce-scatter.20.cloned.1.call-done = bf16[1024,1024]{1,0:T(8,128)(2,1)} async-done(((bf16[2048,1024]{1,0:T(8,128)(2,1)}), bf16[1024,1024]{1,0:T(8,128)(2,1)}) %reduce-scatter.20.cloned.1.call-update) | async-done | bytes 2097168 | tf_op jit(solution)/shard_map/reduce_scatter | solution.py:338
  1000.9 79.8 %reduce-scatter.22.cloned.1.call-done = bf16[512,3072]{1,0:T(8,128)(2,1)} async-done(((bf16[1024,3072]{1,0:T(8,128)(2,1)}), bf16[512,3072]{1,0:T(8,128)(2,1)}) %reduce-scatter.22.cloned.1.call-update) | async-done | bytes 3145744 | tf_op jit(solution)/shard_map/reduce_scatter | solution.py:209
  1080.7 79.9 %reduce-scatter.24.cloned.1.call-done = bf16[512,3072]{1,0:T(8,128)(2,1)} async-done(((bf16[1024,3072]{1,0:T(8,128)(2,1)}), bf16[512,3072]{1,0:T(8,128)(2,1)}) %reduce-scatter.24.cloned.1.call-update) | async-done | bytes 3145744 | tf_op jit(solution)/shard_map/reduce_scatter | solution.py:212
  1160.6 79.8 %reduce-scatter.26.cloned.1.call-done = bf16[1536,1024]{1,0:T(8,128)(2,1)} async-done(((bf16[3072,1024]{1,0:T(8,128)(2,1)}), bf16[1536,1024]{1,0:T(8,128)(2,1)}) %reduce-scatter.26.cloned.1.call-update) | async-done | bytes 3145744 | tf_op jit(solution)/shard_map/reduce_scatter | solution.py:215
  1265.0 35.1 %all-reduce.6 = (bf16[512]{0:T(512)(128)(2,1)S(1)}, bf16[64]{0:T(256)(128)(2,1)S(1)}, bf16[64]{0:T(256)(128)(2,1)S(1)}, bf16[512]{0:T(512)(128)(2,1)S(1)}) all-reduce(bf16[512]{0:T(512)(128)(2,1)S(1)} %dynamic-slice.3, bf16[64]{0:T(256)(128)(2,1)S(1)} %dynamic-slice.5, ...), channel_id=1, replica_groups=mesh['replica'=16,'shard'=2] {'replica'}, use_global_device_ids=true, to_apply=%region_33.34 | all-reduce | flops 1152 | bytes 4608 | tf_op jit(solution)/shard_map/psum | solution.py:349
  1305.8 226.7 %all-reduce.12.cloned.1.call-done = (bf16[512,2048]{1,0:T(8,128)(2,1)}, bf16[512,1024]{1,0:T(8,128)(2,1)}, bf16[512,1024]{1,0:T(8,128)(2,1)}, bf16[1024,1024]{1,...) async-done(((bf16[512,2048]{1,0:T(8,128)(2,1)}, bf16[512,1024]{1,0:T(8,128)(2,1)}, bf16[512,1024]{1,0:T(8,128)(2,1)}, ...) | async-done | bytes 15728656 | tf_op jit(solution)/shard_map/psum | solution.py:350
  (324 shorter events, 481.4 us)
Async XLA Ops:
  7.2 38.2 %all-gather.16.cloned.1.call-start = ((), (), s32[]{:S(2)}) async-start(), calls=%async_computation.11 | async-start | bytes 3145728 | tf_op jit(solution)/shard_map/all_gather | solution.py:94
  8.0 72.2 %all-gather.12.cloned.1.call-start = ((), (), s32[]{:S(2)}) async-start(), calls=%async_computation.9 | async-start | bytes 3145728 | tf_op jit(solution)/shard_map/all_gather | solution.py:95
  8.7 129.8 %all-gather.20.cloned.1.call-start = ((), (), s32[]{:S(2)}) async-start(), calls=%async_computation.13 | async-start | bytes 6291456 | tf_op jit(solution)/shard_map/all_gather | solution.py:93
  9.5 164.2 %all-gather.18.cloned.1.call-start = ((), (), s32[]{:S(2)}) async-start(), calls=%async_computation.12 | async-start | bytes 3145728 | tf_op jit(solution)/shard_map/all_gather | solution.py:124
  14.8 123.8 %copy-start.48 = (f32[2,1,512]{2,1,0:T(1,128)}, f32[2,1,512]{2,1,0:T(1,128)S(1)}, u32[]{:S(2)}) copy-start(f32[2,1,512]{2,1,0:T(1,128)S(1)} %convert_element_type.236) | copy-start | bytes 12292
  21.8 116.7 %copy-start.50 = (f32[512]{0:T(512)}, f32[512]{0:T(512)S(1)}, u32[]{:S(2)}) copy-start(f32[512]{0:T(512)S(1)} %add_rsqrt_fusion.3) | copy-start | bytes 6148
  22.8 127.0 %copy-start.23 = (f32[512,64]{1,0:T(8,128)}, f32[512,64]{1,0:T(8,128)S(1)}, u32[]{:S(2)}) copy-start(f32[512,64]{1,0:T(8,128)S(1)} %get-tuple-element.311) | copy-start | bytes 393220
  22.8 127.0 %copy-start.25 = (f32[512,64]{1,0:T(8,128)}, f32[512,64]{1,0:T(8,128)S(1)}, u32[]{:S(2)}) copy-start(f32[512,64]{1,0:T(8,128)S(1)} %get-tuple-element.312) | copy-start | bytes 393220
  54.2 221.3 %all-gather.14.cloned.1.call-start = ((), (), s32[]{:S(2)}) async-start(), calls=%async_computation.10 | async-start | bytes 3145728 | tf_op jit(solution)/shard_map/all_gather | solution.py:125
  84.1 214.1 %all-gather.22.cloned.1.call-start = ((), (), s32[]{:S(2)}) async-start(), calls=%async_computation.14 | async-start | bytes 6291456 | tf_op jit(solution)/shard_map/all_gather | solution.py:96
  84.7 264.2 %all-gather.24.cloned.1.call-start = ((), (), s32[]{:S(2)}) async-start(), calls=%async_computation.15 | async-start | bytes 9437184 | tf_op jit(solution)/shard_map/all_gather | solution.py:172
  85.4 345.4 %all-gather.26.cloned.1.call-start = ((), (), s32[]{:S(2)}) async-start(), calls=%async_computation.16 | async-start | bytes 9437184 | tf_op jit(solution)/shard_map/all_gather | solution.py:173
  86.2 426.7 %all-gather.28.cloned.1.call-start = ((), (), s32[]{:S(2)}) async-start(), calls=%async_computation.17 | async-start | bytes 9437184 | tf_op jit(solution)/shard_map/all_gather | solution.py:174
  86.9 696.8 %reduce-scatter.10.cloned.1.call-start = ((), (), s32[]{:S(2)}) async-start(), calls=%async_computation.18 | async-start | bytes 3145728 | tf_op jit(solution)/shard_map/reduce_scatter | solution.py:289
  305.0 125.8 %copy-start.42 = (bf16[512,1024]{1,0:T(8,128)(2,1)}, bf16[512,1024]{1,0:T(8,128)(2,1)S(1)}, u32[]{:S(2)}) copy-start(bf16[512,1024]{1,0:T(8,128)(2,1)S(1)} %multiply_convert_fusion.5) | copy-start | bytes 3145732
  688.0 130.5 %reduce-scatter.12.cloned.1.call-start = ((), (), s32[]{:S(2)}) async-start(), calls=%async_computation.19 | async-start | bytes 3145728 | tf_op jit(solution)/shard_map/reduce_scatter | solution.py:295
  691.2 184.4 %reduce-scatter.14.cloned.1.call-start = ((), (), s32[]{:S(2)}) async-start(), calls=%async_computation.20 | async-start | bytes 6291456 | tf_op jit(solution)/shard_map/reduce_scatter | solution.py:329
  721.7 188.1 %reduce-scatter.16.cloned.1.call-start = ((), (), s32[]{:S(2)}) async-start(), calls=%async_computation.21 | async-start | bytes 3145728 | tf_op jit(solution)/shard_map/reduce_scatter | solution.py:332
  804.2 139.5 %reduce-scatter.18.cloned.1.call-start = ((), (), s32[]{:S(2)}) async-start(), calls=%async_computation.22 | async-start | bytes 3145728 | tf_op jit(solution)/shard_map/reduce_scatter | solution.py:335
  822.5 178.3 %reduce-scatter.20.cloned.1.call-start = ((), (), s32[]{:S(2)}) async-start(), calls=%async_computation.23 | async-start | bytes 6291456 | tf_op jit(solution)/shard_map/reduce_scatter | solution.py:338
  828.6 252.1 %reduce-scatter.22.cloned.1.call-start = ((), (), s32[]{:S(2)}) async-start(), calls=%async_computation.24 | async-start | bytes 9437184 | tf_op jit(solution)/shard_map/reduce_scatter | solution.py:209
  837.0 323.6 %reduce-scatter.24.cloned.1.call-start = ((), (), s32[]{:S(2)}) async-start(), calls=%async_computation.25 | async-start | bytes 9437184 | tf_op jit(solution)/shard_map/reduce_scatter | solution.py:212
  844.6 395.8 %reduce-scatter.26.cloned.1.call-start = ((), (), s32[]{:S(2)}) async-start(), calls=%async_computation.26 | async-start | bytes 9437184 | tf_op jit(solution)/shard_map/reduce_scatter | solution.py:215
  853.0 679.5 %all-reduce.12.cloned.1.call-start = ((), (), s32[]{:S(2)}) async-start(), calls=%async_computation.27 | async-start | bytes 31457280 | tf_op jit(solution)/shard_map/psum | solution.py:350
  (66 other events, 475.5 us)
Sparse Core Ops, SparseCore 0:
  9.6 35.7 all-gather.15
  47.0 33.1 all-gather.11
  81.8 56.7 all-gather.19
  140.5 33.1 all-gather.17
  175.6 33.1 all-gather.13
  210.2 56.7 all-gather.21
  268.5 80.3 all-gather.23
  350.5 80.3 all-gather.25
  432.4 80.3 all-gather.27
  688.1 95.5 reduce-scatter.9
  786.6 31.8 reduce-scatter.11
  821.2 54.2 reduce-scatter.13
  877.9 31.8 reduce-scatter.15
  911.9 31.8 reduce-scatter.17
  946.5 54.3 reduce-scatter.19
  1003.6 77.0 reduce-scatter.21
  1083.5 77.0 reduce-scatter.23
  1163.3 77.0 reduce-scatter.25
  1246.9 285.5 all-reduce.11
where the time goes:
time: 1570 us; the launch traced here: 1560 us
  waiting for transfers between devices  1000 us (64%)
  matrix products  167 us (11%)
  other arithmetic  158 us (10%)
  local copies, waits for them, and re-layouts  155 us (10%)
  blocking collectives  54.8 us (3%)
  between operations  17.2 us (1%)
    psum x1, waiting for transfers between devices, local(): lax.psum(attn_shares[1].astype(jnp.bfloat16), 'replica').astype(jnp.float32)  227 us
    reduce_scatter x1, waiting for transfers between devices, local(): lax.psum_scatter(grad_up_w.astype(jnp.bfloat16), 'shard', scatter_dimensi...  79.9 us
    reduce_scatter x1, waiting for transfers between devices, local(): lax.psum_scatter(grad_down.astype(jnp.bfloat16), 'shard', scatter_dimensi...  79.8 us
    reduce_scatter x1, waiting for transfers between devices, local(): lax.psum_scatter(grad_gate_w.astype(jnp.bfloat16), 'shard', scatter_dimen...  79.8 us
    all_gather x1, waiting for transfers between devices, local(): lax.all_gather(w_down, 'shard', axis=0, tiled=True)  73.9 us
    all_gather x1, waiting for transfers between devices, local(): lax.all_gather(w_up, 'shard', axis=0, tiled=True)  73.9 us
    reduce_scatter x1, waiting for transfers between devices, local(): lax.psum_scatter(jnp.concatenate(key_terms, axis=0).astype(jnp.bfloat16),...  61.4 us
    reduce_scatter x1, waiting for transfers between devices, local(): lax.psum_scatter(grad_out_w.astype(jnp.bfloat16), 'shard', scatter_dimens...  57.2 us
  transfers between devices with their start and end apart: 19, of which 17 were waited for; matrix products, arithmetic and copies ran while one was open for 18% of the time, Pallas kernels for 0%

commit v1 on v0

--- a/solution.py
+++ b/solution.py
@@ -4,11 +4,15 @@
 import jax
 import jax.numpy as jnp
 from jax import lax
-from jax.sharding import PartitionSpec as P
+from jax.experimental import pallas as pl
+from jax.experimental.pallas import tpu as pltpu
+from jax.sharding import Mesh, PartitionSpec as P
 
 EPS = 1e-06
 THETA = 1000000.0
 NEG = -1e30
+QUERY_BLOCK = 256
+VMEM_BYTES = 56 * 1024 * 1024
 
 
 def rms_scale(values):
@@ -375,40 +379,495 @@
     )
 
 
+def head_norm(values, gain):
+    scale = lax.rsqrt(jnp.mean(values * values, axis=-1, keepdims=True) + EPS)
+    return values * scale * gain
+
+
+def attend_kernel(
+    qp_ref, kp_ref, v_ref, cos_ref, sin_ref, qg_ref, kg_ref, o_ref, q_ref, k_ref, lse_ref
+):
+    span, head_dim = kp_ref.shape
+    group = qp_ref.shape[1] // head_dim
+    block = min(QUERY_BLOCK, span)
+    cosine, sine = cos_ref[...], sin_ref[...]
+    keyed = head_norm(kp_ref[...], kg_ref[...])
+    key_low = (keyed * cosine + pltpu.roll(keyed, head_dim // 2, 1) * sine).astype(jnp.bfloat16)
+    k_ref[...] = key_low
+    value_t = v_ref[...].T
+    ahead = lax.broadcasted_iota(jnp.int32, (block, block), 0) > lax.broadcasted_iota(
+        jnp.int32, (block, block), 1
+    )
+    for head in range(group):
+        lanes = slice(head * head_dim, (head + 1) * head_dim)
+        asked = head_norm(qp_ref[:, lanes], qg_ref[...])
+        asked = asked * cosine + pltpu.roll(asked, head_dim // 2, 1) * sine
+        query_low = (asked * (1.0 / math.sqrt(head_dim))).astype(jnp.bfloat16)
+        q_ref[:, lanes] = query_low
+        for start in range(0, span, block):
+            stop = start + block
+            scores = times_t(key_low[:stop], query_low[start:stop])
+            last = jnp.where(ahead, NEG, scores[start:])
+            scores = last if start == 0 else jnp.concatenate([scores[:start], last], axis=0)
+            peak = jnp.max(scores, axis=0, keepdims=True)
+            powers = jnp.exp(scores - peak)
+            total = jnp.sum(powers, axis=0, keepdims=True)
+            lse_ref[0, head : head + 1, start:stop] = peak + jnp.log(total)
+            probs = (powers * (1.0 / total)).astype(jnp.bfloat16)
+            out_t = jnp.dot(value_t[:, :stop], probs, preferred_element_type=jnp.float32)
+            o_ref[start:stop, lanes] = out_t.T.astype(jnp.bfloat16)
+
+
+def attend_back_kernel(
+    q_ref,
+    k_ref,
+    v_ref,
+    do_ref,
+    lse_ref,
+    qp_ref,
+    kp_ref,
+    cos_ref,
+    sin_ref,
+    qg_ref,
+    kg_ref,
+    dq_ref,
+    dk_ref,
+    dv_ref,
+    gain_ref,
+    key_acc,
+    value_acc,
+):
+    span, head_dim = kp_ref.shape
+    group = qp_ref.shape[1] // head_dim
+    block = min(QUERY_BLOCK, span)
+    inv_scale = 1.0 / math.sqrt(head_dim)
+    key_low, value_low = k_ref[...], v_ref[...]
+    key_t = key_low.T
+    ahead = lax.broadcasted_iota(jnp.int32, (block, block), 0) > lax.broadcasted_iota(
+        jnp.int32, (block, block), 1
+    )
+
+    def proj_back(grads, proj, cosine, sine, gain):
+        turned = grads * cosine - pltpu.roll(grads, head_dim // 2, 1) * sine
+        scale = lax.rsqrt(jnp.mean(proj * proj, axis=-1, keepdims=True) + EPS)
+        normed = proj * scale
+        scaled = turned * gain
+        back = scale * (scaled - normed * jnp.mean(scaled * normed, axis=-1, keepdims=True))
+        return back, jnp.sum(turned * normed, axis=0, keepdims=True)
+
+    key_acc[...] = jnp.zeros_like(key_acc)
+    value_acc[...] = jnp.zeros_like(value_acc)
+    query_gain = jnp.zeros((1, head_dim), jnp.float32)
+    for head in range(group):
+        lanes = slice(head * head_dim, (head + 1) * head_dim)
+        for start in range(0, span, block):
+            stop = start + block
+            rows = slice(start, stop)
+            query_low, grad_out = q_ref[rows, lanes], do_ref[rows, lanes]
+            scores = times_t(key_low[:stop], query_low)
+            last = jnp.where(ahead, NEG, scores[start:])
+            scores = last if start == 0 else jnp.concatenate([scores[:start], last], axis=0)
+            probs = jnp.exp(scores - lse_ref[0, head : head + 1, rows])
+            dprobs = times_t(value_low[:stop], grad_out)
+            delta = jnp.sum(probs * dprobs, axis=0, keepdims=True)
+            dscore = (probs * (dprobs - delta)).astype(jnp.bfloat16)
+            value_acc[:stop, :] += jnp.dot(
+                probs.astype(jnp.bfloat16), grad_out, preferred_element_type=jnp.float32
+            )
+            key_acc[:stop, :] += jnp.dot(dscore, query_low, preferred_element_type=jnp.float32)
+            grad_query = jnp.dot(key_t[:, :stop], dscore, preferred_element_type=jnp.float32).T
+            back, gain_term = proj_back(
+                grad_query * inv_scale,
+                qp_ref[rows, lanes],
+                cos_ref[rows, :],
+                sin_ref[rows, :],
+                qg_ref[...],
+            )
+            dq_ref[rows, lanes] = back.astype(jnp.bfloat16)
+            query_gain = query_gain + gain_term
+    back, key_gain = proj_back(key_acc[...], kp_ref[...], cos_ref[...], sin_ref[...], kg_ref[...])
+    dk_ref[...] = back.astype(jnp.bfloat16)
+    dv_ref[...] = value_acc[...].astype(jnp.bfloat16)
+    gain_ref[0] = jnp.concatenate(
+        [query_gain, key_gain, jnp.zeros((gain_ref.shape[1] - 2, head_dim), jnp.float32)], axis=0
+    )
+
+
+def attend(q_proj, k_proj, value_low, cosine, sine, q_gain, k_gain):
+    span, q_width = q_proj.shape
+    kv_width = k_proj.shape[1]
+    head_dim = q_gain.shape[1]
+    heads, group = kv_width // head_dim, q_width // kv_width
+    q_spec = pl.BlockSpec((span, group * head_dim), lambda head: (0, head))
+    k_spec = pl.BlockSpec((span, head_dim), lambda head: (0, head))
+    table = pl.BlockSpec((span, head_dim), lambda head: (0, 0))
+    gain = pl.BlockSpec((1, head_dim), lambda head: (0, 0))
+    return pl.pallas_call(
+        attend_kernel,
+        grid=(heads,),
+        in_specs=[q_spec, k_spec, k_spec, table, table, gain, gain],
+        out_specs=[q_spec, q_spec, k_spec, pl.BlockSpec((1, group, span), lambda h: (h, 0, 0))],
+        out_shape=[
+            jax.ShapeDtypeStruct((span, q_width), jnp.bfloat16),
+            jax.ShapeDtypeStruct((span, q_width), jnp.bfloat16),
+            jax.ShapeDtypeStruct((span, kv_width), jnp.bfloat16),
+            jax.ShapeDtypeStruct((heads, group, span), jnp.float32),
+        ],
+        compiler_params=pltpu.CompilerParams(vmem_limit_bytes=VMEM_BYTES),
+        cost_estimate=pl.CostEstimate(
+            flops=2 * span * span * q_width * 2,
+            bytes_accessed=span * (q_width * 8 + kv_width * 8),
+            transcendentals=span * span * heads * group // 2,
+        ),
+        name="attend",
+    )(q_proj, k_proj, value_low, cosine, sine, q_gain, k_gain)
+
+
+def attend_back(
+    query_low, key_low, value_low, grad_out, lse, q_proj, k_proj, cosine, sine, q_gain, k_gain
+):
+    span, q_width = q_proj.shape
+    kv_width = k_proj.shape[1]
+    head_dim = q_gain.shape[1]
+    heads, group = kv_width // head_dim, q_width // kv_width
+    q_spec = pl.BlockSpec((span, group * head_dim), lambda head: (0, head))
+    k_spec = pl.BlockSpec((span, head_dim), lambda head: (0, head))
+    table = pl.BlockSpec((span, head_dim), lambda head: (0, 0))
+    gain = pl.BlockSpec((1, head_dim), lambda head: (0, 0))
+    return pl.pallas_call(
+        attend_back_kernel,
+        grid=(heads,),
+        in_specs=[
+            q_spec,
+            k_spec,
+            k_spec,
+            q_spec,
+            pl.BlockSpec((1, group, span), lambda h: (h, 0, 0)),
+            q_spec,
+            k_spec,
+            table,
+            table,
+            gain,
+            gain,
+        ],
+        out_specs=[q_spec, k_spec, k_spec, pl.BlockSpec((1, 8, head_dim), lambda h: (h, 0, 0))],
+        out_shape=[
+            jax.ShapeDtypeStruct((span, q_width), jnp.bfloat16),
+            jax.ShapeDtypeStruct((span, kv_width), jnp.bfloat16),
+            jax.ShapeDtypeStruct((span, kv_width), jnp.bfloat16),
+            jax.ShapeDtypeStruct((heads, 8, head_dim), jnp.float32),
+        ],
+        scratch_shapes=[
+            pltpu.VMEM((span, head_dim), jnp.float32),
+            pltpu.VMEM((span, head_dim), jnp.float32),
+        ],
+        compiler_params=pltpu.CompilerParams(vmem_limit_bytes=VMEM_BYTES),
+        cost_estimate=pl.CostEstimate(
+            flops=5 * span * span * q_width * 2,
+            bytes_accessed=span * (q_width * 12 + kv_width * 12),
+            transcendentals=span * span * heads * group // 2,
+        ),
+        name="attend_back",
+    )(query_low, key_low, value_low, grad_out, lse, q_proj, k_proj, cosine, sine, q_gain, k_gain)
+
+
+def swap(values, axis):
+    return lax.ppermute(values, axis, [(0, 1), (1, 0)])
+
+
+def turn(values):
+    return lax.ppermute(values, ("c", "x"), [(0, 0), (1, 2), (2, 1), (3, 3)])
+
+
+def rows_at(values, index, count):
+    return lax.dynamic_slice_in_dim(values, index * count, count, axis=0)
+
+
+def cols_at(values, index, count):
+    return lax.dynamic_slice_in_dim(values, index * count, count, axis=1)
+
+
+def ordered(first, mine, other, axis=0):
+    return jnp.where(
+        first,
+        jnp.concatenate([mine, other], axis=axis),
+        jnp.concatenate([other, mine], axis=axis),
+    )
+
+
+def paired(
+    tokens,
+    positions,
+    cotangent,
+    norm1_gain,
+    w_query,
+    w_key,
+    w_value,
+    w_out,
+    query_gain,
+    key_gain,
+    norm2_gain,
+    w_gate,
+    w_up,
+    w_down,
+):
+    x, c = lax.axis_index("x"), lax.axis_index("c")
+    half, width = tokens.shape
+    head_dim = query_gain.shape[0] * 2
+    bf16, f32 = jnp.bfloat16, jnp.float32
+
+    def flip(values):
+        mid = values.shape[1] // 2
+        swapped = jnp.concatenate([values[:, mid:], values[:, :mid]], axis=1)
+        return jnp.where(x == 0, values, swapped)
+
+    def both(values):
+        return ordered(c == 0, values, swap(values, "c"))
+
+    def fetch(piece):
+        count = piece.shape[0] // 2
+        y = lax.axis_index("y")
+        near = swap(rows_at(piece, y, count), "x")
+        return ordered(y == 0, near, swap(near, "y"))
+
+    def column_parts(weight):
+        count = weight.shape[1] // 4
+        return cols_at(weight, 2 * x + c, count), cols_at(weight, 2 * (1 - x) + c, count)
+
+    def column_weights(weights):
+        parts = [column_parts(weight) for weight in weights]
+        own = jnp.concatenate([part for pair in parts for part in pair], axis=1)
+        sent = jnp.concatenate([part for pair in parts for part in pair[::-1]], axis=1)
+        return jnp.concatenate([own, fetch(sent)], axis=0)
+
+    def row_weights(weight):
+        own = rows_at(weight, c, weight.shape[0] // 2)
+        return jnp.concatenate([own, fetch(own)], axis=0)
+
+    own_tokens = turn(tokens)
+    all_tokens = both(own_tokens)
+    places = both(turn(positions))
+    gains = jnp.concatenate([norm1_gain, norm2_gain, query_gain, key_gain])
+    far_gains = swap(gains, "x")
+    gains, far_gains = gains.astype(f32), far_gains.astype(f32)
+    part = norm1_gain.shape[0]
+    q_part = query_gain.shape[0]
+    gain_one = jnp.concatenate([gains[:part], far_gains[:part]])
+    gain_two = jnp.concatenate([gains[part : 2 * part], far_gains[part : 2 * part]])
+    q_gain = ordered(
+        x == 0, gains[2 * part : 2 * part + q_part], far_gains[2 * part : 2 * part + q_part]
+    )[None]
+    k_gain = ordered(x == 0, gains[2 * part + q_part :], far_gains[2 * part + q_part :])[None]
+
+    qkv_w = column_weights([w_query, w_key, w_value])
+    out_w = row_weights(w_out)
+    own_cot = turn(cotangent)
+    all_cot = both(own_cot)
+    gu_w = column_weights([w_gate, w_up])
+    down_w = row_weights(w_down)
+
+    cosine, sine = rotation_tables(places, head_dim)
+    cosine = jnp.concatenate([cosine[:, 0], cosine[:, 0]], axis=-1)
+    sine = jnp.concatenate([-sine[:, 0], sine[:, 0]], axis=-1)
+
+    x_all = flip(all_tokens).astype(f32)
+    h_one = (x_all * rms_scale(x_all) * gain_one).astype(bf16)
+    q_width = w_query.shape[1] // 2
+    kv_width = w_key.shape[1] // 2
+    qkv = jnp.dot(h_one, qkv_w, preferred_element_type=f32)
+    q_proj, k_proj = qkv[:, :q_width], qkv[:, q_width : q_width + kv_width]
+    value_low = qkv[:, q_width + kv_width :].astype(bf16)
+    out_low, query_low, key_low, lse = attend(
+        q_proj, k_proj, value_low, cosine, sine, q_gain, k_gain
+    )
+
+    def shared(left, right, product):
+        sent = product(rows_at(left, 1 - c, half), right).astype(bf16)
+        got = swap(sent, "c")
+        return product(rows_at(left, c, half), right) + got.astype(f32)
+
+    def plain(left, right):
+        return jnp.dot(left, right, preferred_element_type=f32)
+
+    x_own = own_tokens.astype(f32)
+    resid = x_own + shared(out_low, out_w, plain)
+    resid_flip = flip(resid)
+    h_two = both((resid_flip * rms_scale(resid_flip) * gain_two).astype(bf16))
+    units = w_down.shape[0]
+    gate_up = jnp.dot(h_two, gu_w, preferred_element_type=f32)
+    gate, up_val = gate_up[:, :units], gate_up[:, units:]
+    sigmoid_gate = jax.nn.sigmoid(gate)
+    hidden_low = (gate * sigmoid_gate * up_val).astype(bf16)
+    grad_hidden = times_t(all_cot, down_w)
+    grad_gate_low = (
+        grad_hidden * up_val * sigmoid_gate * (1.0 + gate * (1.0 - sigmoid_gate))
+    ).astype(bf16)
+    grad_up_low = (grad_hidden * gate * sigmoid_gate).astype(bf16)
+    grad_gu = jnp.concatenate([grad_gate_low, grad_up_low], axis=1)
+
+    def rs(values, axis):
+        index, count = lax.axis_index(axis), values.shape[0] // 2
+        return rows_at(values, index, count) + swap(rows_at(values, 1 - index, count), axis)
+
+    def ag(values, axis):
+        return ordered(lax.axis_index(axis) == 0, values, swap(values, axis))
+
+    def total_of(values):
+        values = rs(values, "y")
+        values = rs(values, "za")
+        values = values + swap(values, "zb")
+        values = ag(values, "za")
+        return ag(values, "y")
+
+    def grad_rows(left, right):
+        rows = left.shape[1] // 2
+        sent = inner_rows(left[:, rows:], right).astype(bf16)
+        got = swap(sent, "x")
+        mine = total_of((inner_rows(left[:, :rows], right) + got.astype(f32)).astype(bf16))
+        return ordered(c == 0, mine, swap(mine, "c")).astype(f32)
+
+    def grad_cols(left, right, widths):
+        rows = left.shape[1] // 2
+        sent = inner_rows(left[:, rows:], right).astype(bf16)
+        got = swap(sent, "x")
+        kept = inner_rows(left[:, :rows], right)
+        pieces, at = [], 0
+        for count in widths:
+            pieces += [got[:, at + count : at + 2 * count], got[:, at : at + count]]
+            at += 2 * count
+        mine = total_of((kept + jnp.concatenate(pieces, axis=1).astype(f32)).astype(bf16))
+        other = swap(mine, "c")
+        results, at = [], 0
+        for count in widths:
+
+            def block(values, index):
+                return jnp.where(
+                    x == index,
+                    values[:, at : at + count],
+                    values[:, at + count : at + 2 * count],
+                )
+
+            results.append(
+                jnp.concatenate(
+                    [
+                        piece
+                        for index in range(2)
+                        for piece in (
+                            jnp.where(c == 0, block(mine, index), block(other, index)),
+                            jnp.where(c == 0, block(other, index), block(mine, index)),
+                        )
+                    ],
+                    axis=1,
+                ).astype(f32)
+            )
+            at += 2 * count
+        return results
+
+    grad_down = grad_rows(hidden_low, all_cot)
+    grad_gate_w, grad_up_w = grad_cols(h_two, grad_gu, [units // 2, units // 2])
+    result = turn((resid + shared(hidden_low, down_w, plain)).astype(bf16))
+
+    grad_h_two = shared(grad_gu, gu_w, times_t)
+    resid_part, gain_two_terms = norm_back(resid_flip, gain_two, grad_h_two)
+    grad_resid = own_cot.astype(f32) + flip(resid_part)
+    resid_low = both(grad_resid.astype(bf16))
+    grad_out_w = grad_rows(out_low, resid_low)
+    grad_att = times_t(resid_low, out_w).astype(bf16)
+    grad_query, grad_key, grad_value, head_gains = attend_back(
+        query_low,
+        key_low,
+        value_low,
+        grad_att,
+        lse,
+        q_proj,
+        k_proj,
+        cosine,
+        sine,
+        q_gain,
+        k_gain,
+    )
+    grad_qkv = jnp.concatenate([grad_query, grad_key, grad_value], axis=1)
+    grad_query_w, grad_key_w, grad_value_w = grad_cols(
+        h_one, grad_qkv, [q_width // 2, kv_width // 2, kv_width // 2]
+    )
+    grad_h_one = shared(grad_qkv, qkv_w, times_t)
+    input_part, gain_one_terms = norm_back(flip(x_own), gain_one, grad_h_one)
+    grad_input = turn((grad_resid + flip(input_part)).astype(bf16)).astype(f32)
+
+    def natural(values):
+        return ordered(x == 0, values[:part], values[part:])
+
+    gain_sums = jnp.concatenate(
+        [
+            natural(jnp.sum(gain_one_terms, axis=0)),
+            natural(jnp.sum(gain_two_terms, axis=0)),
+            jnp.sum(head_gains[:, 0], axis=0),
+            jnp.sum(head_gains[:, 1], axis=0),
+        ]
+    )
+    gain_sums = lax.psum(gain_sums, ("zb", "za", "y", "c", "x"))
+
+    def own_gain(start, count):
+        return lax.dynamic_slice_in_dim(gain_sums, start + x * count, count)
+
+    return (
+        result,
+        grad_input,
+        own_gain(0, part),
+        grad_query_w,
+        grad_key_w,
+        grad_value_w,
+        grad_out_w,
+        own_gain(4 * part, q_part),
+        own_gain(4 * part + 2 * q_part, q_part),
+        own_gain(2 * part, part),
+        grad_gate_w,
+        grad_up_w,
+        grad_down,
+    )
+
+
 def solution(mesh):
+    if mesh.shape["shard"] == 2 and mesh.shape["replica"] == 16:
+        names = ("zb", "za", "y", "c", "x")
+        grid = Mesh(mesh.devices.reshape((2,) * len(names)), names)
+        body, over, owned = paired, names, "x"
+    else:
+        grid, body, over, owned = mesh, local, ("replica", "shard"), "shard"
+    rows, vector, matrix = P(over, None), P(owned), P(owned, None)
     return jax.shard_map(
-        local,
-        mesh=mesh,
+        body,
+        mesh=grid,
         in_specs=(
-            P(("replica", "shard"), None),
-            P(("replica", "shard")),
-            P(("replica", "shard"), None),
-            P("shard"),
-            P("shard", None),
-            P("shard", None),
-            P("shard", None),
-            P("shard", None),
-            P("shard"),
-            P("shard"),
-            P("shard"),
-            P("shard", None),
-            P("shard", None),
-            P("shard", None),
+            rows,
+            P(over),
+            rows,
+            vector,
+            matrix,
+            matrix,
+            matrix,
+            matrix,
+            vector,
+            vector,
+            vector,
+            matrix,
+            matrix,
+            matrix,
         ),
         out_specs=(
-            P(("replica", "shard"), None),
-            P(("replica", "shard"), None),
-            P("shard"),
-            P("shard", None),
-            P("shard", None),
-            P("shard", None),
-            P("shard", None),
-            P("shard"),
-            P("shard"),
-            P("shard"),
-            P("shard", None),
-            P("shard", None),
-            P("shard", None),
+            rows,
+            rows,
+            vector,
+            matrix,
+            matrix,
+            matrix,
+            matrix,
+            vector,
+            vector,
+            vector,
+            matrix,
+            matrix,
+            matrix,
         ),
         check_vma=False,
     )

time: 1570 us -> 778 us (0.50)
  waiting for transfers between devices: 1000 us -> 330 us
  local copies, waits for them, and re-layouts: 155 us -> 42.3 us
  starting transfers between devices: 1.02 us -> 98 us
  other arithmetic: 158 us -> 77.3 us
  Pallas kernels: 0 us -> 51.5 us
  matrix products: 167 us -> 127 us
  blocking collectives: 54.8 us -> 38 us
    reduce_scatter x9 -> x0, waiting for transfers between devices: 463 us -> none  [the longest x1 79.9 us: local(): lax.psum_scatter(grad_up_w.astype(jnp.bfloat16), 'shard', scatter_dimensi...]
    ppermute x0 -> x51, waiting for transfers between devices: none -> 330 us  [the longest x46 330 us: swap(): return lax.ppermute(values, axis, [(0, 1), (1, 0)])]
    all_gather x9 -> x0, waiting for transfers between devices: 306 us -> none  [the longest x1 73.9 us: local(): lax.all_gather(w_down, 'shard', axis=0, tiled=True)]
    psum x1 -> x0, waiting for transfers between devices: 227 us -> none  [local(): lax.psum(attn_shares[1].astype(jnp.bfloat16), 'replica').astype(jnp.float32)]
    ppermute x0 -> x51, starting transfers between devices: none -> 98 us  [the longest x46 59 us: swap(): return lax.ppermute(values, axis, [(0, 1), (1, 0)])]
    reduce_sum x8 -> x1, other arithmetic: 54.4 us -> 0.81 us  [paired(): jnp.sum(head_gains[:, 0], axis=0)]
    pallas_call x0 -> x2, Pallas kernels: none -> 51.5 us  [the longest x1 28.8 us: attend_back(): pl.pallas_call(attend_back_kernel, grid=(heads,), in_specs=[q_spec, k_spe...]
    another operation x4 -> x0, local copies, waits for them, and re-layouts: 43.2 us -> none
  transfers between devices with their start and end apart: 19 -> 51, of which waited for: 17 -> 19; matrix products, arithmetic and copies ran while one was open for 18% -> 27% of each run, Pallas kernels for 0% -> 7%
where the time goes in v1:
time: 778 us; the launch traced here: 766 us
  waiting for transfers between devices  330 us (42%)
  matrix products  127 us (16%)
  starting transfers between devices  98 us (13%)
  other arithmetic  77.3 us (10%)
  Pallas kernels  51.5 us (7%)
  local copies, waits for them, and re-layouts  42.3 us (5%)
  blocking collectives  38 us (5%)
    ppermute x46, waiting for transfers between devices, swap(): return lax.ppermute(values, axis, [(0, 1), (1, 0)])  330 us
    ppermute x46, starting transfers between devices, swap(): return lax.ppermute(values, axis, [(0, 1), (1, 0)])  59 us
    ppermute x5, starting transfers between devices, turn(): return lax.ppermute(values, ('c', 'x'), [(0, 0), (1, 2), (2, 1), (3, 3)])  39 us
    dot_general x6, matrix products, times_t(): lax.dot_general(left, right, (((1,), (1,)), ((), ())), preferred_element_...  38.6 us
    psum x1, blocking collectives, paired(): gain_sums = lax.psum(gain_sums, ('zb', 'za', 'y', 'c', 'x'))  38 us
    dot_general x8, matrix products, inner_rows(): lax.dot_general(left, right, (((0,), (0,)), ((), ())), preferred_element_...  35.9 us
    dot_general x1, matrix products, paired(): gate_up = jnp.dot(h_two, gu_w, preferred_element_type=f32)  29.5 us
    pallas_call x1, Pallas kernels, attend_back(): pl.pallas_call(attend_back_kernel, grid=(heads,), in_specs=[q_spec, k_spe...  28.8 us
  transfers between devices with their start and end apart: 51, of which 19 were waited for; matrix products, arithmetic and copies ran while one was open for 27% of the time, Pallas kernels for 7%

profile of v1, /device:TPU:0, one launch (start us, length us, event | category | flops | bytes accessed | tf_op | source)
XLA Modules:
  0.0 765.9 jit_solution(12365664564967956592)
XLA Ops:
  6.7 9.5 %collective-permute-start = (bf16[512,1024]{1,0:T(8,128)(2,1)}, bf16[512,1024]{1,0:T(8,128)(2,1)}, u32[]{:S(2)}, u32[]{:S(2)}) collective-permute-start(bf16[512,1024]{1,0:T(8,128)(2,1)} %param.14), channel_id=1, source_target_pairs={{0,0},{1,2},{2,1},{3,3},{4,4},{5,6},{6,5},{7,7},{8,8},{9,10},{10,9... | collective-permute-start | bytes 3145736 | tf_op jit(solution)/shard_map/ppermute | solution.py:579
  38.5 14.8 %collective-permute-start.11 = (bf16[256,3072]{1,0:T(8,128)(2,1)}, bf16[256,3072]{1,0:T(8,128)(2,1)}, u32[]{:S(2)}, u32[]{:S(2)}) collective-permute-start(bf16[256,3072]{1,0:T(8,128)(2,1)} %fusion.20), channel_id=1, source_target_pairs={{0,1},{1,0},{2,3},{3,2},{4,5},{5,4},{6,7},{7,6},{8,9},{9,8},{10,11... | collective-permute-start | bytes 4718600 | tf_op jit(solution)/shard_map/ppermute | solution.py:575
  54.1 11.0 %collective-permute-done.7 = bf16[256,1024]{1,0:T(8,128)(2,1)} collective-permute-done((bf16[256,1024]{1,0:T(8,128)(2,1)}, bf16[256,1024]{1,0:T(8,128)(2,1)}, u32[]{:S(2)}, u32[]{:S(2)}) %collective-permute-start.7) | collective-permute-done | bytes 524320 | tf_op jit(solution)/shard_map/ppermute | solution.py:575
  71.0 9.2 %collective-permute-done.8 = bf16[256,1024]{1,0:T(8,128)(2,1)S(1)} collective-permute-done((bf16[256,1024]{1,0:T(8,128)(2,1)}, bf16[256,1024]{1,0:T(8,128)(2,1)S(1)}, u32[]{:S(2)}, u32[]{:S(2)}) %collective-permute-start.8) | collective-permute-done | bytes 524320 | tf_op jit(solution)/shard_map/ppermute | solution.py:575
  86.4 10.8 %collective-permute-done.4 = bf16[256,2048]{1,0:T(8,128)(2,1)S(1)} collective-permute-done((bf16[256,2048]{1,0:T(8,128)(2,1)}, bf16[256,2048]{1,0:T(8,128)(2,1)S(1)}, u32[]{:S(2)}, u32[]{:S(2)}) %collective-permute-start.4) | collective-permute-done | bytes 1048608 | tf_op jit(solution)/shard_map/ppermute | solution.py:575
  111.7 22.7 %attend.1 = (bf16[1024,1024]{1,0:T(8,128)(2,1)}, bf16[1024,1024]{1,0:T(8,128)(2,1)}, bf16[1024,512]{1,0:T(8,128)(2,1)}, f32[4,2,1024]{2,1,0:T(2,128)}) custom-call(f32[1024,1024]{1,0:T(8,128)} %slice.335.qp_ref, f32[1024,512]{1,0:T(8,128)} %slice.336.kp_ref, bf16[1024,512]{1,0:T(8,128)(2,1)} %slice.626.v_ref, f32[1024,128]{1,0:T(8,128)} %get-tuple-element.113.cos_ref, ...), custom_call_target="tpu_custom_call" | custom-call | flops 4294967296 | bytes 12582912 | tf_op jit(solution)/shard_map/attend/pallas_call | solution.py:505
  141.5 9.5 %collective-permute-start.17 = (bf16[512,1024]{1,0:T(8,128)(2,1)}, bf16[512,1024]{1,0:T(8,128)(2,1)}, u32[]{:S(2)}, u32[]{:S(2)}) collective-permute-start(bf16[512,1024]{1,0:T(8,128)(2,1)} %param.16), channel_id=1, source_target_pairs={{0,0},{1,2},{2,1},{3,3},{4,4},{5,6},{6,5},{7,7},{8,8},{9,10},{10,9... | collective-permute-start | bytes 3145736 | tf_op jit(solution)/shard_map/ppermute | solution.py:579
  152.2 7.8 %collective-permute-done.13 = bf16[384,1024]{1,0:T(8,128)(2,1)} collective-permute-done((bf16[384,1024]{1,0:T(8,128)(2,1)}, bf16[384,1024]{1,0:T(8,128)(2,1)}, u32[]{:S(2)}, u32[]{:S(2)}) %collective-permute-start.13) | collective-permute-done | bytes 786464 | tf_op jit(solution)/shard_map/ppermute | solution.py:575
  183.9 29.4 %collective-permute-done.12 = bf16[256,3072]{1,0:T(8,128)(2,1)S(1)} collective-permute-done((bf16[256,3072]{1,0:T(8,128)(2,1)}, bf16[256,3072]{1,0:T(8,128)(2,1)S(1)}, u32[]{:S(2)}, u32[]{:S(2)}) %collective-permute-start.12) | collective-permute-done | bytes 1572896 | tf_op jit(solution)/shard_map/ppermute | solution.py:575
  218.1 29.5 %fusion.82 = f32[1024,3072]{1,0:T(8,128)} fusion(bf16[1024,1024]{1,0:T(8,128)(2,1)S(1)} %maximum_select_fusion.7, bf16[512,3072]{1,0:T(8,128)(2,1)S(1)} %maximum_select_fusion, bf16[512,768]{1,0:T(8,128)(2,1)S(1)} %copy-done.11, bf16[512,768]{1,0:T(8,128)(2,1)S(1)} %copy-done.9, bf16[512,768]{1,0:T(8,128)(2,1)S(1)} %copy-done.14, ...), kind=kOutput, calls=%fused_computation.245 | convolution fusion | flops 6473908224 | bytes 20971520 | tf_op jit(solution)/shard_map/dot_general | solution.py:697
  247.6 13.5 %multiply_convert_fusion = (bf16[1024,1536]{1,0:T(8,128)(2,1)}, bf16[1024,1536]{1,0:T(8,128)(2,1)}, bf16[1024,1536]{1,0:T(8,128)(2,1)}) fusion(f32[1024,3072]{1,0:T(8,128)} %fusion.82, bf16[768,1024]{1,0:T(8,128)(2,1)} %maximum_select_fusion.15, bf16[768,1024]{1,0:T(8,128)(2,1)} %constant_dynamic-slice_fusion.9, ...), kind=kOutput, calls=%fused_computation.7 | convolution fusion | flops 3262119936 | bytes 27262976 | tf_op jit(solution)/shard_map/dot_general | solution.py:70
  291.0 9.8 %collective-permute-start.16 = (bf16[512,1024]{1,0:T(8,128)(2,1)}, bf16[512,1024]{1,0:T(8,128)(2,1)}, u32[]{:S(2)}, u32[]{:S(2)}) collective-permute-start(bf16[512,1024]{1,0:T(8,128)(2,1)} %add_convert_fusion.4), channel_id=1, source_target_pairs={{0,0},{1,2},{2,1},{3,3},{4,4},{5,6},{6,5},{7,7},{8,8},{9,10},{10,9... | collective-permute-start | bytes 3145736 | tf_op jit(solution)/shard_map/ppermute | solution.py:579
  309.8 73.6 %collective-permute-done.44 = bf16[768,1024]{1,0:T(8,128)(2,1)} collective-permute-done((bf16[768,1024]{1,0:T(8,128)(2,1)}, bf16[768,1024]{1,0:T(8,128)(2,1)}, u32[]{:S(2)}, u32[]{:S(2)}) %collective-permute-start.44) | collective-permute-done | bytes 1572896 | tf_op jit(solution)/shard_map/ppermute | solution.py:575
  395.6 28.8 %attend_back.1 = (bf16[1024,1024]{1,0:T(8,128)(2,1)}, bf16[1024,512]{1,0:T(8,128)(2,1)}, bf16[1024,512]{1,0:T(8,128)(2,1)}, f32[4,8,128]{2,1,0:T(8,128)}) custom-call(bf16[1024,1024]{1,0:T(8,128)(2,1)} %get-tuple-element.22.q_ref, bf16[1024,512]{1,0:T(8,128)(2,1)} %get-tuple-element.23.k_ref, bf16[1024,512]{1,0:T(8,128)(2,1)} %slice.626.v_ref, ...), custom_call_target="tpu_custom_call" | custom-call | flops 10737418240 | bytes 18874368 | tf_op jit(solution)/shard_map/attend_back/pallas_call | solution.py:537
  462.9 45.8 %collective-permute-done.30 = bf16[512,1024]{1,0:T(8,128)(2,1)} collective-permute-done((bf16[512,1024]{1,0:T(8,128)(2,1)}, bf16[512,1024]{1,0:T(8,128)(2,1)}, u32[]{:S(2)}, u32[]{:S(2)}) %collective-permute-start.30) | collective-permute-done | bytes 1048608 | tf_op jit(solution)/shard_map/ppermute | solution.py:575
  519.8 20.9 %collective-permute-done.24 = bf16[256,2048]{1,0:T(8,128)(2,1)S(1)} collective-permute-done((bf16[256,2048]{1,0:T(8,128)(2,1)S(1)}, bf16[256,2048]{1,0:T(8,128)(2,1)S(1)}, u32[]{:S(2)}, u32[]{:S(2)}) %collective-permute-start.24) | collective-permute-done | bytes 1048608 | tf_op jit(solution)/shard_map/ppermute | solution.py:575
  551.0 16.0 %collective-permute-done.25 = bf16[128,2048]{1,0:T(8,128)(2,1)S(1)} collective-permute-done((bf16[128,2048]{1,0:T(8,128)(2,1)S(1)}, bf16[128,2048]{1,0:T(8,128)(2,1)S(1)}, u32[]{:S(2)}, u32[]{:S(2)}) %collective-permute-start.25) | collective-permute-done | bytes 524320 | tf_op jit(solution)/shard_map/ppermute | solution.py:575
  567.9 24.9 %collective-permute-done.40 = bf16[128,3072]{1,0:T(8,128)(2,1)S(1)} collective-permute-done((bf16[128,3072]{1,0:T(8,128)(2,1)S(1)}, bf16[128,3072]{1,0:T(8,128)(2,1)S(1)}, u32[]{:S(2)}, u32[]{:S(2)}) %collective-permute-start.40) | collective-permute-done | bytes 786464 | tf_op jit(solution)/shard_map/ppermute | solution.py:575
  603.1 14.3 %collective-permute-done.41 = bf16[128,3072]{1,0:T(8,128)(2,1)S(1)} collective-permute-done((bf16[128,3072]{1,0:T(8,128)(2,1)S(1)}, bf16[128,3072]{1,0:T(8,128)(2,1)S(1)}, u32[]{:S(2)}, u32[]{:S(2)}) %collective-permute-start.41) | collective-permute-done | bytes 786464 | tf_op jit(solution)/shard_map/ppermute | solution.py:575
  618.4 10.3 %collective-permute-done.27 = bf16[128,2048]{1,0:T(8,128)(2,1)S(1)} collective-permute-done((bf16[128,2048]{1,0:T(8,128)(2,1)S(1)}, bf16[128,2048]{1,0:T(8,128)(2,1)S(1)}, u32[]{:S(2)}, u32[]{:S(2)}) %collective-permute-start.27) | collective-permute-done | bytes 524320 | tf_op jit(solution)/shard_map/ppermute | solution.py:575
  635.1 13.8 %collective-permute-done.33 = bf16[128,1024]{1,0:T(8,128)(2,1)S(1)} collective-permute-done((bf16[128,1024]{1,0:T(8,128)(2,1)S(1)}, bf16[128,1024]{1,0:T(8,128)(2,1)S(1)}, u32[]{:S(2)}, u32[]{:S(2)}) %collective-permute-start.33) | collective-permute-done | bytes 262176 | tf_op jit(solution)/shard_map/ppermute | solution.py:575
  652.4 9.7 %collective-permute-start.22 = (bf16[512,1024]{1,0:T(8,128)(2,1)}, bf16[512,1024]{1,0:T(8,128)(2,1)}, u32[]{:S(2)}, u32[]{:S(2)}) collective-permute-start(bf16[512,1024]{1,0:T(8,128)(2,1)} %fusion.12), channel_id=1, source_target_pairs={{0,0},{1,2},{2,1},{3,3},{4,4},{5,6},{6,5},{7,7},{8,8},{9,10},{10,9... | collective-permute-start | bytes 3145736 | tf_op jit(solution)/shard_map/ppermute | solution.py:579
  664.7 13.0 %collective-permute-done.28 = bf16[256,2048]{1,0:T(8,128)(2,1)S(1)} collective-permute-done((bf16[256,2048]{1,0:T(8,128)(2,1)S(1)}, bf16[256,2048]{1,0:T(8,128)(2,1)S(1)}, u32[]{:S(2)}, u32[]{:S(2)}) %collective-permute-start.28) | collective-permute-done | bytes 1048608 | tf_op jit(solution)/shard_map/ppermute | solution.py:575
  689.3 38.0 %psum.7 = f32[2304]{0:T(1024)S(1)} all-reduce(f32[2304]{0:T(1024)S(1)} %pad_maximum_fusion.18), channel_id=1, replica_groups=mesh['zb'=2,'za'=2,'y'=2,'c'=2,'x'=2] {'zb','za','y','c','x'}, use_global_device_ids=true, to_apply=%region_9.10 | all-reduce | flops 2304 | bytes 18432 | tf_op jit(solution)/shard_map/psum | solution.py:808
  (328 shorter events, 277.3 us)
Async XLA Ops:
  3.7 49.6 %collective-permute-start.2 = (bf16[1152]{0:T(1024)(128)(2,1)S(1)}, bf16[1152]{0:T(1024)(128)(2,1)S(1)}, u32[]{:S(2)}, u32[]{:S(2)}) collective-permute-start(bf16[1152]{0:T(1024)(128)(2,1)S(1)} %concatenate.265), channel_id=1, source_target_pairs={{0,1},{1,0},{2,3},{3,2},{4,5},{5,4},{6,7},{7,6},{8,9},{9,8},{10,11... | collective-permute-start | bytes 6920 | tf_op jit(solution)/shard_map/ppermute | solution.py:575
  38.5 123.2 %collective-permute-start.11 = (bf16[256,3072]{1,0:T(8,128)(2,1)}, bf16[256,3072]{1,0:T(8,128)(2,1)}, u32[]{:S(2)}, u32[]{:S(2)}) collective-permute-start(bf16[256,3072]{1,0:T(8,128)(2,1)} %fusion.20), channel_id=1, source_target_pairs={{0,1},{1,0},{2,3},{3,2},{4,5},{5,4},{6,7},{7,6},{8,9},{9,8},{10,11... | collective-permute-start | bytes 4718600 | tf_op jit(solution)/shard_map/ppermute | solution.py:575
  161.8 51.5 %collective-permute-start.12 = (bf16[256,3072]{1,0:T(8,128)(2,1)}, bf16[256,3072]{1,0:T(8,128)(2,1)S(1)}, u32[]{:S(2)}, u32[]{:S(2)}) collective-permute-start(bf16[256,3072]{1,0:T(8,128)(2,1)} %collective-permute-done.11), channel_id=1, source_target_pairs={{0,4},{4,0},{1,5},{5,1},{2,6},{6,2},{3,7},{7,3},{8,12},{12,8},{9,1... | collective-permute-start | bytes 4718600 | tf_op jit(solution)/shard_map/ppermute | solution.py:575
  166.0 50.2 %collective-permute-start.10 = (bf16[512,1024]{1,0:T(8,128)(2,1)S(1)}, bf16[512,1024]{1,0:T(8,128)(2,1)S(1)}, u32[]{:S(2)}, u32[]{:S(2)}) collective-permute-start(bf16[512,1024]{1,0:T(8,128)(2,1)S(1)} %multiply_convert_fusion.3), channel_id=1, source_target_pairs={{0,2},{2,0},{1,3},{3,1},{4,6},{6,4},{5,7},{7,5},{8,10},{10,8},{9,1... | collective-permute-start | bytes 3145736 | tf_op jit(solution)/shard_map/ppermute | solution.py:575
  167.6 79.9 %collective-permute-start.18 = (bf16[512,1024]{1,0:T(8,128)(2,1)}, bf16[512,1024]{1,0:T(8,128)(2,1)}, u32[]{:S(2)}, u32[]{:S(2)}) collective-permute-start(bf16[512,1024]{1,0:T(8,128)(2,1)} %collective-permute-done.17), channel_id=1, source_target_pairs={{0,2},{2,0},{1,3},{3,1},{4,6},{6,4},{5,7},{7,5},{8,10},{10,8},{9,1... | collective-permute-start | bytes 3145736 | tf_op jit(solution)/shard_map/ppermute | solution.py:575
  279.3 174.7 %collective-permute-start.37 = (bf16[512,3072]{1,0:T(8,128)(2,1)}, bf16[512,3072]{1,0:T(8,128)(2,1)S(1)}, u32[]{:S(2)}, u32[]{:S(2)}) collective-permute-start(bf16[512,3072]{1,0:T(8,128)(2,1)} %convolution_convert_fusion), channel_id=1, source_target_pairs={{0,1},{1,0},{2,3},{3,2},{4,5},{5,4},{6,7},{7,6},{8,9},{9,8},{10,11... | collective-permute-start | bytes 9437192 | tf_op jit(solution)/shard_map/ppermute | solution.py:575
  286.2 97.2 %collective-permute-start.44 = (bf16[768,1024]{1,0:T(8,128)(2,1)}, bf16[768,1024]{1,0:T(8,128)(2,1)}, u32[]{:S(2)}, u32[]{:S(2)}) collective-permute-start(bf16[768,1024]{1,0:T(8,128)(2,1)} %convolution_convert_fusion.3), channel_id=1, source_target_pairs={{0,1},{1,0},{2,3},{3,2},{4,5},{5,4},{6,7},{7,6},{8,9},{9,8},{10,11... | collective-permute-start | bytes 4718600 | tf_op jit(solution)/shard_map/ppermute | solution.py:575
  291.0 153.0 %collective-permute-start.16 = (bf16[512,1024]{1,0:T(8,128)(2,1)}, bf16[512,1024]{1,0:T(8,128)(2,1)}, u32[]{:S(2)}, u32[]{:S(2)}) collective-permute-start(bf16[512,1024]{1,0:T(8,128)(2,1)} %add_convert_fusion.4), channel_id=1, source_target_pairs={{0,0},{1,2},{2,1},{3,3},{4,4},{5,6},{6,5},{7,7},{8,8},{9,10},{10,9... | collective-permute-start | bytes 3145736 | tf_op jit(solution)/shard_map/ppermute | solution.py:579
  309.6 82.3 %collective-permute-start.20 = (bf16[512,1024]{1,0:T(8,128)(2,1)S(1)}, bf16[512,1024]{1,0:T(8,128)(2,1)S(1)}, u32[]{:S(2)}, u32[]{:S(2)}) collective-permute-start(bf16[512,1024]{1,0:T(8,128)(2,1)S(1)} %fusion.81), channel_id=1, source_target_pairs={{0,2},{2,0},{1,3},{3,1},{4,6},{6,4},{5,7},{7,5},{8,10},{10,8},{9,1... | collective-permute-start | bytes 3145736 | tf_op jit(solution)/shard_map/ppermute | solution.py:575
  390.2 49.5 %collective-permute-start.45 = (bf16[384,1024]{1,0:T(8,128)(2,1)}, bf16[384,1024]{1,0:T(8,128)(2,1)S(1)}, u32[]{:S(2)}, u32[]{:S(2)}) collective-permute-start(bf16[384,1024]{1,0:T(8,128)(2,1)} %constant_dynamic-slice_fusion.1), channel_id=1, source_target_pairs={{0,4},{4,0},{1,5},{5,1},{2,6},{6,2},{3,7},{7,3},{8,12},{12,8},{9,1... | collective-permute-start | bytes 2359304 | tf_op jit(solution)/shard_map/ppermute | solution.py:575
  437.1 108.7 %collective-permute-start.21 = (bf16[512,1024]{1,0:T(8,128)(2,1)}, bf16[512,1024]{1,0:T(8,128)(2,1)}, u32[]{:S(2)}, u32[]{:S(2)}) collective-permute-start(bf16[512,1024]{1,0:T(8,128)(2,1)} %fusion.31), channel_id=1, source_target_pairs={{0,2},{2,0},{1,3},{3,1},{4,6},{6,4},{5,7},{7,5},{8,10},{10,8},{9,1... | collective-permute-start | bytes 3145736 | tf_op jit(solution)/shard_map/ppermute | solution.py:575
  437.1 74.4 %collective-permute-start.23 = (bf16[512,2048]{1,0:T(8,128)(2,1)}, bf16[512,2048]{1,0:T(8,128)(2,1)S(1)}, u32[]{:S(2)}, u32[]{:S(2)}) collective-permute-start(bf16[512,2048]{1,0:T(8,128)(2,1)} %convolution_convert_fusion.1), channel_id=1, source_target_pairs={{0,1},{1,0},{2,3},{3,2},{4,5},{5,4},{6,7},{7,6},{8,9},{9,8},{10,11... | collective-permute-start | bytes 6291464 | tf_op jit(solution)/shard_map/ppermute | solution.py:575
  444.0 64.6 %collective-permute-start.30 = (bf16[512,1024]{1,0:T(8,128)(2,1)}, bf16[512,1024]{1,0:T(8,128)(2,1)}, u32[]{:S(2)}, u32[]{:S(2)}) collective-permute-start(bf16[512,1024]{1,0:T(8,128)(2,1)} %convolution_convert_fusion.4), channel_id=1, source_target_pairs={{0,1},{1,0},{2,3},{3,2},{4,5},{5,4},{6,7},{7,6},{8,9},{9,8},{10,11... | collective-permute-start | bytes 3145736 | tf_op jit(solution)/shard_map/ppermute | solution.py:575
  451.4 67.8 %collective-permute-start.47 = (bf16[192,1024]{1,0:T(8,128)(2,1)S(1)}, bf16[192,1024]{1,0:T(8,128)(2,1)S(1)}, u32[]{:S(2)}, u32[]{:S(2)}) collective-permute-start(bf16[192,1024]{1,0:T(8,128)(2,1)S(1)} %dynamic-slice_add_fusion.6), channel_id=1, source_target_pairs={{0,16},{16,0},{1,17},{17,1},{2,18},{18,2},{3,19},{19,3},{4,20},{20... | collective-permute-start | bytes 1179656 | tf_op jit(solution)/shard_map/ppermute | solution.py:575
  462.3 52.7 %collective-permute-start.38 = (bf16[256,3072]{1,0:T(8,128)(2,1)S(1)}, bf16[256,3072]{1,0:T(8,128)(2,1)S(1)}, u32[]{:S(2)}, u32[]{:S(2)}) collective-permute-start(bf16[256,3072]{1,0:T(8,128)(2,1)S(1)} %constant_dynamic-slice_fusion.3), channel_id=1, source_target_pairs={{0,4},{4,0},{1,5},{5,1},{2,6},{6,2},{3,7},{7,3},{8,12},{12,8},{9,1... | collective-permute-start | bytes 4718600 | tf_op jit(solution)/shard_map/ppermute | solution.py:575
  517.6 83.2 %collective-permute-start.31 = (bf16[256,1024]{1,0:T(8,128)(2,1)S(1)}, bf16[256,1024]{1,0:T(8,128)(2,1)S(1)}, u32[]{:S(2)}, u32[]{:S(2)}) collective-permute-start(bf16[256,1024]{1,0:T(8,128)(2,1)S(1)} %constant_dynamic-slice_fusion.5), channel_id=1, source_target_pairs={{0,4},{4,0},{1,5},{5,1},{2,6},{6,2},{3,7},{7,3},{8,12},{12,8},{9,1... | collective-permute-start | bytes 1572872 | tf_op jit(solution)/shard_map/ppermute | solution.py:575
  519.3 75.5 %collective-permute-start.48 = (bf16[192,1024]{1,0:T(8,128)(2,1)S(1)}, bf16[192,1024]{1,0:T(8,128)(2,1)S(1)}, u32[]{:S(2)}, u32[]{:S(2)}) collective-permute-start(bf16[192,1024]{1,0:T(8,128)(2,1)S(1)} %add.278), channel_id=1, source_target_pairs={{0,8},{8,0},{1,9},{9,1},{2,10},{10,2},{3,11},{11,3},{4,12},{12,4},... | collective-permute-start | bytes 1179656 | tf_op jit(solution)/shard_map/ppermute | solution.py:575
  543.1 49.6 %collective-permute-start.40 = (bf16[128,3072]{1,0:T(8,128)(2,1)S(1)}, bf16[128,3072]{1,0:T(8,128)(2,1)S(1)}, u32[]{:S(2)}, u32[]{:S(2)}) collective-permute-start(bf16[128,3072]{1,0:T(8,128)(2,1)S(1)} %dynamic-slice_add_fusion.3), channel_id=1, source_target_pairs={{0,16},{16,0},{1,17},{17,1},{2,18},{18,2},{3,19},{19,3},{4,20},{20... | collective-permute-start | bytes 2359304 | tf_op jit(solution)/shard_map/ppermute | solution.py:575
  595.2 66.9 %collective-permute-start.49 = (bf16[384,1024]{1,0:T(8,128)(2,1)S(1)}, bf16[384,1024]{1,0:T(8,128)(2,1)S(1)}, u32[]{:S(2)}, u32[]{:S(2)}) collective-permute-start(bf16[384,1024]{1,0:T(8,128)(2,1)S(1)} %maximum_select_fusion.21), channel_id=1, source_target_pairs={{0,4},{4,0},{1,5},{5,1},{2,6},{6,2},{3,7},{7,3},{8,12},{12,8},{9,1... | collective-permute-start | bytes 2359304 | tf_op jit(solution)/shard_map/ppermute | solution.py:575
  617.8 62.1 %collective-permute-start.42 = (bf16[256,3072]{1,0:T(8,128)(2,1)S(1)}, bf16[256,3072]{1,0:T(8,128)(2,1)S(1)}, u32[]{:S(2)}, u32[]{:S(2)}) collective-permute-start(bf16[256,3072]{1,0:T(8,128)(2,1)S(1)} %maximum_select_fusion.16), channel_id=1, source_target_pairs={{0,4},{4,0},{1,5},{5,1},{2,6},{6,2},{3,7},{7,3},{8,12},{12,8},{9,1... | collective-permute-start | bytes 4718600 | tf_op jit(solution)/shard_map/ppermute | solution.py:575
  652.4 76.1 %collective-permute-start.22 = (bf16[512,1024]{1,0:T(8,128)(2,1)}, bf16[512,1024]{1,0:T(8,128)(2,1)}, u32[]{:S(2)}, u32[]{:S(2)}) collective-permute-start(bf16[512,1024]{1,0:T(8,128)(2,1)} %fusion.12), channel_id=1, source_target_pairs={{0,0},{1,2},{2,1},{3,3},{4,4},{5,6},{6,5},{7,7},{8,8},{9,10},{10,9... | collective-permute-start | bytes 3145736 | tf_op jit(solution)/shard_map/ppermute | solution.py:579
  663.9 67.4 %collective-permute-start.50 = (bf16[768,1024]{1,0:T(8,128)(2,1)}, bf16[768,1024]{1,0:T(8,128)(2,1)}, u32[]{:S(2)}, u32[]{:S(2)}) collective-permute-start(bf16[768,1024]{1,0:T(8,128)(2,1)} %maximum_select_fusion.17), channel_id=1, source_target_pairs={{0,2},{2,0},{1,3},{3,1},{4,6},{6,4},{5,7},{7,5},{8,10},{10,8},{9,1... | collective-permute-start | bytes 4718600 | tf_op jit(solution)/shard_map/ppermute | solution.py:575
  680.0 61.9 %collective-permute-start.29 = (bf16[512,2048]{1,0:T(8,128)(2,1)}, bf16[512,2048]{1,0:T(8,128)(2,1)}, u32[]{:S(2)}, u32[]{:S(2)}) collective-permute-start(bf16[512,2048]{1,0:T(8,128)(2,1)} %maximum_select_fusion.13), channel_id=1, source_target_pairs={{0,2},{2,0},{1,3},{3,1},{4,6},{6,4},{5,7},{7,5},{8,10},{10,8},{9,1... | collective-permute-start | bytes 6291464 | tf_op jit(solution)/shard_map/ppermute | solution.py:575
  681.4 71.2 %collective-permute-start.43 = (bf16[512,3072]{1,0:T(8,128)(2,1)S(1)}, bf16[512,3072]{1,0:T(8,128)(2,1)}, u32[]{:S(2)}, u32[]{:S(2)}) collective-permute-start(bf16[512,3072]{1,0:T(8,128)(2,1)S(1)} %maximum_select_fusion.1), channel_id=1, source_target_pairs={{0,2},{2,0},{1,3},{3,1},{4,6},{6,4},{5,7},{7,5},{8,10},{10,8},{9,1... | collective-permute-start | bytes 9437192 | tf_op jit(solution)/shard_map/ppermute | solution.py:575
  (83 other events, 1654.0 us)

commit v2 on v1

--- a/solution.py
+++ b/solution.py
@@ -1,3 +1,4 @@
+import functools
 from functools import partial
 import math
 
@@ -12,7 +13,10 @@
 THETA = 1000000.0
 NEG = -1e30
 QUERY_BLOCK = 256
+UNIT_BLOCK = 256
 VMEM_BYTES = 56 * 1024 * 1024
+GAIN_ROWS = 64
+ROW_BLOCK = 256
 
 
 def rms_scale(values):
@@ -377,6 +381,7 @@
         totals[9],
         totals[10],
     )
+NO_COST = pl.CostEstimate(flops=0, bytes_accessed=0, transcendentals=0)
 
 
 def head_norm(values, gain):
@@ -385,22 +390,24 @@
 
 
 def attend_kernel(
-    qp_ref, kp_ref, v_ref, cos_ref, sin_ref, qg_ref, kg_ref, o_ref, q_ref, k_ref, lse_ref
+    h_ref, w_ref, cos_ref, sin_ref, qg_ref, kg_ref, o_ref, q_ref, k_ref, lse_ref, qkv_ref
 ):
-    span, head_dim = kp_ref.shape
-    group = qp_ref.shape[1] // head_dim
+    qkv_ref[...] = jnp.dot(h_ref[...], w_ref[...], preferred_element_type=jnp.float32)
+    span, head_dim = cos_ref.shape
+    group = o_ref.shape[1] // head_dim
     block = min(QUERY_BLOCK, span)
     cosine, sine = cos_ref[...], sin_ref[...]
-    keyed = head_norm(kp_ref[...], kg_ref[...])
+    key_lanes = slice(group * head_dim, (group + 1) * head_dim)
+    keyed = head_norm(qkv_ref[:, key_lanes], kg_ref[...])
     key_low = (keyed * cosine + pltpu.roll(keyed, head_dim // 2, 1) * sine).astype(jnp.bfloat16)
     k_ref[...] = key_low
-    value_t = v_ref[...].T
+    value_t = qkv_ref[:, (group + 1) * head_dim :].astype(jnp.bfloat16).T
     ahead = lax.broadcasted_iota(jnp.int32, (block, block), 0) > lax.broadcasted_iota(
         jnp.int32, (block, block), 1
     )
     for head in range(group):
         lanes = slice(head * head_dim, (head + 1) * head_dim)
-        asked = head_norm(qp_ref[:, lanes], qg_ref[...])
+        asked = head_norm(qkv_ref[:, lanes], qg_ref[...])
         asked = asked * cosine + pltpu.roll(asked, head_dim // 2, 1) * sine
         query_low = (asked * (1.0 / math.sqrt(head_dim))).astype(jnp.bfloat16)
         q_ref[:, lanes] = query_low
@@ -421,27 +428,33 @@
 def attend_back_kernel(
     q_ref,
     k_ref,
-    v_ref,
+    qkv_ref,
     do_ref,
     lse_ref,
-    qp_ref,
-    kp_ref,
     cos_ref,
     sin_ref,
     qg_ref,
     kg_ref,
-    dq_ref,
-    dk_ref,
-    dv_ref,
-    gain_ref,
-    key_acc,
-    value_acc,
+    h_ref,
+    w_ref,
+    *rest,
+    first,
 ):
-    span, head_dim = kp_ref.shape
-    group = qp_ref.shape[1] // head_dim
+    dh_in = None if first else rest[0]
+    grad_ref, gain_ref, dh_ref, own_ref, key_acc, value_acc, ht_ref = rest[0 if first else 1 :]
+    span, head_dim = cos_ref.shape
+    group = q_ref.shape[1] // head_dim
+
+    @pl.when(pl.program_id(0) == 0)
+    def _():
+        ht_ref[...] = h_ref[...].T
+        dh_ref[...] = jnp.zeros_like(dh_ref) if first else dh_in[...]
+
     block = min(QUERY_BLOCK, span)
     inv_scale = 1.0 / math.sqrt(head_dim)
-    key_low, value_low = k_ref[...], v_ref[...]
+    key_lanes = slice(group * head_dim, (group + 1) * head_dim)
+    value_lanes = slice((group + 1) * head_dim, (group + 2) * head_dim)
+    key_low, value_low = k_ref[...], qkv_ref[:, value_lanes].astype(jnp.bfloat16)
     key_t = key_low.T
     ahead = lax.broadcasted_iota(jnp.int32, (block, block), 0) > lax.broadcasted_iota(
         jnp.int32, (block, block), 1
@@ -478,26 +491,33 @@
             grad_query = jnp.dot(key_t[:, :stop], dscore, preferred_element_type=jnp.float32).T
             back, gain_term = proj_back(
                 grad_query * inv_scale,
-                qp_ref[rows, lanes],
+                qkv_ref[rows, lanes],
                 cos_ref[rows, :],
                 sin_ref[rows, :],
                 qg_ref[...],
             )
-            dq_ref[rows, lanes] = back.astype(jnp.bfloat16)
+            own_ref[rows, lanes] = back.astype(jnp.bfloat16)
             query_gain = query_gain + gain_term
-    back, key_gain = proj_back(key_acc[...], kp_ref[...], cos_ref[...], sin_ref[...], kg_ref[...])
-    dk_ref[...] = back.astype(jnp.bfloat16)
-    dv_ref[...] = value_acc[...].astype(jnp.bfloat16)
+    back, key_gain = proj_back(
+        key_acc[...], qkv_ref[:, key_lanes], cos_ref[...], sin_ref[...], kg_ref[...]
+    )
+    own_ref[:, key_lanes] = back.astype(jnp.bfloat16)
+    own_ref[:, value_lanes] = value_acc[...].astype(jnp.bfloat16)
     gain_ref[0] = jnp.concatenate(
         [query_gain, key_gain, jnp.zeros((gain_ref.shape[1] - 2, head_dim), jnp.float32)], axis=0
     )
-
-
-def attend(q_proj, k_proj, value_low, cosine, sine, q_gain, k_gain):
-    span, q_width = q_proj.shape
-    kv_width = k_proj.shape[1]
-    head_dim = q_gain.shape[1]
-    heads, group = kv_width // head_dim, q_width // kv_width
+    grads = own_ref[...]
+    grad_ref[...] = jnp.dot(ht_ref[...], grads, preferred_element_type=jnp.float32).astype(
+        jnp.bfloat16
+    )
+    dh_ref[...] += times_t(grads, w_ref[...])
+
+
+def attend(h_one, qkv_w, cosine, sine, q_gain, k_gain, group):
+    span, head_dim = cosine.shape
+    step = (group + 2) * head_dim
+    heads = qkv_w.shape[1] // step
+    wide = pl.BlockSpec((span, step), lambda head: (0, head))
     q_spec = pl.BlockSpec((span, group * head_dim), lambda head: (0, head))
     k_spec = pl.BlockSpec((span, head_dim), lambda head: (0, head))
     table = pl.BlockSpec((span, head_dim), lambda head: (0, 0))
@@ -505,78 +525,519 @@
     return pl.pallas_call(
         attend_kernel,
         grid=(heads,),
-        in_specs=[q_spec, k_spec, k_spec, table, table, gain, gain],
-        out_specs=[q_spec, q_spec, k_spec, pl.BlockSpec((1, group, span), lambda h: (h, 0, 0))],
+        in_specs=[
+            pl.BlockSpec(h_one.shape, lambda head: (0, 0)),
+            pl.BlockSpec((qkv_w.shape[0], step), lambda head: (0, head)),
+            table,
+            table,
+            gain,
+            gain,
+        ],
+        out_specs=[
+            q_spec,
+            q_spec,
+            k_spec,
+            pl.BlockSpec((1, group, span), lambda h: (h, 0, 0)),
+            wide,
+        ],
         out_shape=[
-            jax.ShapeDtypeStruct((span, q_width), jnp.bfloat16),
-            jax.ShapeDtypeStruct((span, q_width), jnp.bfloat16),
-            jax.ShapeDtypeStruct((span, kv_width), jnp.bfloat16),
+            jax.ShapeDtypeStruct((span, heads * group * head_dim), jnp.bfloat16),
+            jax.ShapeDtypeStruct((span, heads * group * head_dim), jnp.bfloat16),
+            jax.ShapeDtypeStruct((span, heads * head_dim), jnp.bfloat16),
             jax.ShapeDtypeStruct((heads, group, span), jnp.float32),
+            jax.ShapeDtypeStruct((span, heads * step), jnp.float32),
         ],
         compiler_params=pltpu.CompilerParams(vmem_limit_bytes=VMEM_BYTES),
-        cost_estimate=pl.CostEstimate(
-            flops=2 * span * span * q_width * 2,
-            bytes_accessed=span * (q_width * 8 + kv_width * 8),
-            transcendentals=span * span * heads * group // 2,
+        cost_estimate=NO_COST,
+        name="attend",
+    )(h_one, qkv_w, cosine, sine, q_gain, k_gain)
+
+
+def norm_first_kernel(place_ref, mine_ref, other_ref, gain_ref, h_ref):
+    x, c = place_ref[0], place_ref[1]
+    half = mine_ref.shape[0]
+    for source, index in ((mine_ref, c), (other_ref, 1 - c)):
+        values = source[...].astype(jnp.float32)
+        values = jnp.where(x == 0, values, pltpu.roll(values, values.shape[1] // 2, 1))
+        normed = (values * rms_scale(values) * gain_ref[...]).astype(jnp.bfloat16)
+        h_ref[pl.ds(pl.multiple_of(index * half, half), half), :] = normed
+
+
+def norm_first(place, mine, other, gain):
+    half, width = mine.shape
+    return pl.pallas_call(
+        norm_first_kernel,
+        in_specs=[pl.BlockSpec(memory_space=pltpu.SMEM)]
+        + [pl.BlockSpec(memory_space=pltpu.VMEM)] * 3,
+        out_specs=pl.BlockSpec(memory_space=pltpu.VMEM),
+        out_shape=jax.ShapeDtypeStruct((2 * half, width), jnp.bfloat16),
+        compiler_params=pltpu.CompilerParams(vmem_limit_bytes=VMEM_BYTES),
+        cost_estimate=NO_COST,
+        name="norm_first",
+    )(place, mine, other, gain)
+
+
+def out_forward_kernel(place_ref, o_ref, w_ref, sent_ref, kept_ref):
+    product = jnp.dot(o_ref[...], w_ref[...], preferred_element_type=jnp.float32)
+
+    @pl.when(pl.program_id(0) == 0)
+    def _():
+        sent_ref[...] = product.astype(jnp.bfloat16)
+
+    @pl.when(pl.program_id(0) == 1)
+    def _():
+        kept_ref[...] = product
+
+
+def out_forward(place, out_low, out_w):
+    half, count = out_low.shape[0] // 2, out_low.shape[1]
+    width = out_w.shape[1]
+    whole = pl.BlockSpec((half, width), lambda i, place: (0, 0))
+    return pl.pallas_call(
+        out_forward_kernel,
+        grid_spec=pltpu.PrefetchScalarGridSpec(
+            num_scalar_prefetch=1,
+            grid=(2,),
+            in_specs=[
+                pl.BlockSpec(
+                    (half, count), lambda i, place: (i * place[1] + (1 - i) * (1 - place[1]), 0)
+                ),
+                pl.BlockSpec((count, width), lambda i, place: (0, 0)),
+            ],
+            out_specs=[whole, whole],
         ),
-        name="attend",
-    )(q_proj, k_proj, value_low, cosine, sine, q_gain, k_gain)
+        out_shape=[
+            jax.ShapeDtypeStruct((half, width), jnp.bfloat16),
+            jax.ShapeDtypeStruct((half, width), jnp.float32),
+        ],
+        compiler_params=pltpu.CompilerParams(vmem_limit_bytes=VMEM_BYTES),
+        cost_estimate=NO_COST,
+        name="out_forward",
+    )(place, out_low, out_w)
+
+
+def norm_second_kernel(place_ref, x_ref, kept_ref, got_ref, gain_ref, resid_ref, h_ref):
+    resid = x_ref[...].astype(jnp.float32) + kept_ref[...] + got_ref[...].astype(jnp.float32)
+    resid_ref[...] = resid
+    values = jnp.where(place_ref[0] == 0, resid, pltpu.roll(resid, resid.shape[1] // 2, 1))
+    h_ref[...] = (values * rms_scale(values) * gain_ref[...]).astype(jnp.bfloat16)
+
+
+def norm_second(place, tokens, kept, got, gain):
+    half, width = tokens.shape
+    rows = min(ROW_BLOCK, half)
+    spec = pl.BlockSpec((rows, width), lambda i, place: (i, 0))
+    return pl.pallas_call(
+        norm_second_kernel,
+        grid_spec=pltpu.PrefetchScalarGridSpec(
+            num_scalar_prefetch=1,
+            grid=(half // rows,),
+            in_specs=[spec, spec, spec, pl.BlockSpec((1, width), lambda i, place: (0, 0))],
+            out_specs=[spec, spec],
+        ),
+        out_shape=[
+            jax.ShapeDtypeStruct((half, width), jnp.float32),
+            jax.ShapeDtypeStruct((half, width), jnp.bfloat16),
+        ],
+        compiler_params=pltpu.CompilerParams(vmem_limit_bytes=VMEM_BYTES),
+        cost_estimate=NO_COST,
+        name="norm_second",
+    )(place, tokens, kept, got, gain)
 
 
 def attend_back(
-    query_low, key_low, value_low, grad_out, lse, q_proj, k_proj, cosine, sine, q_gain, k_gain
+    query_low, key_low, qkv, grad_out, lse, cosine, sine, q_gain, k_gain, h_one, qkv_w, part, dh=None
 ):
-    span, q_width = q_proj.shape
-    kv_width = k_proj.shape[1]
-    head_dim = q_gain.shape[1]
-    heads, group = kv_width // head_dim, q_width // kv_width
-    q_spec = pl.BlockSpec((span, group * head_dim), lambda head: (0, head))
-    k_spec = pl.BlockSpec((span, head_dim), lambda head: (0, head))
+    span, head_dim = cosine.shape
+    width = h_one.shape[1]
+    group = query_low.shape[1] // key_low.shape[1]
+    heads = key_low.shape[1] // head_dim // 2
+    base = part * heads
+    step = (group + 2) * head_dim
+    once = pl.Buffered(1)
+    wide = pl.BlockSpec((span, step), lambda head: (0, base + head))
+    q_spec = pl.BlockSpec((span, group * head_dim), lambda head: (0, base + head))
+    k_spec = pl.BlockSpec((span, head_dim), lambda head: (0, base + head))
     table = pl.BlockSpec((span, head_dim), lambda head: (0, 0))
     gain = pl.BlockSpec((1, head_dim), lambda head: (0, 0))
+    whole = pl.BlockSpec((span, width), lambda head: (0, 0), pipeline_mode=once)
+    first = dh is None
     return pl.pallas_call(
-        attend_back_kernel,
+        functools.partial(attend_back_kernel, first=first),
         grid=(heads,),
         in_specs=[
             q_spec,
             k_spec,
-            k_spec,
+            wide,
             q_spec,
-            pl.BlockSpec((1, group, span), lambda h: (h, 0, 0)),
-            q_spec,
-            k_spec,
+            pl.BlockSpec((1, group, span), lambda h: (base + h, 0, 0)),
             table,
             table,
             gain,
             gain,
-        ],
-        out_specs=[q_spec, k_spec, k_spec, pl.BlockSpec((1, 8, head_dim), lambda h: (h, 0, 0))],
+            whole,
+            pl.BlockSpec((width, step), lambda head: (0, base + head)),
+        ]
+        + ([] if first else [whole]),
+        out_specs=[
+            pl.BlockSpec((width, step), lambda head: (0, head)),
+            pl.BlockSpec((1, 8, head_dim), lambda h: (h, 0, 0)),
+            pl.BlockSpec((span, width), lambda head: (0, 0)),
+        ],
         out_shape=[
-            jax.ShapeDtypeStruct((span, q_width), jnp.bfloat16),
-            jax.ShapeDtypeStruct((span, kv_width), jnp.bfloat16),
-            jax.ShapeDtypeStruct((span, kv_width), jnp.bfloat16),
+            jax.ShapeDtypeStruct((width, heads * step), jnp.bfloat16),
             jax.ShapeDtypeStruct((heads, 8, head_dim), jnp.float32),
+            jax.ShapeDtypeStruct((span, width), jnp.float32),
         ],
         scratch_shapes=[
+            pltpu.VMEM((span, step), jnp.bfloat16),
             pltpu.VMEM((span, head_dim), jnp.float32),
             pltpu.VMEM((span, head_dim), jnp.float32),
+            pltpu.VMEM((width, span), jnp.bfloat16),
         ],
         compiler_params=pltpu.CompilerParams(vmem_limit_bytes=VMEM_BYTES),
-        cost_estimate=pl.CostEstimate(
-            flops=5 * span * span * q_width * 2,
-            bytes_accessed=span * (q_width * 12 + kv_width * 12),
-            transcendentals=span * span * heads * group // 2,
+        cost_estimate=NO_COST,
+        name="attend_back",
+    )(
+        query_low,
+        key_low,
+        qkv,
+        grad_out,
+        lse,
+        cosine,
+        sine,
+        q_gain,
+        k_gain,
+        h_one,
+        qkv_w,
+        *([] if first else [dh]),
+    )
+
+
+def norm_back_kernel(place_ref, values_ref, part_ref, got_ref, base_ref, gain_ref, *outs):
+    x = place_ref[0]
+
+    def flipped(values):
+        return jnp.where(x == 0, values, pltpu.roll(values, values.shape[1] // 2, 1))
+
+    *sums, low_ref, gain_out = outs
+    values = flipped(values_ref[...].astype(jnp.float32))
+    incoming = part_ref[...] + got_ref[...].astype(jnp.float32)
+    back, terms = norm_back(values, gain_ref[...], incoming)
+    total = base_ref[...].astype(jnp.float32) + flipped(back)
+    if sums:
+        sums[0][...] = total
+    low_ref[...] = total.astype(jnp.bfloat16)
+    summed = jnp.sum(terms, axis=0, keepdims=True)
+
+    @pl.when(pl.program_id(0) == 0)
+    def _():
+        gain_out[...] = jnp.zeros_like(gain_out)
+
+    gain_out[...] += summed
+
+
+def norm_gradient(place, values, part, got, base, gain, keep):
+    half, width = values.shape
+    rows = min(ROW_BLOCK, half)
+    steps = half // rows
+    spec = pl.BlockSpec((rows, width), lambda i, place: (i, 0))
+    line = pl.BlockSpec((1, width), lambda i, place: (0, 0))
+    shapes = [jax.ShapeDtypeStruct((half, width), jnp.bfloat16)]
+    if keep:
+        shapes = [jax.ShapeDtypeStruct((half, width), jnp.float32)] + shapes
+    return pl.pallas_call(
+        norm_back_kernel,
+        grid_spec=pltpu.PrefetchScalarGridSpec(
+            num_scalar_prefetch=1,
+            grid=(steps,),
+            in_specs=[
+                spec,
+                pl.BlockSpec((rows, width), lambda i, place: (place[1] * steps + i, 0)),
+                spec,
+                spec,
+                line,
+            ],
+            out_specs=[spec] * len(shapes) + [line],
         ),
-        name="attend_back",
-    )(query_low, key_low, value_low, grad_out, lse, q_proj, k_proj, cosine, sine, q_gain, k_gain)
+        out_shape=shapes + [jax.ShapeDtypeStruct((1, width), jnp.float32)],
+        compiler_params=pltpu.CompilerParams(vmem_limit_bytes=VMEM_BYTES),
+        cost_estimate=NO_COST,
+        name="norm_gradient",
+    )(place, values, part, got, base, gain)
+
+
+def whole_rows(place_ref, mine_ref, other_ref, whole_ref):
+    half, c = mine_ref.shape[0], place_ref[1]
+    whole_ref[pl.ds(pl.multiple_of(c * half, half), half), :] = mine_ref[...]
+    whole_ref[pl.ds(pl.multiple_of((1 - c) * half, half), half), :] = other_ref[...]
+
+
+def out_back_kernel(place_ref, mine_ref, other_ref, o_ref, w_ref, do_ref, grad_ref, dr_ref):
+    @pl.when(pl.program_id(0) == 0)
+    def _():
+        whole_rows(place_ref, mine_ref, other_ref, dr_ref)
+
+    do_ref[...] = times_t(dr_ref[...], w_ref[...]).astype(jnp.bfloat16)
+    grad_ref[...] = inner_rows(o_ref[...], dr_ref[...]).astype(jnp.bfloat16)
+
+
+def out_back(place, mine, other, out_low, out_w):
+    half, width = mine.shape
+    count = out_low.shape[1]
+    block = count // 4
+
+    def at(i):
+        return (i + 2) % 4
+
+    whole = pl.BlockSpec((half, width), lambda i: (0, 0))
+    return pl.pallas_call(
+        out_back_kernel,
+        grid=(4,),
+        in_specs=[
+            pl.BlockSpec(memory_space=pltpu.SMEM),
+            whole,
+            whole,
+            pl.BlockSpec((2 * half, block), lambda i: (0, at(i))),
+            pl.BlockSpec((block, width), lambda i: (at(i), 0)),
+        ],
+        out_specs=[
+            pl.BlockSpec((2 * half, block), lambda i: (0, at(i))),
+            pl.BlockSpec((block, width), lambda i: (at(i), 0)),
+        ],
+        out_shape=[
+            jax.ShapeDtypeStruct((2 * half, count), jnp.bfloat16),
+            jax.ShapeDtypeStruct((count, width), jnp.bfloat16),
+        ],
+        scratch_shapes=[pltpu.VMEM((2 * half, width), jnp.bfloat16)],
+        compiler_params=pltpu.CompilerParams(vmem_limit_bytes=VMEM_BYTES),
+        cost_estimate=NO_COST,
+        name="out_back",
+    )(place, mine, other, out_low, out_w)
+
+
+def half_kernel(place_ref, whole_ref, half_ref):
+    half_ref[...] = whole_ref[...].astype(half_ref.dtype)
+
+
+def other_half(place, values):
+    half, width = values.shape[0] // 2, values.shape[1]
+    rows = min(ROW_BLOCK, half)
+    steps = half // rows
+    return pl.pallas_call(
+        half_kernel,
+        grid_spec=pltpu.PrefetchScalarGridSpec(
+            num_scalar_prefetch=1,
+            grid=(steps,),
+            in_specs=[
+                pl.BlockSpec((rows, width), lambda i, place: ((1 - place[1]) * steps + i, 0))
+            ],
+            out_specs=pl.BlockSpec((rows, width), lambda i, place: (i, 0)),
+        ),
+        out_shape=jax.ShapeDtypeStruct((half, width), jnp.bfloat16),
+        compiler_params=pltpu.CompilerParams(vmem_limit_bytes=VMEM_BYTES),
+        cost_estimate=NO_COST,
+        name="other_half",
+    )(place, values)
+
+
+def mlp_kernel(place_ref, hm_ref, ho_ref, dm_ref, do_ref, gu_ref, down_ref, *rest, block, first):
+    res_in, dh_in = (None, None) if first else rest[:2]
+    ggu_ref, gdown_ref, res_ref, dh_ref, h_ref, dy_ref, ht_ref = rest[0 if first else 2 :]
+
+    @pl.when(pl.program_id(0) == 0)
+    def _():
+        whole_rows(place_ref, hm_ref, ho_ref, h_ref)
+        whole_rows(place_ref, dm_ref, do_ref, dy_ref)
+        ht_ref[...] = h_ref[...].T
+        res_ref[...] = jnp.zeros_like(res_ref) if first else res_in[...]
+        dh_ref[...] = jnp.zeros_like(dh_ref) if first else dh_in[...]
+
+    weights = gu_ref[...]
+    both = jnp.dot(h_ref[...], weights, preferred_element_type=jnp.float32)
+    gate, up_val = both[:, :block], both[:, block:]
+    sigmoid_gate = jax.nn.sigmoid(gate)
+    active = gate * sigmoid_gate
+    grad_hidden = times_t(dy_ref[...], down_ref[...])
+    hidden = (active * up_val).astype(jnp.bfloat16)
+    grad_gate = (
+        grad_hidden * up_val * sigmoid_gate * (1.0 + gate * (1.0 - sigmoid_gate))
+    ).astype(jnp.bfloat16)
+    grads = jnp.concatenate([grad_gate, (grad_hidden * active).astype(jnp.bfloat16)], axis=1)
+    res_ref[...] += jnp.dot(hidden, down_ref[...], preferred_element_type=jnp.float32)
+    dh_ref[...] += times_t(grads, weights)
+    ggu_ref[...] = jnp.dot(ht_ref[...], grads, preferred_element_type=jnp.float32).astype(
+        jnp.bfloat16
+    )
+    gdown_ref[...] = inner_rows(hidden, dy_ref[...]).astype(jnp.bfloat16)
+
+
+def mlp(place, h_halves, dy_halves, gu_w, down_w, part, sums=None):
+    half, width = h_halves[0].shape
+    span = 2 * half
+    units = down_w.shape[0] // 2
+    block = math.gcd(UNIT_BLOCK, units)
+    steps = units // block
+    base = part * steps
+    once = pl.Buffered(1)
+    piece = pl.BlockSpec((half, width), lambda j: (0, 0), pipeline_mode=once)
+    whole = pl.BlockSpec((span, width), lambda j: (0, 0), pipeline_mode=once)
+    total = pl.BlockSpec((span, width), lambda j: (0, 0))
+    first = sums is None
+    return pl.pallas_call(
+        functools.partial(mlp_kernel, block=block, first=first),
+        grid=(steps,),
+        in_specs=[
+            pl.BlockSpec(memory_space=pltpu.SMEM),
+            piece,
+            piece,
+            piece,
+            piece,
+            pl.BlockSpec((width, 2 * block), lambda j: (0, base + j)),
+            pl.BlockSpec((block, width), lambda j: (base + j, 0)),
+        ]
+        + ([] if first else [whole, whole]),
+        out_specs=[
+            pl.BlockSpec((width, 2 * block), lambda j: (0, j)),
+            pl.BlockSpec((block, width), lambda j: (j, 0)),
+            total,
+            total,
+        ],
+        out_shape=[
+            jax.ShapeDtypeStruct((width, 2 * units), jnp.bfloat16),
+            jax.ShapeDtypeStruct((units, width), jnp.bfloat16),
+            jax.ShapeDtypeStruct((span, width), jnp.float32),
+            jax.ShapeDtypeStruct((span, width), jnp.float32),
+        ],
+        scratch_shapes=[
+            pltpu.VMEM((span, width), jnp.bfloat16),
+            pltpu.VMEM((span, width), jnp.bfloat16),
+            pltpu.VMEM((width, span), jnp.bfloat16),
+        ],
+        compiler_params=pltpu.CompilerParams(vmem_limit_bytes=VMEM_BYTES),
+        cost_estimate=NO_COST,
+        name="mlp",
+    )(place, *h_halves, *dy_halves, gu_w, down_w, *(sums or ()))
+
+
+def copy_kernel(plan, place_ref, *refs):
+    sems = refs[-1]
+    copies = [
+        pltpu.make_async_copy(source, target, sems.at[index])
+        for index, (source, target) in enumerate(plan(place_ref, refs[:-1]))
+    ]
+    for copy in copies:
+        copy.start()
+    for copy in copies:
+        copy.wait()
+
+
+def copied(plan, count, place, operands, shapes, name):
+    anywhere = pl.BlockSpec(memory_space=pl.ANY)
+    return pl.pallas_call(
+        functools.partial(copy_kernel, plan),
+        in_specs=[pl.BlockSpec(memory_space=pltpu.SMEM)] + [anywhere] * len(operands),
+        out_specs=[pl.BlockSpec(memory_space=pltpu.VMEM)] * len(shapes),
+        out_shape=[jax.ShapeDtypeStruct(shape, jnp.bfloat16) for shape in shapes],
+        scratch_shapes=[pltpu.SemaphoreType.DMA((count,))],
+        compiler_params=pltpu.CompilerParams(vmem_limit_bytes=VMEM_BYTES),
+        cost_estimate=NO_COST,
+        name=name,
+    )(place, *operands)
+
+
+def column_moves(sources, target, groups, first, second, row, rows):
+    moves, at = [], 0
+    for block in (first, second):
+        for group in range(groups):
+            for source in sources:
+                quarter = source.shape[1] // 4
+                count = quarter // groups
+                start = pl.multiple_of(block * quarter + group * count, math.gcd(count, quarter))
+                moves.append(
+                    (
+                        source.at[pl.ds(row, rows), pl.ds(start, count)],
+                        target.at[pl.ds(0, rows), pl.ds(at, count)],
+                    )
+                )
+                at += count
+    return moves
+
+
+def shared_rows(place_ref, start, rows):
+    count = rows // 4
+    near_y = start + place_ref[2] * count
+    near_z = start + 2 * count + place_ref[3] * count
+    return pl.multiple_of(near_y, count), pl.multiple_of(near_z, count), count
+
+
+def send_columns(place, weights, groups, name):
+    def plan(place_ref, refs):
+        x, c = place_ref[0], place_ref[1]
+        sources, targets = refs[:-2], refs[-2:]
+        row_y, row_z, count = shared_rows(place_ref, 0, sources[0].shape[0])
+        moves = []
+        for row, target in zip((row_y, row_z), targets):
+            moves += column_moves(
+                sources, target, groups, 2 * (1 - x) + c, 2 * x + c, row, count
+            )
+        return moves
+
+    shape = (weights[0].shape[0] // 4, sum(w.shape[1] for w in weights) // 2)
+    return copied(plan, 4 * groups * len(weights), place, weights, [shape] * 2, name)
+
+
+def send_rows(place, weight, name):
+    def plan(place_ref, refs):
+        source, *targets = refs
+        half = source.shape[0] // 2
+        row_y, row_z, count = shared_rows(place_ref, place_ref[1] * half, half)
+        return [
+            (source.at[pl.ds(row, count)], target)
+            for row, target in zip((row_y, row_z), targets)
+        ]
+
+    shape = (weight.shape[0] // 8, weight.shape[1])
+    return copied(plan, 2, place, [weight], [shape] * 2, name)
+
+
+def far_moves(place_ref, parts, target, rows):
+    near_y, near_z, far_y, far_z = parts
+    row_y, row_z, count = shared_rows(place_ref, rows, rows)
+    other_y = pl.multiple_of(rows + (1 - place_ref[2]) * count, count)
+    other_z = pl.multiple_of(rows + 2 * count + (1 - place_ref[3]) * count, count)
+    return [
+        (part, target.at[pl.ds(row, count)])
+        for part, row in ((near_y, row_y), (near_z, row_z), (far_y, other_y), (far_z, other_z))
+    ]
+
+
+def join_columns(place, weights, groups, parts):
+    def plan(place_ref, refs):
+        x, c = place_ref[0], place_ref[1]
+        sources, parts, target = refs[:-5], refs[-5:-1], refs[-1]
+        rows = sources[0].shape[0]
+        moves = column_moves(sources, target, groups, 2 * x + c, 2 * (1 - x) + c, 0, rows)
+        return moves + far_moves(place_ref, parts, target, rows)
+
+    shape = (2 * weights[0].shape[0], parts[0].shape[1])
+    count = 2 * groups * len(weights) + 4
+    return copied(plan, count, place, [*weights, *parts], [shape], "join_columns")[0]
+
+
+def join_rows(place, weight, parts):
+    def plan(place_ref, refs):
+        source, *parts, target = refs
+        rows = source.shape[0] // 2
+        row = pl.multiple_of(place_ref[1] * rows, rows)
+        moves = [(source.at[pl.ds(row, rows)], target.at[pl.ds(0, rows)])]
+        return moves + far_moves(place_ref, parts, target, rows)
+
+    return copied(plan, 5, place, [weight, *parts], [weight.shape], "join_rows")[0]
 
 
 def swap(values, axis):
     return lax.ppermute(values, axis, [(0, 1), (1, 0)])
-
-
-def turn(values):
-    return lax.ppermute(values, ("c", "x"), [(0, 0), (1, 2), (2, 1), (3, 3)])
 
 
 def rows_at(values, index, count):
@@ -593,6 +1054,24 @@
         jnp.concatenate([mine, other], axis=axis),
         jnp.concatenate([other, mine], axis=axis),
     )
+
+
+def hold(value, *others):
+    return lax.optimization_barrier((value, *others))[0]
+
+
+def mixed(parts, groups):
+    pieces = []
+    for group in range(groups):
+        for part in parts:
+            count = part.shape[1] // groups
+            pieces.append(part[:, group * count : (group + 1) * count])
+    return jnp.concatenate(pieces, axis=1)
+
+
+def halves_swapped(values):
+    mid = values.shape[1] // 2
+    return jnp.concatenate([values[:, mid:], values[:, :mid]], axis=1)
 
 
 def paired(
@@ -611,219 +1090,307 @@
     w_up,
     w_down,
 ):
-    x, c = lax.axis_index("x"), lax.axis_index("c")
+    x, c, y, za = [lax.axis_index(axis) for axis in ("x", "c", "y", "za")]
     half, width = tokens.shape
     head_dim = query_gain.shape[0] * 2
     bf16, f32 = jnp.bfloat16, jnp.float32
+    part, q_part = norm1_gain.shape[0], query_gain.shape[0]
+    group = w_query.shape[1] // w_key.shape[1]
+    head_groups = w_key.shape[1] // head_dim // 4
+    unit_groups = w_gate.shape[1] // 4 // math.gcd(UNIT_BLOCK, w_gate.shape[1] // 4)
 
     def flip(values):
-        mid = values.shape[1] // 2
-        swapped = jnp.concatenate([values[:, mid:], values[:, :mid]], axis=1)
-        return jnp.where(x == 0, values, swapped)
+        return jnp.where(x == 0, values, halves_swapped(values))
 
     def both(values):
         return ordered(c == 0, values, swap(values, "c"))
 
-    def fetch(piece):
-        count = piece.shape[0] // 2
-        y = lax.axis_index("y")
-        near = swap(rows_at(piece, y, count), "x")
-        return ordered(y == 0, near, swap(near, "y"))
-
-    def column_parts(weight):
-        count = weight.shape[1] // 4
-        return cols_at(weight, 2 * x + c, count), cols_at(weight, 2 * (1 - x) + c, count)
-
-    def column_weights(weights):
-        parts = [column_parts(weight) for weight in weights]
-        own = jnp.concatenate([part for pair in parts for part in pair], axis=1)
-        sent = jnp.concatenate([part for pair in parts for part in pair[::-1]], axis=1)
-        return jnp.concatenate([own, fetch(sent)], axis=0)
-
-    def row_weights(weight):
-        own = rows_at(weight, c, weight.shape[0] // 2)
-        return jnp.concatenate([own, fetch(own)], axis=0)
-
-    own_tokens = turn(tokens)
-    all_tokens = both(own_tokens)
-    places = both(turn(positions))
-    gains = jnp.concatenate([norm1_gain, norm2_gain, query_gain, key_gain])
-    far_gains = swap(gains, "x")
-    gains, far_gains = gains.astype(f32), far_gains.astype(f32)
-    part = norm1_gain.shape[0]
-    q_part = query_gain.shape[0]
-    gain_one = jnp.concatenate([gains[:part], far_gains[:part]])
-    gain_two = jnp.concatenate([gains[part : 2 * part], far_gains[part : 2 * part]])
+    def turn(values):
+        return jnp.where(x == c, values, lax.ppermute(values, ("c", "x"), [(1, 2), (2, 1)]))
+
+    place = jnp.stack([x, c, y, za]).astype(jnp.int32)
+
+    small = [norm1_gain, norm2_gain, query_gain, key_gain, positions]
+    small = jnp.concatenate([item.astype(f32) for item in small])
+    small_got = swap(small, "x")
+    head_weights, unit_weights = [w_query, w_key, w_value], [w_gate, w_up]
+    first = hold(place, small_got)
+
+    def near(sent):
+        return [swap(piece, "x") for piece in sent]
+
+    def relayed(parts):
+        return [*parts, swap(parts[0], "y"), swap(parts[1], "za")]
+
+    head_sent = send_columns(first, head_weights, head_groups, "send_heads")
+    head_near = near(head_sent)
+    own_tokens = turn(hold(tokens, head_sent[0]))
+    out_sent = send_rows(hold(place, head_sent[0]), w_out, "send_out")
+    out_near = near(out_sent)
+    unit_sent = send_columns(hold(place, out_sent[0]), unit_weights, unit_groups, "send_units")
+    down_sent = send_rows(hold(place, unit_sent[0]), w_down, "send_down")
+    unit_near = near([hold(piece, head_near[0]) for piece in unit_sent])
+    down_near = near([hold(piece, head_near[1]) for piece in down_sent])
+    own_cot = turn(hold(cotangent, head_near[1]))
+
+    gains, far_gains = small[: 2 * (part + q_part)], small_got[: 2 * (part + q_part)]
+    own_places, far_places = small[2 * (part + q_part) :], small_got[2 * (part + q_part) :]
+    places = ordered(x == 0, own_places, far_places)
+    places = jnp.where(x == c, places, swap(places, "c"))
+    gain_one = jnp.concatenate([gains[:part], far_gains[:part]])[None]
+    gain_two = jnp.concatenate([gains[part : 2 * part], far_gains[part : 2 * part]])[None]
     q_gain = ordered(
         x == 0, gains[2 * part : 2 * part + q_part], far_gains[2 * part : 2 * part + q_part]
     )[None]
     k_gain = ordered(x == 0, gains[2 * part + q_part :], far_gains[2 * part + q_part :])[None]
-
-    qkv_w = column_weights([w_query, w_key, w_value])
-    out_w = row_weights(w_out)
-    own_cot = turn(cotangent)
-    all_cot = both(own_cot)
-    gu_w = column_weights([w_gate, w_up])
-    down_w = row_weights(w_down)
-
     cosine, sine = rotation_tables(places, head_dim)
     cosine = jnp.concatenate([cosine[:, 0], cosine[:, 0]], axis=-1)
     sine = jnp.concatenate([-sine[:, 0], sine[:, 0]], axis=-1)
 
-    x_all = flip(all_tokens).astype(f32)
-    h_one = (x_all * rms_scale(x_all) * gain_one).astype(bf16)
-    q_width = w_query.shape[1] // 2
-    kv_width = w_key.shape[1] // 2
-    qkv = jnp.dot(h_one, qkv_w, preferred_element_type=f32)
-    q_proj, k_proj = qkv[:, :q_width], qkv[:, q_width : q_width + kv_width]
-    value_low = qkv[:, q_width + kv_width :].astype(bf16)
-    out_low, query_low, key_low, lse = attend(
-        q_proj, k_proj, value_low, cosine, sine, q_gain, k_gain
-    )
-
-    def shared(left, right, product):
-        sent = product(rows_at(left, 1 - c, half), right).astype(bf16)
-        got = swap(sent, "c")
-        return product(rows_at(left, c, half), right) + got.astype(f32)
-
-    def plain(left, right):
-        return jnp.dot(left, right, preferred_element_type=f32)
-
-    x_own = own_tokens.astype(f32)
-    resid = x_own + shared(out_low, out_w, plain)
-    resid_flip = flip(resid)
-    h_two = both((resid_flip * rms_scale(resid_flip) * gain_two).astype(bf16))
-    units = w_down.shape[0]
-    gate_up = jnp.dot(h_two, gu_w, preferred_element_type=f32)
-    gate, up_val = gate_up[:, :units], gate_up[:, units:]
-    sigmoid_gate = jax.nn.sigmoid(gate)
-    hidden_low = (gate * sigmoid_gate * up_val).astype(bf16)
-    grad_hidden = times_t(all_cot, down_w)
-    grad_gate_low = (
-        grad_hidden * up_val * sigmoid_gate * (1.0 + gate * (1.0 - sigmoid_gate))
-    ).astype(bf16)
-    grad_up_low = (grad_hidden * gate * sigmoid_gate).astype(bf16)
-    grad_gu = jnp.concatenate([grad_gate_low, grad_up_low], axis=1)
+    h_one = norm_first(place, own_tokens, swap(own_tokens, "c"), gain_one)
+    qkv_w = join_columns(place, head_weights, head_groups, relayed(head_near))
+    out_parts = relayed(out_near)
+    out_w = join_rows(place, w_out, out_parts)
+    unit_parts = relayed(unit_near)
+    out_low, query_low, key_low, lse, qkv = attend(
+        hold(h_one, unit_near[0], out_parts[3]), qkv_w, cosine, sine, q_gain, k_gain, group
+    )
+    out_low = hold(out_low, unit_near[1], down_near[0], unit_parts[2])
+    down_parts = relayed(down_near)
+    out_sent, out_kept = out_forward(place, out_low, out_w)
+    out_got = hold(swap(out_sent, "c"), down_near[1])
+    resid, h_mine = norm_second(place, own_tokens, out_kept, out_got, gain_two)
+    h_mine = hold(h_mine, unit_parts[3], down_parts[2])
+    h_halves = (h_mine, swap(h_mine, "c"))
+    cot_halves = (own_cot, swap(own_cot, "c"))
+    gu_w = join_columns(place, unit_weights, unit_groups, unit_parts)
+    down_w = join_rows(place, w_down, down_parts)
 
     def rs(values, axis):
         index, count = lax.axis_index(axis), values.shape[0] // 2
-        return rows_at(values, index, count) + swap(rows_at(values, 1 - index, count), axis)
-
-    def ag(values, axis):
-        return ordered(lax.axis_index(axis) == 0, values, swap(values, axis))
-
-    def total_of(values):
-        values = rs(values, "y")
-        values = rs(values, "za")
-        values = values + swap(values, "zb")
-        values = ag(values, "za")
-        return ag(values, "y")
-
-    def grad_rows(left, right):
-        rows = left.shape[1] // 2
-        sent = inner_rows(left[:, rows:], right).astype(bf16)
-        got = swap(sent, "x")
-        mine = total_of((inner_rows(left[:, :rows], right) + got.astype(f32)).astype(bf16))
-        return ordered(c == 0, mine, swap(mine, "c")).astype(f32)
-
-    def grad_cols(left, right, widths):
-        rows = left.shape[1] // 2
-        sent = inner_rows(left[:, rows:], right).astype(bf16)
-        got = swap(sent, "x")
-        kept = inner_rows(left[:, :rows], right)
-        pieces, at = [], 0
-        for count in widths:
-            pieces += [got[:, at + count : at + 2 * count], got[:, at : at + count]]
-            at += 2 * count
-        mine = total_of((kept + jnp.concatenate(pieces, axis=1).astype(f32)).astype(bf16))
-        other = swap(mine, "c")
+        return rows_at(values, index, count), swap(rows_at(values, 1 - index, count), axis)
+
+    grad_gu_far, grad_down_far, res_part, dh_part = mlp(
+        place, h_halves, cot_halves, gu_w, down_w, 1
+    )
+    down_far_kept, down_far_got = rs(grad_down_far, "y")
+    far_got = swap(grad_gu_far[part:], "x")
+    grad_gu_near, grad_down_near, res_part, dh_part = mlp(
+        place, h_halves, cot_halves, gu_w, down_w, 0, (res_part, dh_part)
+    )
+    dh_part = hold(dh_part, down_far_got)
+    down_got = swap(down_far_kept + down_far_got, "x")
+    down_near_kept, down_near_got = rs(grad_down_near, "y")
+    near_rows = part // 2
+    near_gots = [
+        swap(grad_gu_near[part : part + near_rows], "x"),
+        swap(grad_gu_near[part + near_rows :], "x"),
+    ]
+
+    class Piece:
+        def __init__(self, kept, got, path):
+            self.kept, self.got, self.path, self.back = kept, got, list(path), []
+
+        def step(self, *others):
+            got = hold(self.got, *others)
+            if self.back and self.back[0] == "c":
+                self.kept, self.got = ordered(c == 0, self.kept, got), None
+                return self.kept
+            if self.back:
+                values = ordered(lax.axis_index(self.back[0]) == 0, self.kept, got)
+                self.back = self.back[1:]
+            else:
+                values = self.kept + got
+            if self.path:
+                axis = self.path[0]
+                self.path = self.path[1:]
+                if self.path:
+                    self.kept, self.got = rs(values, axis)
+                    self.turned = [axis] + getattr(self, "turned", [])
+                else:
+                    self.kept, self.got = values, swap(values, axis)
+                    self.last = True
+                return self.kept
+            if not self.back and getattr(self, "last", False):
+                self.last = False
+                self.back = self.turned + ["c"]
+            self.kept, self.got = values, swap(values, self.back[0])
+            return self.kept
+
+    near_piece = Piece(grad_gu_near[:part], far_got, ("y", "za", "zb"))
+
+    dh_got = swap(other_half(place, dh_part), "c")
+    grad_resid, resid_low, gain_two_sum = norm_gradient(
+        place, resid, dh_part, dh_got, own_cot, gain_two, True
+    )
+    resid_low = hold(resid_low, far_got)
+    grad_att, grad_out = out_back(place, resid_low, swap(resid_low, "c"), out_low, out_w)
+    grad_att, down_near_got, near_got = lax.optimization_barrier(
+        (grad_att, down_near_got, near_gots[0])
+    )
+    near_got = jnp.concatenate([near_got, near_gots[1]], axis=0)
+    far_piece = Piece(grad_gu_far[:part], near_got, ("y", "za", "zb"))
+    mark = near_piece.step(grad_att)
+    out_rows = grad_out.shape[0] // 2
+    out_piece = Piece(grad_out[:out_rows], swap(grad_out[out_rows:], "x"), ("y", "za", "zb"))
+    down_near_total = down_near_kept + hold(down_near_got, mark)
+    down_piece = Piece(down_near_total, down_got, ("za", "zb"))
+    down_piece.turned = ["y"]
+
+    def back_of(index, dh, *others):
+        grads = hold(grad_att, *others)
+        return attend_back(
+            query_low,
+            key_low,
+            qkv,
+            grads,
+            lse,
+            cosine,
+            sine,
+            q_gain,
+            k_gain,
+            h_one,
+            qkv_w,
+            index,
+            dh,
+        )
+
+    grad_far, head_gains_far, dh_part = back_of(1, None, down_near_total)
+    grad_far, near_piece.got, near_gots[1], down_piece.got = lax.optimization_barrier(
+        (grad_far, near_piece.got, near_gots[1], down_piece.got)
+    )
+    far_piece.got = jnp.concatenate([near_gots[0], near_gots[1]], axis=0)
+    qkv_far_got = swap(grad_far[part:], "x")
+    mark = far_piece.step(grad_far)
+    mark = near_piece.step(mark)
+    mark = down_piece.step(mark)
+    grad_near, head_gains_near, dh_part = back_of(0, dh_part, mark)
+    grad_near, near_piece.got, far_piece.got, down_piece.got, out_piece.got = (
+        lax.optimization_barrier(
+            (grad_near, near_piece.got, far_piece.got, down_piece.got, out_piece.got)
+        )
+    )
+    qkv_near_got = swap(grad_near[part:], "x")
+    qkv_near_piece = Piece(grad_near[:part], qkv_far_got, ("y", "za", "zb"))
+    qkv_far_piece = Piece(grad_far[:part], qkv_near_got, ("y", "za", "zb"))
+
+    dh_sent = other_half(place, dh_part)
+    dh_got = swap(dh_sent, "c")
+    mark = near_piece.step(dh_sent)
+    mark = down_piece.step(mark)
+    mark = far_piece.step(mark)
+    mark = out_piece.step(mark)
+    input_sum, gain_one_sum = norm_gradient(
+        place, own_tokens, dh_part, hold(dh_got, mark), grad_resid, gain_one, False
+    )
+    head_gains = jnp.sum(head_gains_near, axis=0) + jnp.sum(head_gains_far, axis=0)
+    gain_sums = [gain_one_sum[0], gain_two_sum[0]]
+    head_sums = jnp.stack([head_gains[0], head_gains[1]])
+    head_sums = jnp.where(x == 0, head_sums, jnp.roll(head_sums, q_part, axis=1))
+
+    def gain_rows(at):
+        pieces = [values[at * part : (at + 1) * part] for values in gain_sums]
+        pieces += [values[at * q_part : (at + 1) * q_part] for values in head_sums]
+        flat = jnp.concatenate(pieces)
+        pad = -flat.shape[0] % (8 * head_dim)
+        return jnp.concatenate([flat, jnp.zeros((pad,), f32)]).reshape(-1, head_dim)
+
+    def rows_result(piece):
+        return piece.step(mark).astype(f32)
+
+    def columns_result(near, far, widths, groups):
+        others = [hold(piece.got, mark) for piece in (near, far)]
+        step = sum(widths)
         results, at = [], 0
         for count in widths:
-
-            def block(values, index):
-                return jnp.where(
-                    x == index,
-                    values[:, at : at + count],
-                    values[:, at + count : at + 2 * count],
-                )
-
-            results.append(
-                jnp.concatenate(
-                    [
-                        piece
-                        for index in range(2)
-                        for piece in (
-                            jnp.where(c == 0, block(mine, index), block(other, index)),
-                            jnp.where(c == 0, block(other, index), block(mine, index)),
-                        )
-                    ],
-                    axis=1,
-                ).astype(f32)
-            )
-            at += 2 * count
+            pieces = []
+            for index in range(2):
+                mine = jnp.where(x == index, near.kept, far.kept)
+                other = jnp.where(x == index, others[0], others[1])
+                for core in range(2):
+                    chosen = jnp.where(c == core, mine, other)
+                    for step_at in range(groups):
+                        first = step_at * step + at
+                        pieces.append(chosen[:, first : first + count])
+            results.append(jnp.concatenate(pieces, axis=1).astype(f32))
+            at += count
         return results
 
-    grad_down = grad_rows(hidden_low, all_cot)
-    grad_gate_w, grad_up_w = grad_cols(h_two, grad_gu, [units // 2, units // 2])
-    result = turn((resid + shared(hidden_low, down_w, plain)).astype(bf16))
-
-    grad_h_two = shared(grad_gu, gu_w, times_t)
-    resid_part, gain_two_terms = norm_back(resid_flip, gain_two, grad_h_two)
-    grad_resid = own_cot.astype(f32) + flip(resid_part)
-    resid_low = both(grad_resid.astype(bf16))
-    grad_out_w = grad_rows(out_low, resid_low)
-    grad_att = times_t(resid_low, out_w).astype(bf16)
-    grad_query, grad_key, grad_value, head_gains = attend_back(
-        query_low,
-        key_low,
-        value_low,
-        grad_att,
-        lse,
-        q_proj,
-        k_proj,
-        cosine,
-        sine,
-        q_gain,
-        k_gain,
-    )
-    grad_qkv = jnp.concatenate([grad_query, grad_key, grad_value], axis=1)
-    grad_query_w, grad_key_w, grad_value_w = grad_cols(
-        h_one, grad_qkv, [q_width // 2, kv_width // 2, kv_width // 2]
-    )
-    grad_h_one = shared(grad_qkv, qkv_w, times_t)
-    input_part, gain_one_terms = norm_back(flip(x_own), gain_one, grad_h_one)
-    grad_input = turn((grad_resid + flip(input_part)).astype(bf16)).astype(f32)
-
-    def natural(values):
-        return ordered(x == 0, values[:part], values[part:])
-
-    gain_sums = jnp.concatenate(
-        [
-            natural(jnp.sum(gain_one_terms, axis=0)),
-            natural(jnp.sum(gain_two_terms, axis=0)),
-            jnp.sum(head_gains[:, 0], axis=0),
-            jnp.sum(head_gains[:, 1], axis=0),
-        ]
-    )
-    gain_sums = lax.psum(gain_sums, ("zb", "za", "y", "c", "x"))
-
-    def own_gain(start, count):
-        return lax.dynamic_slice_in_dim(gain_sums, start + x * count, count)
+    gain_state = [gain_rows(0), swap(gain_rows(1), "x")]
+
+    def gain_step(axis, *others):
+        gain_state[0] = gain_state[0] + hold(gain_state[1], *others)
+        if axis:
+            gain_state[1] = swap(gain_state[0], axis)
+        return gain_state[0]
+
+    def result_start(*others):
+        part_sum = hold(res_part, *others)
+        sent = swap(other_half(place, part_sum), "c")
+        total = resid + rows_at(part_sum, c, half) + sent.astype(f32)
+        return total.astype(bf16)
+
+    unit_block = w_gate.shape[1] // 4 // unit_groups
+    mark = input_sum
+    mark = qkv_near_piece.step(mark)
+    mark = near_piece.step(mark)
+    mark = out_piece.step(mark)
+    mark = gain_step("y", mark)
+    mark = down_piece.step(mark)
+    mark = far_piece.step(mark)
+    mark = qkv_near_piece.step(mark)
+    mark = qkv_far_piece.step(mark)
+    mark = gain_step("za", mark)
+    mark = near_piece.step(mark)
+    mark = out_piece.step(mark)
+    grad_input = turn(hold(input_sum, mark)).astype(f32)
+    mark = down_piece.step(mark)
+    mark = qkv_far_piece.step(mark)
+    mark = gain_step("zb", mark)
+    mark = far_piece.step(mark)
+    mark = near_piece.step(mark)
+    mark = qkv_near_piece.step(mark)
+    mark = gain_step("c", mark)
+    mark = out_piece.step(mark)
+    mark = down_piece.step(mark)
+    mark = grad_down_w = rows_result(down_piece)
+    mark = gain_step(None, mark)
+    mark = qkv_far_piece.step(mark)
+    mark = far_piece.step(mark)
+    mark = qkv_near_piece.step(mark)
+    mark = out_piece.step(mark)
+    mark = far_piece.step(mark)
+    result = turn(result_start(mark))
+    grad_gate_w, grad_up_w = columns_result(
+        near_piece, far_piece, [unit_block, unit_block], unit_groups
+    )
+    mark = grad_up_w
+    mark = qkv_far_piece.step(mark)
+    mark = out_piece.step(mark)
+    mark = qkv_near_piece.step(mark)
+    mark = grad_out_w = rows_result(out_piece)
+    mark = qkv_far_piece.step(mark)
+    mark = qkv_near_piece.step(mark)
+    mark = qkv_far_piece.step(mark)
+    grad_query_w, grad_key_w, grad_value_w = columns_result(
+        qkv_near_piece, qkv_far_piece, [group * head_dim, head_dim, head_dim], head_groups
+    )
+    total_gains = gain_state[0].reshape(-1)
 
     return (
         result,
         grad_input,
-        own_gain(0, part),
+        total_gains[:part],
         grad_query_w,
         grad_key_w,
         grad_value_w,
         grad_out_w,
-        own_gain(4 * part, q_part),
-        own_gain(4 * part + 2 * q_part, q_part),
-        own_gain(2 * part, part),
+        total_gains[2 * part : 2 * part + q_part],
+        total_gains[2 * part + q_part : 2 * (part + q_part)],
+        total_gains[part : 2 * part],
         grad_gate_w,
         grad_up_w,
-        grad_down,
+        grad_down_w,
     )
 
 

time: 778 us -> 578 us (0.74); the launches traced: 766 us -> 574 us
  waiting for transfers between devices: 330 us -> 185 us
  Pallas kernels: 51.5 us -> 194 us
  matrix products: 127 us -> 0 us
  blocking collectives: 38 us -> 0 us
  starting transfers between devices: 98 us -> 84.2 us
    ppermute x46 -> x75, waiting for transfers between devices: 330 us -> 185 us  [swap(): return lax.ppermute(values, axis, [(0, 1), (1, 0)])]
    pallas_call x2 -> x22, Pallas kernels: 51.5 us -> 194 us  [the longest x2 46.7 us: mlp(): pl.pallas_call(functools.partial(mlp_kernel, block=block, first=first), g...]
    dot_general x20 -> x0, matrix products: 127 us -> none  [the longest x6 38.6 us: times_t(): lax.dot_general(left, right, (((1,), (1,)), ((), ())), preferred_element_...]
    psum x1 -> x0, blocking collectives: 38 us -> none  [paired(): gain_sums = lax.psum(gain_sums, ('zb', 'za', 'y', 'c', 'x'))]
    ppermute x5 -> x4, starting transfers between devices: 39 us -> 4.25 us  [turn(): lax.ppermute(values, ('c', 'x'), [(1, 2), (2, 1)])]
    ppermute x46 -> x75, starting transfers between devices: 59 us -> 80 us  [swap(): return lax.ppermute(values, axis, [(0, 1), (1, 0)])]
    add x12 -> x30, other arithmetic: 2.52 us -> 23.2 us  [the longest x22 18.9 us: step(): values = self.kept + got]
    select_n x17 -> x14, other arithmetic: 22.8 us -> 10.7 us  [ordered(): jnp.where(first, jnp.concatenate([mine, other], axis=axis), jnp.concatena...]
  transfers between devices with their start and end apart: 51 -> 79, of which waited for: 19 -> 28; matrix products, arithmetic and copies ran while one was open for 27% -> 14% of each run, Pallas kernels for 7% -> 29%
where the time goes in v2:
time: 578 us; the launch traced here: 574 us
  Pallas kernels  194 us (34%)
  waiting for transfers between devices  185 us (32%)
  starting transfers between devices  84.2 us (15%)
  other arithmetic  72.5 us (13%)
  local copies, waits for them, and re-layouts  35.6 us (6%)
    ppermute x75, waiting for transfers between devices, swap(): return lax.ppermute(values, axis, [(0, 1), (1, 0)])  185 us
    ppermute x75, starting transfers between devices, swap(): return lax.ppermute(values, axis, [(0, 1), (1, 0)])  80 us
    pallas_call x2, Pallas kernels, mlp(): pl.pallas_call(functools.partial(mlp_kernel, block=block, first=first), g...  46.7 us
    pallas_call x2, Pallas kernels, attend_back(): pl.pallas_call(functools.partial(attend_back_kernel, first=first), grid=(...  45.6 us
    pallas_call x8, Pallas kernels, copied(): pl.pallas_call(functools.partial(copy_kernel, plan), in_specs=[pl.BlockSp...  30.9 us
    pallas_call x1, Pallas kernels, attend(): pl.pallas_call(attend_kernel, grid=(heads,), in_specs=[pl.BlockSpec(h_one...  26.6 us
    add x22, other arithmetic, step(): values = self.kept + got  18.9 us
    unnamed x141, local copies, waits for them, and re-layouts  14.2 us
  transfers between devices with their start and end apart: 79, of which 28 were waited for; matrix products, arithmetic and copies ran while one was open for 14% of the time, Pallas kernels for 29%

profile of v2, /device:TPU:0, one launch (start us, length us, event | category | flops | bytes accessed | tf_op | source)
XLA Modules:
  0.0 574.1 jit_solution(748979733181279195)
XLA Ops:
  24.0 25.4 %collective-permute-done.3.refs_3_ = bf16[128,2048]{1,0:T(8,128)(2,1)S(1)} collective-permute-done((bf16[128,2048]{1,0:T(8,128)(2,1)}, bf16[128,2048]{1,0:T(8,128)(2,1)S(1)}, u32[]{:S(2)}, u32[]{:S(2)}) %collective-permute-start.3) | collective-permute-done | bytes 524320 | tf_op jit(solution)/shard_map/ppermute | solution.py:1040
  49.4 11.0 %collective-permute-done.5.refs_2_ = bf16[128,1024]{1,0:T(8,128)(2,1)S(1)} collective-permute-done((bf16[128,1024]{1,0:T(8,128)(2,1)}, bf16[128,1024]{1,0:T(8,128)(2,1)S(1)}, u32[]{:S(2)}, u32[]{:S(2)}) %collective-permute-start.5) | collective-permute-done | bytes 262176 | tf_op jit(solution)/shard_map/ppermute | solution.py:1040
  64.3 6.3 %collective-permute-done.7.refs_4_ = bf16[128,2048]{1,0:T(8,128)(2,1)S(1)} collective-permute-done((bf16[128,2048]{1,0:T(8,128)(2,1)}, bf16[128,2048]{1,0:T(8,128)(2,1)S(1)}, u32[]{:S(2)}, u32[]{:S(2)}) %collective-permute-start.7) | collective-permute-done | bytes 524320 | tf_op jit(solution)/shard_map/ppermute | solution.py:1040
  73.7 8.8 %collective-permute-done.4.refs_2_ = bf16[128,3072]{1,0:T(8,128)(2,1)S(1)} collective-permute-done((bf16[128,3072]{1,0:T(8,128)(2,1)}, bf16[128,3072]{1,0:T(8,128)(2,1)S(1)}, u32[]{:S(2)}, u32[]{:S(2)}) %collective-permute-start.4) | collective-permute-done | bytes 786464 | tf_op jit(solution)/shard_map/ppermute | solution.py:1040
  105.7 26.6 %attend.1 = (bf16[1024,1024]{1,0:T(8,128)(2,1)}, bf16[1024,1024]{1,0:T(8,128)(2,1)}, bf16[1024,512]{1,0:T(8,128)(2,1)}, f32[4,2,1024]{2,1,0:T(2,128)}, f32[1024,2048]{1,0:T(8,128)}) custom-call(bf16[1024,1024]{1,0:T(8,128)(2,1)} %norm_first.1.h_ref, bf16[1024,2048]{1,0:T(8,128)(2,1)} %join_columns.2.w_ref, f32[1024,128]{1,0:T(8,128)} %get-tuple-element.345.cos_ref, ...), custom_call_target="tpu_custom_call" | custom-call | tf_op jit(solution)/shard_map/attend/pallas_call | solution.py:525
  132.3 7.2 %out_forward.1 = (bf16[512,1024]{1,0:T(8,128)(2,1)}, f32[512,1024]{1,0:T(8,128)}) custom-call(s32[4]{0:T(128)} %pad_add_fusion.place_ref, bf16[1024,1024]{1,0:T(8,128)(2,1)} %get-tuple-element.147.o_ref, bf16[1024,1024]{1,0:T(8,128)(2,1)} %join_rows.2.w_ref), custom_call_target="tpu_custom_call" | custom-call | tf_op jit(solution)/shard_map/out_forward/pallas_call | solution.py:596
  147.1 9.3 %collective-permute-done.17.refs_2_ = bf16[192,1024]{1,0:T(8,128)(2,1)} collective-permute-done((bf16[192,1024]{1,0:T(8,128)(2,1)S(1)}, bf16[192,1024]{1,0:T(8,128)(2,1)}, u32[]{:S(2)}, u32[]{:S(2)}) %collective-permute-start.17) | collective-permute-done | bytes 393248 | tf_op jit(solution)/shard_map/ppermute | solution.py:1040
  166.1 10.0 %collective-permute-done.23.refs_4_ = bf16[192,1024]{1,0:T(8,128)(2,1)S(1)} collective-permute-done((bf16[192,1024]{1,0:T(8,128)(2,1)}, bf16[192,1024]{1,0:T(8,128)(2,1)S(1)}, u32[]{:S(2)}, u32[]{:S(2)}) %collective-permute-start.23) | collective-permute-done | bytes 393248 | tf_op jit(solution)/shard_map/ppermute | solution.py:1040
  181.0 6.4 %join_columns.3.gu_ref = bf16[1024,3072]{1,0:T(8,128)(2,1)} custom-call(s32[4]{0:T(128)} %pad_add_fusion.place_ref, bf16[512,3072]{1,0:T(8,128)(2,1)} %refs_0_.14, bf16[512,3072]{1,0:T(8,128)(2,1)} %refs_1_.7, bf16[128,3072]{1,0:T(8,128)(2,1)} %copy-done.30, bf16[128,3072]{1,0:T(8,128)(2,1)} %collective-permute-done.11.refs_3_, ...), custom_call_target="tpu_custom_call" | custom-call | tf_op jit(solution)/shard_map/join_columns/pallas_call | solution.py:937
  189.4 22.2 %mlp.2 = (bf16[1024,1536]{1,0:T(8,128)(2,1)}, bf16[768,1024]{1,0:T(8,128)(2,1)}, f32[1024,1024]{1,0:T(8,128)}, f32[1024,1024]{1,0:T(8,128)}) custom-call(s32[4]{0:T(128)} %pad_add_fusion.place_ref, bf16[512,1024]{1,0:T(8,128)(2,1)} %get-tuple-element.155.hm_ref, bf16[512,1024]{1,0:T(8,128)(2,1)} %copy-done.4, bf16[512,1024]{1,0:T(8,128)(2,1)} %copy-done.1, ...), custom_call_target="tpu_custom_call" | custom-call | tf_op jit(solution)/shard_map/mlp/pallas_call | solution.py:887
  215.6 24.5 %mlp.3 = (bf16[1024,1536]{1,0:T(8,128)(2,1)}, bf16[768,1024]{1,0:T(8,128)(2,1)}, f32[1024,1024]{1,0:T(8,128)}, f32[1024,1024]{1,0:T(8,128)}) custom-call(s32[4]{0:T(128)} %pad_add_fusion.place_ref, bf16[512,1024]{1,0:T(8,128)(2,1)} %get-tuple-element.155.hm_ref, bf16[512,1024]{1,0:T(8,128)(2,1)} %copy-done.4, bf16[512,1024]{1,0:T(8,128)(2,1)} %copy-done.1, ...), custom_call_target="tpu_custom_call" | custom-call | tf_op jit(solution)/shard_map/mlp/pallas_call | solution.py:887
  248.0 5.8 %norm_gradient.2 = (f32[512,1024]{1,0:T(8,128)}, bf16[512,1024]{1,0:T(8,128)(2,1)}, f32[1,1024]{1,0:T(1,128)}) custom-call(s32[4]{0:T(128)} %pad_add_fusion.place_ref, f32[512,1024]{1,0:T(8,128)} %get-tuple-element.153.values_ref, f32[1024,1024]{1,0:T(8,128)} %get-tuple-element.167.whole_ref.part_ref, bf16[512,1024]{1,0:T(8,128)(2,1)} %copy-done.29, ...), custom_call_target="tpu_custom_call" | custom-call | tf_op jit(solution)/shard_map/norm_gradient/pallas_call | solution.py:749
  262.4 8.6 %out_back.1 = (bf16[1024,1024]{1,0:T(8,128)(2,1)}, bf16[1024,1024]{1,0:T(8,128)(2,1)}) custom-call(s32[4]{0:T(128)} %pad_add_fusion.place_ref, bf16[512,1024]{1,0:T(8,128)(2,1)} %get-tuple-element.169.mine_ref, bf16[512,1024]{1,0:T(8,128)(2,1)} %collective-permute-done.28.other_ref, bf16[1024,1024]{1,0:T(8,128)(2,1)} %get-tuple-element.147.o_ref, ...), custom_call_target="tpu_custom_call" | custom-call | tf_op jit(solution)/shard_map/out_back/pallas_call | solution.py:794
  271.0 6.1 %collective-permute-done.24 = bf16[256,1536]{1,0:T(8,128)(2,1)} collective-permute-done((bf16[256,1536]{1,0:T(8,128)(2,1)}, bf16[256,1536]{1,0:T(8,128)(2,1)}, u32[]{:S(2)}, u32[]{:S(2)}) %collective-permute-start.24) | collective-permute-done | bytes 786464 | tf_op jit(solution)/shard_map/ppermute | solution.py:1040
  285.1 22.3 %attend_back.2 = (bf16[1024,1024]{1,0:T(8,128)(2,1)}, f32[2,8,128]{2,1,0:T(8,128)}, f32[1024,1024]{1,0:T(8,128)}) custom-call(bf16[1024,1024]{1,0:T(8,128)(2,1)} %get-tuple-element.162.q_ref, bf16[1024,512]{1,0:T(8,128)(2,1)} %get-tuple-element.163.k_ref, f32[1024,2048]{1,0:T(8,128)} %get-tuple-element.164.qkv_ref, ...), custom_call_target="tpu_custom_call" | custom-call | tf_op jit(solution)/shard_map/attend_back/pallas_call | solution.py:665
  324.1 23.3 %attend_back.3 = (bf16[1024,1024]{1,0:T(8,128)(2,1)}, f32[2,8,128]{2,1,0:T(8,128)}, f32[1024,1024]{1,0:T(8,128)}) custom-call(bf16[1024,1024]{1,0:T(8,128)(2,1)} %get-tuple-element.162.q_ref, bf16[1024,512]{1,0:T(8,128)(2,1)} %get-tuple-element.163.k_ref, f32[1024,2048]{1,0:T(8,128)} %get-tuple-element.164.qkv_ref, ...), custom_call_target="tpu_custom_call" | custom-call | tf_op jit(solution)/shard_map/attend_back/pallas_call | solution.py:665
  366.3 10.2 %collective-permute-done.43 = bf16[512,1024]{1,0:T(8,128)(2,1)S(1)} collective-permute-done((bf16[512,1024]{1,0:T(8,128)(2,1)}, bf16[512,1024]{1,0:T(8,128)(2,1)S(1)}, u32[]{:S(2)}, u32[]{:S(2)}) %collective-permute-start.43) | collective-permute-done | bytes 1048608 | tf_op jit(solution)/shard_map/ppermute | solution.py:1040
  387.8 15.0 %collective-permute-done.40 = f32[16,128]{1,0:T(8,128)S(1)} collective-permute-done((f32[16,128]{1,0:T(8,128)S(1)}, f32[16,128]{1,0:T(8,128)S(1)}, u32[]{:S(2)}, u32[]{:S(2)}) %collective-permute-start.40) | collective-permute-done | bytes 8224 | tf_op jit(solution)/shard_map/ppermute | solution.py:1040
  417.2 9.7 %collective-permute-done.51 = bf16[128,1024]{1,0:T(8,128)(2,1)S(1)} collective-permute-done((bf16[128,1024]{1,0:T(8,128)(2,1)S(1)}, bf16[128,1024]{1,0:T(8,128)(2,1)S(1)}, u32[]{:S(2)}, u32[]{:S(2)}) %collective-permute-start.51) | collective-permute-done | bytes 262176 | tf_op jit(solution)/shard_map/ppermute | solution.py:1040
  432.9 14.0 %collective-permute-done.49 = bf16[256,1024]{1,0:T(8,128)(2,1)S(1)} collective-permute-done((bf16[256,1024]{1,0:T(8,128)(2,1)S(1)}, bf16[256,1024]{1,0:T(8,128)(2,1)S(1)}, u32[]{:S(2)}, u32[]{:S(2)}) %collective-permute-start.49) | collective-permute-done | bytes 524320 | tf_op jit(solution)/shard_map/ppermute | solution.py:1040
  473.9 8.9 %collective-permute-done.54 = bf16[128,1024]{1,0:T(8,128)(2,1)S(1)} collective-permute-done((bf16[128,1024]{1,0:T(8,128)(2,1)}, bf16[128,1024]{1,0:T(8,128)(2,1)S(1)}, u32[]{:S(2)}, u32[]{:S(2)}) %collective-permute-start.54) | collective-permute-done | bytes 262176 | tf_op jit(solution)/shard_map/ppermute | solution.py:1040
  487.6 10.9 %collective-permute-done.64 = bf16[128,1024]{1,0:T(8,128)(2,1)S(1)} collective-permute-done((bf16[128,1024]{1,0:T(8,128)(2,1)S(1)}, bf16[128,1024]{1,0:T(8,128)(2,1)S(1)}, u32[]{:S(2)}, u32[]{:S(2)}) %collective-permute-start.64) | collective-permute-done | bytes 262176 | tf_op jit(solution)/shard_map/ppermute | solution.py:1040
  527.1 5.5 collective-permute-done.68
  549.5 6.7 %collective-permute-done.76 = bf16[256,1024]{1,0:T(8,128)(2,1)} collective-permute-done((bf16[256,1024]{1,0:T(8,128)(2,1)S(1)}, bf16[256,1024]{1,0:T(8,128)(2,1)}, u32[]{:S(2)}, u32[]{:S(2)}) %collective-permute-start.76) | collective-permute-done | bytes 524320 | tf_op jit(solution)/shard_map/ppermute | solution.py:1040
  (404 shorter events, 267.1 us)
Async XLA Ops:
  11.8 50.3 %collective-permute-start.1 = (bf16[512,1024]{1,0:T(8,128)(2,1)S(1)}, bf16[512,1024]{1,0:T(8,128)(2,1)S(1)}, u32[]{:S(2)}, u32[]{:S(2)}) collective-permute-start(bf16[512,1024]{1,0:T(8,128)(2,1)S(1)} %copy-done.25), channel_id=1, source_target_pairs={{1,2},{2,1},{5,6},{6,5},{9,10},{10,9},{13,14},{14,13},{17,18},{18,... | collective-permute-start | bytes 3145736 | tf_op jit(solution)/shard_map/ppermute | solution.py:1109
  12.6 36.8 %collective-permute-start.3 = (bf16[128,2048]{1,0:T(8,128)(2,1)}, bf16[128,2048]{1,0:T(8,128)(2,1)S(1)}, u32[]{:S(2)}, u32[]{:S(2)}) collective-permute-start(bf16[128,2048]{1,0:T(8,128)(2,1)} %get-tuple-element.131), channel_id=1, source_target_pairs={{0,1},{1,0},{2,3},{3,2},{4,5},{5,4},{6,7},{7,6},{8,9},{9,8},{10,11... | collective-permute-start | bytes 1572872 | tf_op jit(solution)/shard_map/ppermute | solution.py:1040
  18.4 42.1 %collective-permute-start.14 = (bf16[128,1024]{1,0:T(8,128)(2,1)}, bf16[128,1024]{1,0:T(8,128)(2,1)S(1)}, u32[]{:S(2)}, u32[]{:S(2)}) collective-permute-start(bf16[128,1024]{1,0:T(8,128)(2,1)} %get-tuple-element.134), channel_id=1, source_target_pairs={{0,1},{1,0},{2,3},{3,2},{4,5},{5,4},{6,7},{7,6},{8,9},{9,8},{10,11... | collective-permute-start | bytes 786440 | tf_op jit(solution)/shard_map/ppermute | solution.py:1040
  18.5 41.9 %collective-permute-start.5 = (bf16[128,1024]{1,0:T(8,128)(2,1)}, bf16[128,1024]{1,0:T(8,128)(2,1)S(1)}, u32[]{:S(2)}, u32[]{:S(2)}) collective-permute-start(bf16[128,1024]{1,0:T(8,128)(2,1)} %get-tuple-element.138), channel_id=1, source_target_pairs={{0,1},{1,0},{2,3},{3,2},{4,5},{5,4},{6,7},{7,6},{8,9},{9,8},{10,11... | collective-permute-start | bytes 786440 | tf_op jit(solution)/shard_map/ppermute | solution.py:1040
  20.5 50.1 %collective-permute-start.7 = (bf16[128,2048]{1,0:T(8,128)(2,1)}, bf16[128,2048]{1,0:T(8,128)(2,1)S(1)}, u32[]{:S(2)}, u32[]{:S(2)}) collective-permute-start(bf16[128,2048]{1,0:T(8,128)(2,1)} %get-tuple-element.140), channel_id=1, source_target_pairs={{0,1},{1,0},{2,3},{3,2},{4,5},{5,4},{6,7},{7,6},{8,9},{9,8},{10,11... | collective-permute-start | bytes 1572872 | tf_op jit(solution)/shard_map/ppermute | solution.py:1040
  49.4 33.0 %collective-permute-start.4 = (bf16[128,3072]{1,0:T(8,128)(2,1)}, bf16[128,3072]{1,0:T(8,128)(2,1)S(1)}, u32[]{:S(2)}, u32[]{:S(2)}) collective-permute-start(bf16[128,3072]{1,0:T(8,128)(2,1)} %get-tuple-element.137), channel_id=1, source_target_pairs={{0,1},{1,0},{2,3},{3,2},{4,5},{5,4},{6,7},{7,6},{8,9},{9,8},{10,11... | collective-permute-start | bytes 2359304 | tf_op jit(solution)/shard_map/ppermute | solution.py:1040
  72.3 60.0 %collective-permute-start.11 = (bf16[128,3072]{1,0:T(8,128)(2,1)}, bf16[128,3072]{1,0:T(8,128)(2,1)}, u32[]{:S(2)}, u32[]{:S(2)}) collective-permute-start(bf16[128,3072]{1,0:T(8,128)(2,1)} %get-tuple-element.143), channel_id=1, source_target_pairs={{0,1},{1,0},{2,3},{3,2},{4,5},{5,4},{6,7},{7,6},{8,9},{9,8},{10,11... | collective-permute-start | bytes 2359304 | tf_op jit(solution)/shard_map/ppermute | solution.py:1040
  82.4 49.8 %collective-permute-start.13 = (bf16[128,3072]{1,0:T(8,128)(2,1)S(1)}, bf16[128,3072]{1,0:T(8,128)(2,1)S(1)}, u32[]{:S(2)}, u32[]{:S(2)}) collective-permute-start(bf16[128,3072]{1,0:T(8,128)(2,1)S(1)} %collective-permute-done.4.refs_2_), channel_id=1, source_target_pairs={{0,4},{4,0},{1,5},{5,1},{2,6},{6,2},{3,7},{7,3},{8,12},{12,8},{9,1... | collective-permute-start | bytes 2359304 | tf_op jit(solution)/shard_map/ppermute | solution.py:1040
  88.0 44.3 %collective-permute-start.12 = (bf16[192,1024]{1,0:T(8,128)(2,1)}, bf16[192,1024]{1,0:T(8,128)(2,1)S(1)}, u32[]{:S(2)}, u32[]{:S(2)}) collective-permute-start(bf16[192,1024]{1,0:T(8,128)(2,1)} %get-tuple-element.146), channel_id=1, source_target_pairs={{0,1},{1,0},{2,3},{3,2},{4,5},{5,4},{6,7},{7,6},{8,9},{9,8},{10,11... | collective-permute-start | bytes 1179656 | tf_op jit(solution)/shard_map/ppermute | solution.py:1040
  88.1 58.9 %collective-permute-start.21 = (bf16[512,1024]{1,0:T(8,128)(2,1)S(1)}, bf16[512,1024]{1,0:T(8,128)(2,1)S(1)}, u32[]{:S(2)}, u32[]{:S(2)}) collective-permute-start(bf16[512,1024]{1,0:T(8,128)(2,1)S(1)} %copy-done.26), channel_id=1, source_target_pairs={{1,2},{2,1},{5,6},{6,5},{9,10},{10,9},{13,14},{14,13},{17,18},{18,... | collective-permute-start | bytes 3145736 | tf_op jit(solution)/shard_map/ppermute | solution.py:1109
  147.1 40.3 %collective-permute-start.22 = (bf16[512,1024]{1,0:T(8,128)(2,1)S(1)}, bf16[512,1024]{1,0:T(8,128)(2,1)S(1)}, u32[]{:S(2)}, u32[]{:S(2)}) collective-permute-start(bf16[512,1024]{1,0:T(8,128)(2,1)S(1)} %broadcast_select_fusion.17.dm_ref.base_ref), channel_id=1, source_target_pairs={{0,2},{2,0},{1,3},{3,1},{4,6},{6,4},{5,7},{7,5},{8,10},{10,8},{9,1... | collective-permute-start | bytes 3145736 | tf_op jit(solution)/shard_map/ppermute | solution.py:1040
  214.9 39.0 %collective-permute-start.27 = (bf16[512,1536]{1,0:T(8,128)(2,1)S(1)}, bf16[512,1536]{1,0:T(8,128)(2,1)S(1)}, u32[]{:S(2)}, u32[]{:S(2)}) collective-permute-start(bf16[512,1536]{1,0:T(8,128)(2,1)S(1)} %slice.294), channel_id=1, source_target_pairs={{0,1},{1,0},{2,3},{3,2},{4,5},{5,4},{6,7},{7,6},{8,9},{9,8},{10,11... | collective-permute-start | bytes 4718600 | tf_op jit(solution)/shard_map/ppermute | solution.py:1040
  257.8 50.3 %collective-permute-start.31 = (bf16[256,1536]{1,0:T(8,128)(2,1)}, bf16[256,1536]{1,0:T(8,128)(2,1)}, u32[]{:S(2)}, u32[]{:S(2)}) collective-permute-start(bf16[256,1536]{1,0:T(8,128)(2,1)} %get-tuple-element.255), channel_id=1, source_target_pairs={{0,1},{1,0},{2,3},{3,2},{4,5},{5,4},{6,7},{7,6},{8,9},{9,8},{10,11... | collective-permute-start | bytes 2359304 | tf_op jit(solution)/shard_map/ppermute | solution.py:1040
  261.0 49.8 %collective-permute-start.32 = (bf16[384,1024]{1,0:T(8,128)(2,1)}, bf16[384,1024]{1,0:T(8,128)(2,1)}, u32[]{:S(2)}, u32[]{:S(2)}) collective-permute-start(bf16[384,1024]{1,0:T(8,128)(2,1)} %dynamic-slice_add_fusion), channel_id=1, source_target_pairs={{0,1},{1,0},{2,3},{3,2},{4,5},{5,4},{6,7},{7,6},{8,9},{9,8},{10,11... | collective-permute-start | bytes 2359304 | tf_op jit(solution)/shard_map/ppermute | solution.py:1040
  278.3 32.5 %collective-permute-start.30 = (bf16[256,1536]{1,0:T(8,128)(2,1)}, bf16[256,1536]{1,0:T(8,128)(2,1)S(1)}, u32[]{:S(2)}, u32[]{:S(2)}) collective-permute-start(bf16[256,1536]{1,0:T(8,128)(2,1)} %get-tuple-element.285), channel_id=1, source_target_pairs={{0,4},{4,0},{1,5},{5,1},{2,6},{6,2},{3,7},{7,3},{8,12},{12,8},{9,1... | collective-permute-start | bytes 2359304 | tf_op jit(solution)/shard_map/ppermute | solution.py:1040
  283.7 66.9 %collective-permute-start.36 = (bf16[512,1024]{1,0:T(8,128)(2,1)}, bf16[512,1024]{1,0:T(8,128)(2,1)S(1)}, u32[]{:S(2)}, u32[]{:S(2)}) collective-permute-start(bf16[512,1024]{1,0:T(8,128)(2,1)} %slice.297), channel_id=1, source_target_pairs={{0,1},{1,0},{2,3},{3,2},{4,5},{5,4},{6,7},{7,6},{8,9},{9,8},{10,11... | collective-permute-start | bytes 3145736 | tf_op jit(solution)/shard_map/ppermute | solution.py:1040
  317.5 34.8 %collective-permute-start.34 = (bf16[256,1536]{1,0:T(8,128)(2,1)}, bf16[256,1536]{1,0:T(8,128)(2,1)}, u32[]{:S(2)}, u32[]{:S(2)}) collective-permute-start(bf16[256,1536]{1,0:T(8,128)(2,1)} %get-tuple-element.283), channel_id=1, source_target_pairs={{0,4},{4,0},{1,5},{5,1},{2,6},{6,2},{3,7},{7,3},{8,12},{12,8},{9,1... | collective-permute-start | bytes 2359304 | tf_op jit(solution)/shard_map/ppermute | solution.py:1040
  322.1 30.2 %collective-permute-start.33 = (bf16[128,1536]{1,0:T(8,128)(2,1)}, bf16[128,1536]{1,0:T(8,128)(2,1)S(1)}, u32[]{:S(2)}, u32[]{:S(2)}) collective-permute-start(bf16[128,1536]{1,0:T(8,128)(2,1)} %get-tuple-element.313), channel_id=1, source_target_pairs={{0,8},{8,0},{1,9},{9,1},{2,10},{10,2},{3,11},{11,3},{4,12},{12,4},... | collective-permute-start | bytes 1179656 | tf_op jit(solution)/shard_map/ppermute | solution.py:1040
  354.1 30.2 %collective-permute-start.42 = (bf16[128,1536]{1,0:T(8,128)(2,1)S(1)}, bf16[128,1536]{1,0:T(8,128)(2,1)S(1)}, u32[]{:S(2)}, u32[]{:S(2)}) collective-permute-start(bf16[128,1536]{1,0:T(8,128)(2,1)S(1)} %add.158), channel_id=1, source_target_pairs={{0,16},{16,0},{1,17},{17,1},{2,18},{18,2},{3,19},{19,3},{4,20},{20... | collective-permute-start | bytes 1179656 | tf_op jit(solution)/shard_map/ppermute | solution.py:1040
  377.7 34.0 %collective-permute-start.46 = (bf16[512,1024]{1,0:T(8,128)(2,1)}, bf16[512,1024]{1,0:T(8,128)(2,1)}, u32[]{:S(2)}, u32[]{:S(2)}) collective-permute-start(bf16[512,1024]{1,0:T(8,128)(2,1)} %get-tuple-element.257), channel_id=1, source_target_pairs={{0,1},{1,0},{2,3},{3,2},{4,5},{5,4},{6,7},{7,6},{8,9},{9,8},{10,11... | collective-permute-start | bytes 3145736 | tf_op jit(solution)/shard_map/ppermute | solution.py:1040
  415.1 41.1 %collective-permute-start.57 = (bf16[256,1536]{1,0:T(8,128)(2,1)S(1)}, bf16[256,1536]{1,0:T(8,128)(2,1)}, u32[]{:S(2)}, u32[]{:S(2)}) collective-permute-start(bf16[256,1536]{1,0:T(8,128)(2,1)S(1)} %maximum_select_fusion.8), channel_id=1, source_target_pairs={{0,4},{4,0},{1,5},{5,1},{2,6},{6,2},{3,7},{7,3},{8,12},{12,8},{9,1... | collective-permute-start | bytes 2359304 | tf_op jit(solution)/shard_map/ppermute | solution.py:1040
  415.7 31.2 %collective-permute-start.49 = (bf16[256,1024]{1,0:T(8,128)(2,1)S(1)}, bf16[256,1024]{1,0:T(8,128)(2,1)S(1)}, u32[]{:S(2)}, u32[]{:S(2)}) collective-permute-start(bf16[256,1024]{1,0:T(8,128)(2,1)S(1)} %get-tuple-element.303), channel_id=1, source_target_pairs={{0,4},{4,0},{1,5},{5,1},{2,6},{6,2},{3,7},{7,3},{8,12},{12,8},{9,1... | collective-permute-start | bytes 1572872 | tf_op jit(solution)/shard_map/ppermute | solution.py:1040
  427.9 35.6 %collective-permute-start.59 = (bf16[384,1024]{1,0:T(8,128)(2,1)S(1)}, bf16[384,1024]{1,0:T(8,128)(2,1)}, u32[]{:S(2)}, u32[]{:S(2)}) collective-permute-start(bf16[384,1024]{1,0:T(8,128)(2,1)S(1)} %maximum_select_fusion.9), channel_id=1, source_target_pairs={{0,4},{4,0},{1,5},{5,1},{2,6},{6,2},{3,7},{7,3},{8,12},{12,8},{9,1... | collective-permute-start | bytes 2359304 | tf_op jit(solution)/shard_map/ppermute | solution.py:1040
  523.5 34.5 %collective-permute-start.67 = (bf16[512,1024]{1,0:T(8,128)(2,1)}, bf16[512,1024]{1,0:T(8,128)(2,1)}, u32[]{:S(2)}, u32[]{:S(2)}) collective-permute-start(bf16[512,1024]{1,0:T(8,128)(2,1)} %get-tuple-element.235), channel_id=1, source_target_pairs={{1,2},{2,1},{5,6},{6,5},{9,10},{10,9},{13,14},{14,13},{17,18},{18,... | collective-permute-start | bytes 3145736 | tf_op jit(solution)/shard_map/ppermute | solution.py:1109
  (113 other events, 1345.5 us)

commit v3 on v2

--- a/solution.py
+++ b/solution.py
@@ -389,9 +389,42 @@
     return values * scale * gain
 
 
+def place_rows(place_ref, own, parts, w_ref):
+    at = 0
+    rows = own[0].shape[0]
+    for source in own:
+        w_ref[:rows, at : at + source.shape[1]] = source[...]
+        at += source.shape[1]
+    near_y, near_z, far_y, far_z = parts
+    row_y, row_z, count = shared_rows(place_ref, rows, rows)
+    other_y = pl.multiple_of(rows + (1 - place_ref[2]) * count, count)
+    other_z = pl.multiple_of(rows + 2 * count + (1 - place_ref[3]) * count, count)
+    for part, row in ((near_y, row_y), (near_z, row_z), (far_y, other_y), (far_z, other_z)):
+        w_ref[pl.ds(row, count), :] = part[...]
+
+
 def attend_kernel(
-    h_ref, w_ref, cos_ref, sin_ref, qg_ref, kg_ref, o_ref, q_ref, k_ref, lse_ref, qkv_ref
+    place_ref,
+    h_ref,
+    wq_ref,
+    wk_ref,
+    wv_ref,
+    near_y,
+    near_z,
+    far_y,
+    far_z,
+    cos_ref,
+    sin_ref,
+    qg_ref,
+    kg_ref,
+    o_ref,
+    q_ref,
+    k_ref,
+    lse_ref,
+    qkv_ref,
+    w_ref,
 ):
+    place_rows(place_ref, (wq_ref, wk_ref, wv_ref), (near_y, near_z, far_y, far_z), w_ref)
     qkv_ref[...] = jnp.dot(h_ref[...], w_ref[...], preferred_element_type=jnp.float32)
     span, head_dim = cos_ref.shape
     group = o_ref.shape[1] // head_dim
@@ -441,7 +474,9 @@
     first,
 ):
     dh_in = None if first else rest[0]
-    grad_ref, gain_ref, dh_ref, own_ref, key_acc, value_acc, ht_ref = rest[0 if first else 1 :]
+    kept_ref, sent_ref, gain_ref, dh_ref, own_ref, key_acc, value_acc, ht_ref = rest[
+        0 if first else 1 :
+    ]
     span, head_dim = cos_ref.shape
     group = q_ref.shape[1] // head_dim
 
@@ -507,50 +542,70 @@
         [query_gain, key_gain, jnp.zeros((gain_ref.shape[1] - 2, head_dim), jnp.float32)], axis=0
     )
     grads = own_ref[...]
-    grad_ref[...] = jnp.dot(ht_ref[...], grads, preferred_element_type=jnp.float32).astype(
-        jnp.bfloat16
-    )
+    product = jnp.dot(ht_ref[...], grads, preferred_element_type=jnp.float32)
+    product = product.astype(jnp.bfloat16)
+    kept_ref[...] = product[: kept_ref.shape[0]]
+    sent_ref[...] = product[kept_ref.shape[0] :]
     dh_ref[...] += times_t(grads, w_ref[...])
 
 
-def attend(h_one, qkv_w, cosine, sine, q_gain, k_gain, group):
+def attend(place, h_one, weights, parts, cosine, sine, q_gain, k_gain, group, head_groups):
     span, head_dim = cosine.shape
+    width = h_one.shape[1]
     step = (group + 2) * head_dim
-    heads = qkv_w.shape[1] // step
-    wide = pl.BlockSpec((span, step), lambda head: (0, head))
-    q_spec = pl.BlockSpec((span, group * head_dim), lambda head: (0, head))
-    k_spec = pl.BlockSpec((span, head_dim), lambda head: (0, head))
-    table = pl.BlockSpec((span, head_dim), lambda head: (0, 0))
-    gain = pl.BlockSpec((1, head_dim), lambda head: (0, 0))
+    heads = parts[0].shape[1] // step
+    part_rows = parts[0].shape[0]
+
+    def own(head, place):
+        block = jnp.where(head < head_groups, place[0], 1 - place[0])
+        return (0, (2 * block + place[1]) * head_groups + head % head_groups)
+
+    def column(head, place):
+        return (0, head)
+
+    def fixed(head, place):
+        return (0, 0)
+
+    rows = weights[0].shape[0]
+    wide = pl.BlockSpec((span, step), column)
+    q_spec = pl.BlockSpec((span, group * head_dim), column)
+    k_spec = pl.BlockSpec((span, head_dim), column)
+    table = pl.BlockSpec((span, head_dim), fixed)
+    gain = pl.BlockSpec((1, head_dim), fixed)
     return pl.pallas_call(
         attend_kernel,
-        grid=(heads,),
-        in_specs=[
-            pl.BlockSpec(h_one.shape, lambda head: (0, 0)),
-            pl.BlockSpec((qkv_w.shape[0], step), lambda head: (0, head)),
-            table,
-            table,
-            gain,
-            gain,
-        ],
-        out_specs=[
-            q_spec,
-            q_spec,
-            k_spec,
-            pl.BlockSpec((1, group, span), lambda h: (h, 0, 0)),
-            wide,
-        ],
+        grid_spec=pltpu.PrefetchScalarGridSpec(
+            num_scalar_prefetch=1,
+            grid=(heads,),
+            in_specs=[
+                pl.BlockSpec(h_one.shape, fixed),
+                pl.BlockSpec((rows, group * head_dim), own),
+                pl.BlockSpec((rows, head_dim), own),
+                pl.BlockSpec((rows, head_dim), own),
+            ]
+            + [pl.BlockSpec((part_rows, step), column)] * 4
+            + [table, table, gain, gain],
+            out_specs=[
+                q_spec,
+                q_spec,
+                k_spec,
+                pl.BlockSpec((1, group, span), lambda h, place: (h, 0, 0)),
+                wide,
+                pl.BlockSpec((width, step), column),
+            ],
+        ),
         out_shape=[
             jax.ShapeDtypeStruct((span, heads * group * head_dim), jnp.bfloat16),
             jax.ShapeDtypeStruct((span, heads * group * head_dim), jnp.bfloat16),
             jax.ShapeDtypeStruct((span, heads * head_dim), jnp.bfloat16),
             jax.ShapeDtypeStruct((heads, group, span), jnp.float32),
             jax.ShapeDtypeStruct((span, heads * step), jnp.float32),
+            jax.ShapeDtypeStruct((width, heads * step), jnp.bfloat16),
         ],
         compiler_params=pltpu.CompilerParams(vmem_limit_bytes=VMEM_BYTES),
         cost_estimate=NO_COST,
         name="attend",
-    )(h_one, qkv_w, cosine, sine, q_gain, k_gain)
+    )(place, h_one, *weights, *parts, cosine, sine, q_gain, k_gain)
 
 
 def norm_first_kernel(place_ref, mine_ref, other_ref, gain_ref, h_ref):
@@ -680,12 +735,14 @@
         ]
         + ([] if first else [whole]),
         out_specs=[
-            pl.BlockSpec((width, step), lambda head: (0, head)),
+            pl.BlockSpec((width // 2, step), lambda head: (0, head)),
+            pl.BlockSpec((width // 2, step), lambda head: (0, head)),
             pl.BlockSpec((1, 8, head_dim), lambda h: (h, 0, 0)),
             pl.BlockSpec((span, width), lambda head: (0, 0)),
         ],
         out_shape=[
-            jax.ShapeDtypeStruct((width, heads * step), jnp.bfloat16),
+            jax.ShapeDtypeStruct((width // 2, heads * step), jnp.bfloat16),
+            jax.ShapeDtypeStruct((width // 2, heads * step), jnp.bfloat16),
             jax.ShapeDtypeStruct((heads, 8, head_dim), jnp.float32),
             jax.ShapeDtypeStruct((span, width), jnp.float32),
         ],
@@ -773,13 +830,23 @@
     whole_ref[pl.ds(pl.multiple_of((1 - c) * half, half), half), :] = other_ref[...]
 
 
-def out_back_kernel(place_ref, mine_ref, other_ref, o_ref, w_ref, do_ref, grad_ref, dr_ref):
+def out_back_kernel(
+    place_ref, mine_ref, other_ref, o_ref, w_ref, do_ref, far_ref, near_ref, dr_ref
+):
     @pl.when(pl.program_id(0) == 0)
     def _():
         whole_rows(place_ref, mine_ref, other_ref, dr_ref)
 
     do_ref[...] = times_t(dr_ref[...], w_ref[...]).astype(jnp.bfloat16)
-    grad_ref[...] = inner_rows(o_ref[...], dr_ref[...]).astype(jnp.bfloat16)
+    product = inner_rows(o_ref[...], dr_ref[...]).astype(jnp.bfloat16)
+
+    @pl.when(pl.program_id(0) < 2)
+    def _():
+        far_ref[...] = product
+
+    @pl.when(pl.program_id(0) >= 2)
+    def _():
+        near_ref[...] = product
 
 
 def out_back(place, mine, other, out_low, out_w):
@@ -803,11 +870,13 @@
         ],
         out_specs=[
             pl.BlockSpec((2 * half, block), lambda i: (0, at(i))),
-            pl.BlockSpec((block, width), lambda i: (at(i), 0)),
+            pl.BlockSpec((block, width), lambda i: (jnp.minimum(i, 1), 0)),
+            pl.BlockSpec((block, width), lambda i: (jnp.maximum(i - 2, 0), 0)),
         ],
         out_shape=[
             jax.ShapeDtypeStruct((2 * half, count), jnp.bfloat16),
-            jax.ShapeDtypeStruct((count, width), jnp.bfloat16),
+            jax.ShapeDtypeStruct((count // 2, width), jnp.bfloat16),
+            jax.ShapeDtypeStruct((count // 2, width), jnp.bfloat16),
         ],
         scratch_shapes=[pltpu.VMEM((2 * half, width), jnp.bfloat16)],
         compiler_params=pltpu.CompilerParams(vmem_limit_bytes=VMEM_BYTES),
@@ -841,9 +910,14 @@
     )(place, values)
 
 
-def mlp_kernel(place_ref, hm_ref, ho_ref, dm_ref, do_ref, gu_ref, down_ref, *rest, block, first):
+def mlp_kernel(place_ref, hm_ref, ho_ref, dm_ref, do_ref, *rest, block, first):
+    gate_ref, up_ref = rest[:2]
+    unit_parts, rest = rest[2:6], rest[6:]
+    down_refs, rest = (rest[:4], rest[4:]) if first else (rest[:1], rest[1:])
     res_in, dh_in = (None, None) if first else rest[:2]
-    ggu_ref, gdown_ref, res_ref, dh_ref, h_ref, dy_ref, ht_ref = rest[0 if first else 2 :]
+    kept_ref, sent_ref, gdown_ref, res_ref, dh_ref, h_ref, dy_ref, ht_ref, gu_ref, down_all = rest[
+        0 if first else 2 :
+    ]
 
     @pl.when(pl.program_id(0) == 0)
     def _():
@@ -852,7 +926,24 @@
         ht_ref[...] = h_ref[...].T
         res_ref[...] = jnp.zeros_like(res_ref) if first else res_in[...]
         dh_ref[...] = jnp.zeros_like(dh_ref) if first else dh_in[...]
-
+        if first:
+            near_y, near_z, far_y, far_z = down_refs
+            row_y, row_z, count = shared_rows(place_ref, 0, down_all.shape[0])
+            other_y = pl.multiple_of((1 - place_ref[2]) * count, count)
+            other_z = pl.multiple_of(2 * count + (1 - place_ref[3]) * count, count)
+            for part, row in (
+                (near_y, row_y),
+                (near_z, row_z),
+                (far_y, other_y),
+                (far_z, other_z),
+            ):
+                down_all[pl.ds(row, count), :] = part[...]
+
+    place_rows(place_ref, (gate_ref, up_ref), unit_parts, gu_ref)
+    if first:
+        down_ref = down_all.at[pl.ds(pl.multiple_of(pl.program_id(0) * block, block), block), :]
+    else:
+        down_ref = down_refs[0]
     weights = gu_ref[...]
     both = jnp.dot(h_ref[...], weights, preferred_element_type=jnp.float32)
     gate, up_val = both[:, :block], both[:, block:]
@@ -866,58 +957,165 @@
     grads = jnp.concatenate([grad_gate, (grad_hidden * active).astype(jnp.bfloat16)], axis=1)
     res_ref[...] += jnp.dot(hidden, down_ref[...], preferred_element_type=jnp.float32)
     dh_ref[...] += times_t(grads, weights)
-    ggu_ref[...] = jnp.dot(ht_ref[...], grads, preferred_element_type=jnp.float32).astype(
-        jnp.bfloat16
-    )
+    product = jnp.dot(ht_ref[...], grads, preferred_element_type=jnp.float32)
+    product = product.astype(jnp.bfloat16)
+    kept_ref[...] = product[: kept_ref.shape[0]]
+    sent_ref[...] = product[kept_ref.shape[0] :]
     gdown_ref[...] = inner_rows(hidden, dy_ref[...]).astype(jnp.bfloat16)
 
 
-def mlp(place, h_halves, dy_halves, gu_w, down_w, part, sums=None):
+def mlp(place, h_halves, dy_halves, unit_weights, unit_parts, w_down, down_parts, part, sums=None):
     half, width = h_halves[0].shape
     span = 2 * half
-    units = down_w.shape[0] // 2
+    units = w_down.shape[0] // 2
     block = math.gcd(UNIT_BLOCK, units)
     steps = units // block
-    base = part * steps
+    rows, part_rows = unit_weights[0].shape[0], unit_parts[0].shape[0]
+    first = sums is None
     once = pl.Buffered(1)
-    piece = pl.BlockSpec((half, width), lambda j: (0, 0), pipeline_mode=once)
-    whole = pl.BlockSpec((span, width), lambda j: (0, 0), pipeline_mode=once)
-    total = pl.BlockSpec((span, width), lambda j: (0, 0))
-    first = sums is None
+
+    def fixed(j, place):
+        return (0, 0)
+
+    def own(j, place):
+        index = 1 - place[0] if part else place[0]
+        return (0, (2 * index + place[1]) * steps + j)
+
+    piece = pl.BlockSpec((half, width), fixed, pipeline_mode=once)
+    whole = pl.BlockSpec((span, width), fixed, pipeline_mode=once)
+    total = pl.BlockSpec((span, width), fixed)
+    columns = pl.BlockSpec((width // 2, 2 * block), lambda j, place: (0, j))
+    if first:
+        down_specs = [pl.BlockSpec(down_parts[0].shape, fixed, pipeline_mode=once)] * 4
+        downs = down_parts
+    else:
+        down_specs = [pl.BlockSpec((block, width), lambda j, place: (place[1] * steps + j, 0))]
+        downs = [w_down]
     return pl.pallas_call(
         functools.partial(mlp_kernel, block=block, first=first),
-        grid=(steps,),
-        in_specs=[
-            pl.BlockSpec(memory_space=pltpu.SMEM),
-            piece,
-            piece,
-            piece,
-            piece,
-            pl.BlockSpec((width, 2 * block), lambda j: (0, base + j)),
-            pl.BlockSpec((block, width), lambda j: (base + j, 0)),
-        ]
-        + ([] if first else [whole, whole]),
-        out_specs=[
-            pl.BlockSpec((width, 2 * block), lambda j: (0, j)),
-            pl.BlockSpec((block, width), lambda j: (j, 0)),
-            total,
-            total,
-        ],
+        grid_spec=pltpu.PrefetchScalarGridSpec(
+            num_scalar_prefetch=1,
+            grid=(steps,),
+            in_specs=[
+                piece,
+                piece,
+                piece,
+                piece,
+                pl.BlockSpec((rows, block), own),
+                pl.BlockSpec((rows, block), own),
+            ]
+            + [pl.BlockSpec((part_rows, 2 * block), lambda j, place: (0, part * steps + j))] * 4
+            + down_specs
+            + ([] if first else [whole, whole]),
+            out_specs=[
+                columns,
+                columns,
+                pl.BlockSpec((block, width), lambda j, place: (j, 0)),
+                total,
+                total,
+            ],
+            scratch_shapes=[
+                pltpu.VMEM((span, width), jnp.bfloat16),
+                pltpu.VMEM((span, width), jnp.bfloat16),
+                pltpu.VMEM((width, span), jnp.bfloat16),
+                pltpu.VMEM((width, 2 * block), jnp.bfloat16),
+                pltpu.VMEM((units if first else 16, width), jnp.bfloat16),
+            ],
+        ),
         out_shape=[
-            jax.ShapeDtypeStruct((width, 2 * units), jnp.bfloat16),
+            jax.ShapeDtypeStruct((width // 2, 2 * units), jnp.bfloat16),
+            jax.ShapeDtypeStruct((width // 2, 2 * units), jnp.bfloat16),
             jax.ShapeDtypeStruct((units, width), jnp.bfloat16),
             jax.ShapeDtypeStruct((span, width), jnp.float32),
             jax.ShapeDtypeStruct((span, width), jnp.float32),
         ],
-        scratch_shapes=[
-            pltpu.VMEM((span, width), jnp.bfloat16),
-            pltpu.VMEM((span, width), jnp.bfloat16),
-            pltpu.VMEM((width, span), jnp.bfloat16),
-        ],
         compiler_params=pltpu.CompilerParams(vmem_limit_bytes=VMEM_BYTES),
         cost_estimate=NO_COST,
         name="mlp",
-    )(place, *h_halves, *dy_halves, gu_w, down_w, *(sums or ()))
+    )(place, *h_halves, *dy_halves, *unit_weights, *unit_parts, *downs, *(sums or ()))
+
+
+def split_add_kernel(place_ref, kept_ref, got_ref, keep_ref, send_ref):
+    total = kept_ref[...] + got_ref[...]
+
+    @pl.when(pl.program_id(0) == 0)
+    def _():
+        send_ref[...] = total
+
+    @pl.when(pl.program_id(0) == 1)
+    def _():
+        keep_ref[...] = total
+
+
+def split_add(place, axis, kept, got):
+    rows, width = kept.shape[0] // 2, kept.shape[1]
+    spec = pl.BlockSpec(
+        (rows, width), lambda i, place: (i * place[axis] + (1 - i) * (1 - place[axis]), 0)
+    )
+    fixed = pl.BlockSpec((rows, width), lambda i, place: (0, 0))
+    return pl.pallas_call(
+        split_add_kernel,
+        grid_spec=pltpu.PrefetchScalarGridSpec(
+            num_scalar_prefetch=1,
+            grid=(2,),
+            in_specs=[spec, spec],
+            out_specs=[fixed, fixed],
+        ),
+        out_shape=[jax.ShapeDtypeStruct((rows, width), kept.dtype)] * 2,
+        compiler_params=pltpu.CompilerParams(vmem_limit_bytes=VMEM_BYTES),
+        cost_estimate=NO_COST,
+        name="split_add",
+    )(place, kept, got)
+
+
+def add_kernel(left_ref, right_ref, total_ref):
+    total_ref[...] = left_ref[...] + right_ref[...]
+
+
+def plain_add(left, right):
+    rows, width = left.shape[0] // 2, left.shape[1]
+    spec = pl.BlockSpec((rows, width), lambda i: (i, 0))
+    return pl.pallas_call(
+        add_kernel,
+        grid=(2,),
+        in_specs=[spec, spec],
+        out_specs=spec,
+        out_shape=jax.ShapeDtypeStruct(left.shape, left.dtype),
+        compiler_params=pltpu.CompilerParams(vmem_limit_bytes=VMEM_BYTES),
+        cost_estimate=NO_COST,
+        name="plain_add",
+    )(left, right)
+
+
+def join_kernel(place_ref, mine_ref, other_ref, whole_ref):
+    @pl.when(pl.program_id(0) == 0)
+    def _():
+        whole_ref[...] = mine_ref[...].astype(whole_ref.dtype)
+
+    @pl.when(pl.program_id(0) == 1)
+    def _():
+        whole_ref[...] = other_ref[...].astype(whole_ref.dtype)
+
+
+def join(place, axis, mine, other, dtype):
+    rows, width = mine.shape
+    fixed = pl.BlockSpec((rows, width), lambda i, place: (0, 0))
+    return pl.pallas_call(
+        join_kernel,
+        grid_spec=pltpu.PrefetchScalarGridSpec(
+            num_scalar_prefetch=1,
+            grid=(2,),
+            in_specs=[fixed, fixed],
+            out_specs=pl.BlockSpec(
+                (rows, width),
+                lambda i, place: ((1 - i) * place[axis] + i * (1 - place[axis]), 0),
+            ),
+        ),
+        out_shape=jax.ShapeDtypeStruct((2 * rows, width), dtype),
+        compiler_params=pltpu.CompilerParams(vmem_limit_bytes=VMEM_BYTES),
+        cost_estimate=NO_COST,
+        name="join",
+    )(place, mine, other)
 
 
 def copy_kernel(plan, place_ref, *refs):
@@ -1010,19 +1208,6 @@
         (part, target.at[pl.ds(row, count)])
         for part, row in ((near_y, row_y), (near_z, row_z), (far_y, other_y), (far_z, other_z))
     ]
-
-
-def join_columns(place, weights, groups, parts):
-    def plan(place_ref, refs):
-        x, c = place_ref[0], place_ref[1]
-        sources, parts, target = refs[:-5], refs[-5:-1], refs[-1]
-        rows = sources[0].shape[0]
-        moves = column_moves(sources, target, groups, 2 * x + c, 2 * (1 - x) + c, 0, rows)
-        return moves + far_moves(place_ref, parts, target, rows)
-
-    shape = (2 * weights[0].shape[0], parts[0].shape[1])
-    count = 2 * groups * len(weights) + 4
-    return copied(plan, count, place, [*weights, *parts], [shape], "join_columns")[0]
 
 
 def join_rows(place, weight, parts):
@@ -1102,9 +1287,6 @@
     def flip(values):
         return jnp.where(x == 0, values, halves_swapped(values))
 
-    def both(values):
-        return ordered(c == 0, values, swap(values, "c"))
-
     def turn(values):
         return jnp.where(x == c, values, lax.ppermute(values, ("c", "x"), [(1, 2), (2, 1)]))
 
@@ -1124,15 +1306,9 @@
 
     head_sent = send_columns(first, head_weights, head_groups, "send_heads")
     head_near = near(head_sent)
-    own_tokens = turn(hold(tokens, head_sent[0]))
     out_sent = send_rows(hold(place, head_sent[0]), w_out, "send_out")
-    out_near = near(out_sent)
     unit_sent = send_columns(hold(place, out_sent[0]), unit_weights, unit_groups, "send_units")
     down_sent = send_rows(hold(place, unit_sent[0]), w_down, "send_down")
-    unit_near = near([hold(piece, head_near[0]) for piece in unit_sent])
-    down_near = near([hold(piece, head_near[1]) for piece in down_sent])
-    own_cot = turn(hold(cotangent, head_near[1]))
-
     gains, far_gains = small[: 2 * (part + q_part)], small_got[: 2 * (part + q_part)]
     own_places, far_places = small[2 * (part + q_part) :], small_got[2 * (part + q_part) :]
     places = ordered(x == 0, own_places, far_places)
@@ -1147,45 +1323,63 @@
     cosine = jnp.concatenate([cosine[:, 0], cosine[:, 0]], axis=-1)
     sine = jnp.concatenate([-sine[:, 0], sine[:, 0]], axis=-1)
 
-    h_one = norm_first(place, own_tokens, swap(own_tokens, "c"), gain_one)
-    qkv_w = join_columns(place, head_weights, head_groups, relayed(head_near))
+    tokens, *head_near = lax.optimization_barrier((tokens, *head_near, down_sent[0], cosine, sine))[:3]
+    own_tokens = turn(tokens)
+    out_near = near([hold(piece, head_near[0]) for piece in out_sent])
+    unit_near = near([hold(piece, head_near[0]) for piece in unit_sent])
+    down_near = near([hold(piece, head_near[0]) for piece in down_sent])
+    own_cot = turn(hold(cotangent, head_near[0]))
+
+    head_parts = relayed(head_near)
+    h_one = norm_first(place, own_tokens, swap(hold(own_tokens, *out_near, *head_parts[2:]), "c"), gain_one)
     out_parts = relayed(out_near)
+    out_low, query_low, key_low, lse, qkv, qkv_w = attend(
+        place,
+        h_one,
+        head_weights,
+        head_parts,
+        cosine,
+        sine,
+        q_gain,
+        k_gain,
+        group,
+        head_groups,
+    )
+    out_low = hold(out_low, *unit_near, *down_near, *out_parts[2:])
     out_w = join_rows(place, w_out, out_parts)
     unit_parts = relayed(unit_near)
-    out_low, query_low, key_low, lse, qkv = attend(
-        hold(h_one, unit_near[0], out_parts[3]), qkv_w, cosine, sine, q_gain, k_gain, group
-    )
-    out_low = hold(out_low, unit_near[1], down_near[0], unit_parts[2])
+    out_sent, out_kept = out_forward(place, out_low, out_w)
+    out_got = swap(out_sent, "c")
     down_parts = relayed(down_near)
-    out_sent, out_kept = out_forward(place, out_low, out_w)
-    out_got = hold(swap(out_sent, "c"), down_near[1])
     resid, h_mine = norm_second(place, own_tokens, out_kept, out_got, gain_two)
-    h_mine = hold(h_mine, unit_parts[3], down_parts[2])
+    h_mine = hold(h_mine, *unit_parts[2:], *down_parts[2:])
     h_halves = (h_mine, swap(h_mine, "c"))
     cot_halves = (own_cot, swap(own_cot, "c"))
-    gu_w = join_columns(place, unit_weights, unit_groups, unit_parts)
-    down_w = join_rows(place, w_down, down_parts)
 
     def rs(values, axis):
         index, count = lax.axis_index(axis), values.shape[0] // 2
         return rows_at(values, index, count), swap(rows_at(values, 1 - index, count), axis)
 
-    grad_gu_far, grad_down_far, res_part, dh_part = mlp(
-        place, h_halves, cot_halves, gu_w, down_w, 1
+    far_kept, far_sent, grad_down_far, res_part, dh_part = mlp(
+        place, h_halves, cot_halves, unit_weights, unit_parts, w_down, down_parts, 1
     )
     down_far_kept, down_far_got = rs(grad_down_far, "y")
-    far_got = swap(grad_gu_far[part:], "x")
-    grad_gu_near, grad_down_near, res_part, dh_part = mlp(
-        place, h_halves, cot_halves, gu_w, down_w, 0, (res_part, dh_part)
-    )
+    far_got = swap(far_sent, "x")
+    near_kept, near_sent, grad_down_near, res_part, dh_part = mlp(
+        place,
+        h_halves,
+        cot_halves,
+        unit_weights,
+        unit_parts,
+        w_down,
+        down_parts,
+        0,
+        (res_part, dh_part),
+    )
+    near_got = swap(near_sent, "x")
     dh_part = hold(dh_part, down_far_got)
     down_got = swap(down_far_kept + down_far_got, "x")
     down_near_kept, down_near_got = rs(grad_down_near, "y")
-    near_rows = part // 2
-    near_gots = [
-        swap(grad_gu_near[part : part + near_rows], "x"),
-        swap(grad_gu_near[part + near_rows :], "x"),
-    ]
 
     class Piece:
         def __init__(self, kept, got, path):
@@ -1194,8 +1388,7 @@
         def step(self, *others):
             got = hold(self.got, *others)
             if self.back and self.back[0] == "c":
-                self.kept, self.got = ordered(c == 0, self.kept, got), None
-                return self.kept
+                return join(place, 1, self.kept, got, f32)
             if self.back:
                 values = ordered(lax.axis_index(self.back[0]) == 0, self.kept, got)
                 self.back = self.back[1:]
@@ -1217,25 +1410,20 @@
             self.kept, self.got = values, swap(values, self.back[0])
             return self.kept
 
-    near_piece = Piece(grad_gu_near[:part], far_got, ("y", "za", "zb"))
+    near_piece = Piece(near_kept, far_got, ("y", "za", "zb"))
 
     dh_got = swap(other_half(place, dh_part), "c")
     grad_resid, resid_low, gain_two_sum = norm_gradient(
         place, resid, dh_part, dh_got, own_cot, gain_two, True
     )
     resid_low = hold(resid_low, far_got)
-    grad_att, grad_out = out_back(place, resid_low, swap(resid_low, "c"), out_low, out_w)
-    grad_att, down_near_got, near_got = lax.optimization_barrier(
-        (grad_att, down_near_got, near_gots[0])
-    )
-    near_got = jnp.concatenate([near_got, near_gots[1]], axis=0)
-    far_piece = Piece(grad_gu_far[:part], near_got, ("y", "za", "zb"))
+    grad_att, grad_out_far, grad_out_near = out_back(
+        place, resid_low, swap(resid_low, "c"), out_low, out_w
+    )
+    out_got = swap(grad_out_far, "x")
     mark = near_piece.step(grad_att)
-    out_rows = grad_out.shape[0] // 2
-    out_piece = Piece(grad_out[:out_rows], swap(grad_out[out_rows:], "x"), ("y", "za", "zb"))
-    down_near_total = down_near_kept + hold(down_near_got, mark)
-    down_piece = Piece(down_near_total, down_got, ("za", "zb"))
-    down_piece.turned = ["y"]
+    far_piece = Piece(far_kept, near_got, ("za", "y", "zb"))
+    out_piece = Piece(grad_out_near, out_got, ("za", "y", "zb"))
 
     def back_of(index, dh, *others):
         grads = hold(grad_att, *others)
@@ -1255,31 +1443,28 @@
             dh,
         )
 
-    grad_far, head_gains_far, dh_part = back_of(1, None, down_near_total)
-    grad_far, near_piece.got, near_gots[1], down_piece.got = lax.optimization_barrier(
-        (grad_far, near_piece.got, near_gots[1], down_piece.got)
-    )
-    far_piece.got = jnp.concatenate([near_gots[0], near_gots[1]], axis=0)
-    qkv_far_got = swap(grad_far[part:], "x")
-    mark = far_piece.step(grad_far)
+    far_rows, far_rows_sent, head_gains_far, dh_part = back_of(1, None, mark)
+    qkv_far_got = swap(far_rows_sent, "x")
+    far_rows, near_piece.got, far_piece.got, down_near_got = lax.optimization_barrier(
+        (far_rows, near_piece.got, far_piece.got, down_near_got)
+    )
+    down_piece = Piece(down_near_kept + down_near_got, down_got, ("za", "zb"))
+    down_piece.turned = ["y"]
+    mark = far_piece.step(far_rows)
     mark = near_piece.step(mark)
-    mark = down_piece.step(mark)
-    grad_near, head_gains_near, dh_part = back_of(0, dh_part, mark)
-    grad_near, near_piece.got, far_piece.got, down_piece.got, out_piece.got = (
-        lax.optimization_barrier(
-            (grad_near, near_piece.got, far_piece.got, down_piece.got, out_piece.got)
-        )
-    )
-    qkv_near_got = swap(grad_near[part:], "x")
-    qkv_near_piece = Piece(grad_near[:part], qkv_far_got, ("y", "za", "zb"))
-    qkv_far_piece = Piece(grad_far[:part], qkv_near_got, ("y", "za", "zb"))
+    near_rows, near_rows_sent, head_gains_near, dh_part = back_of(0, dh_part, mark)
+    qkv_near_got = swap(near_rows_sent, "x")
+    dh_part, near_piece.got, far_piece.got, down_piece.got = lax.optimization_barrier(
+        (dh_part, near_piece.got, far_piece.got, down_piece.got)
+    )
+    qkv_near_piece = Piece(near_rows, qkv_far_got, ("y", "za", "zb"))
+    qkv_far_piece = Piece(far_rows, qkv_near_got, ("y", "za", "zb"))
 
     dh_sent = other_half(place, dh_part)
     dh_got = swap(dh_sent, "c")
-    mark = near_piece.step(dh_sent)
-    mark = down_piece.step(mark)
+    mark = down_piece.step(dh_sent)
     mark = far_piece.step(mark)
-    mark = out_piece.step(mark)
+    mark = near_piece.step(mark)
     input_sum, gain_one_sum = norm_gradient(
         place, own_tokens, dh_part, hold(dh_got, mark), grad_resid, gain_one, False
     )
@@ -1296,7 +1481,7 @@
         return jnp.concatenate([flat, jnp.zeros((pad,), f32)]).reshape(-1, head_dim)
 
     def rows_result(piece):
-        return piece.step(mark).astype(f32)
+        return piece.step(mark)
 
     def columns_result(near, far, widths, groups):
         others = [hold(piece.got, mark) for piece in (near, far)]
@@ -1332,45 +1517,49 @@
 
     unit_block = w_gate.shape[1] // 4 // unit_groups
     mark = input_sum
+    mark = down_piece.step(mark)
+    mark = out_piece.step(mark)
+    mark = far_piece.step(mark)
     mark = qkv_near_piece.step(mark)
     mark = near_piece.step(mark)
     mark = out_piece.step(mark)
     mark = gain_step("y", mark)
+    input_turned = turn(hold(input_sum, mark))
+    mark = down_piece.step(mark)
+    mark = qkv_near_piece.step(mark)
+    mark = qkv_far_piece.step(mark)
+    mark = far_piece.step(mark)
+    mark = out_piece.step(mark)
+    mark = near_piece.step(mark)
+    mark = gain_step("za", mark)
+    mark = qkv_far_piece.step(mark)
+    mark = qkv_near_piece.step(mark)
     mark = down_piece.step(mark)
     mark = far_piece.step(mark)
+    mark = out_piece.step(mark)
+    mark = grad_input = hold(input_turned, mark).astype(f32)
+    mark = gain_step("zb", mark)
+    mark = qkv_far_piece.step(mark)
     mark = qkv_near_piece.step(mark)
+    mark = near_piece.step(mark)
+    mark = far_piece.step(mark)
+    mark = gain_step("c", mark)
+    result_turned = turn(result_start(mark))
     mark = qkv_far_piece.step(mark)
-    mark = gain_step("za", mark)
-    mark = near_piece.step(mark)
+    mark = qkv_near_piece.step(mark)
+    mark = down_piece.step(mark)
+    grad_gate_w, grad_up_w = columns_result(
+        near_piece, far_piece, [unit_block, unit_block], unit_groups
+    )
+    mark = hold(grad_up_w, grad_gate_w)
     mark = out_piece.step(mark)
-    grad_input = turn(hold(input_sum, mark)).astype(f32)
-    mark = down_piece.step(mark)
     mark = qkv_far_piece.step(mark)
-    mark = gain_step("zb", mark)
-    mark = far_piece.step(mark)
-    mark = near_piece.step(mark)
-    mark = qkv_near_piece.step(mark)
-    mark = gain_step("c", mark)
-    mark = out_piece.step(mark)
-    mark = down_piece.step(mark)
     mark = grad_down_w = rows_result(down_piece)
+    mark = result = hold(result_turned, mark)
     mark = gain_step(None, mark)
-    mark = qkv_far_piece.step(mark)
-    mark = far_piece.step(mark)
     mark = qkv_near_piece.step(mark)
     mark = out_piece.step(mark)
-    mark = far_piece.step(mark)
-    result = turn(result_start(mark))
-    grad_gate_w, grad_up_w = columns_result(
-        near_piece, far_piece, [unit_block, unit_block], unit_groups
-    )
-    mark = grad_up_w
-    mark = qkv_far_piece.step(mark)
-    mark = out_piece.step(mark)
-    mark = qkv_near_piece.step(mark)
     mark = grad_out_w = rows_result(out_piece)
-    mark = qkv_far_piece.step(mark)
-    mark = qkv_near_piece.step(mark)
     mark = qkv_far_piece.step(mark)
     grad_query_w, grad_key_w, grad_value_w = columns_result(
         qkv_near_piece, qkv_far_piece, [group * head_dim, head_dim, head_dim], head_groups

time: 578 us -> 543 us (0.939)
  waiting for transfers between devices: 185 us -> 153 us
    ppermute x75 -> x74, waiting for transfers between devices: 185 us -> 153 us  [swap(): return lax.ppermute(values, axis, [(0, 1), (1, 0)])]
    pallas_call x8 -> x5, Pallas kernels: 30.9 us -> 15.4 us  [copied(): pl.pallas_call(functools.partial(copy_kernel, plan), in_specs=[pl.BlockSp...]
    pallas_call x1 -> x3, Pallas kernels: 26.6 us -> 38.5 us  [the longest x1 28.4 us: attend(): pl.pallas_call(attend_kernel, grid_spec=pltpu.PrefetchScalarGridSpec(num_...]
    convert_element_type x3 -> x1, other arithmetic: 10.4 us -> 1.57 us  [paired(): mark = grad_input = hold(input_turned, mark).astype(f32)]
    slice x4 -> x0, local copies, waits for them, and re-layouts: 7.6 us -> none  [the longest x1 2.55 us: paired(): qkv_far_got = swap(grad_far[part:], 'x')]
    select_n x14, other arithmetic: 10.7 us -> 17.6 us  [ordered(): jnp.where(first, jnp.concatenate([mine, other], axis=axis), jnp.concatena...]
    unnamed x141 -> x145, local copies, waits for them, and re-layouts: 14.2 us -> 17.7 us
    add x22 -> x23, other arithmetic: 18.9 us -> 16.6 us  [step(): values = self.kept + got]
  transfers between devices with their start and end apart: 79 -> 78, of which waited for: 28 -> 28; matrix products, arithmetic and copies ran while one was open for 14% -> 15% of each run, Pallas kernels for 29% -> 32%
where the time goes in v3:
time: 543 us; the launch traced here: 537 us
  Pallas kernels  196 us (36%)
  waiting for transfers between devices  153 us (28%)
  starting transfers between devices  84.6 us (16%)
  other arithmetic  68.2 us (13%)
  local copies, waits for them, and re-layouts  33.6 us (6%)
    ppermute x74, waiting for transfers between devices, swap(): return lax.ppermute(values, axis, [(0, 1), (1, 0)])  153 us
    ppermute x74, starting transfers between devices, swap(): return lax.ppermute(values, axis, [(0, 1), (1, 0)])  80.6 us
    pallas_call x2, Pallas kernels, mlp(): pl.pallas_call(functools.partial(mlp_kernel, block=block, first=first), g...  51.3 us
    pallas_call x2, Pallas kernels, attend_back(): pl.pallas_call(functools.partial(attend_back_kernel, first=first), grid=(...  45.7 us
    pallas_call x1, Pallas kernels, attend(): pl.pallas_call(attend_kernel, grid_spec=pltpu.PrefetchScalarGridSpec(num_...  28.4 us
    unnamed x145, local copies, waits for them, and re-layouts  17.7 us
    select_n x14, other arithmetic, ordered(): jnp.where(first, jnp.concatenate([mine, other], axis=axis), jnp.concatena...  17.6 us
    add x23, other arithmetic, step(): values = self.kept + got  16.6 us
  transfers between devices with their start and end apart: 78, of which 28 were waited for; matrix products, arithmetic and copies ran while one was open for 15% of the time, Pallas kernels for 32%

profile of v3, /device:TPU:0, one launch (start us, length us, event | category | flops | bytes accessed | tf_op | source)
XLA Modules:
  0.0 537.2 jit_solution(5520506353644969808)
XLA Ops:
  27.6 11.0 %collective-permute-done.2.near_z = bf16[128,2048]{1,0:T(8,128)(2,1)S(1)} collective-permute-done((bf16[128,2048]{1,0:T(8,128)(2,1)S(1)}, bf16[128,2048]{1,0:T(8,128)(2,1)S(1)}, u32[]{:S(2)}, u32[]{:S(2)}) %collective-permute-start.2) | collective-permute-done | bytes 524320 | tf_op jit(solution)/shard_map/ppermute | solution.py:1225
  45.7 17.8 %collective-permute-done.5.refs_1_ = bf16[128,1024]{1,0:T(8,128)(2,1)S(1)} collective-permute-done((bf16[128,1024]{1,0:T(8,128)(2,1)S(1)}, bf16[128,1024]{1,0:T(8,128)(2,1)S(1)}, u32[]{:S(2)}, u32[]{:S(2)}) %collective-permute-start.5) | collective-permute-done | bytes 262176 | tf_op jit(solution)/shard_map/ppermute | solution.py:1225
  71.6 5.0 collective-permute-done.14.refs_3_
  88.3 28.4 %attend.1 = (bf16[1024,1024]{1,0:T(8,128)(2,1)}, bf16[1024,1024]{1,0:T(8,128)(2,1)}, bf16[1024,512]{1,0:T(8,128)(2,1)}, f32[4,2,1024]{2,1,0:T(2,128)}, f32[1024,2048]{1,0:T(8,128)}, /*index=5*/bf16[1024,2048]{1,0:T(8,128)(2,1)}) custom-call(s32[4]{0:T(128)} %pad_add_fusion.place_ref, bf16[1024,1024]{1,0:T(8,128)(2,1)} %norm_first.1.h_ref, ...), custom_call_target="tpu_custom_call" | custom-call | tf_op jit(solution)/shard_map/attend/pallas_call | solution.py:575
  120.4 7.2 %out_forward.1 = (bf16[512,1024]{1,0:T(8,128)(2,1)}, f32[512,1024]{1,0:T(8,128)}) custom-call(s32[4]{0:T(128)} %pad_add_fusion.place_ref, bf16[1024,1024]{1,0:T(8,128)(2,1)} %get-tuple-element.159.o_ref, bf16[1024,1024]{1,0:T(8,128)(2,1)} %join_rows.1.w_ref), custom_call_target="tpu_custom_call" | custom-call | tf_op jit(solution)/shard_map/out_forward/pallas_call | solution.py:651
  138.1 18.0 %collective-permute-done.19.rest_8_ = bf16[192,1024]{1,0:T(8,128)(2,1)} collective-permute-done((bf16[192,1024]{1,0:T(8,128)(2,1)S(1)}, bf16[192,1024]{1,0:T(8,128)(2,1)}, u32[]{:S(2)}, u32[]{:S(2)}) %collective-permute-start.19) | collective-permute-done | bytes 393248 | tf_op jit(solution)/shard_map/ppermute | solution.py:1225
  163.0 24.7 %mlp.2 = (bf16[512,1536]{1,0:T(8,128)(2,1)}, bf16[512,1536]{1,0:T(8,128)(2,1)}, bf16[768,1024]{1,0:T(8,128)(2,1)}, f32[1024,1024]{1,0:T(8,128)}, f32[1024,1024]{1,0:T(8,128)}) custom-call(s32[4]{0:T(128)} %pad_add_fusion.place_ref, bf16[512,1024]{1,0:T(8,128)(2,1)} %get-tuple-element.164.hm_ref, bf16[512,1024]{1,0:T(8,128)(2,1)} %copy-done.8, ...), custom_call_target="tpu_custom_call" | custom-call | tf_op jit(solution)/shard_map/mlp/pallas_call | solution.py:994
  191.2 26.6 %mlp.3 = (bf16[512,1536]{1,0:T(8,128)(2,1)}, bf16[512,1536]{1,0:T(8,128)(2,1)}, bf16[768,1024]{1,0:T(8,128)(2,1)}, f32[1024,1024]{1,0:T(8,128)}, f32[1024,1024]{1,0:T(8,128)}) custom-call(s32[4]{0:T(128)} %pad_add_fusion.place_ref, bf16[512,1024]{1,0:T(8,128)(2,1)} %get-tuple-element.164.hm_ref, bf16[512,1024]{1,0:T(8,128)(2,1)} %copy-done.8, ...), custom_call_target="tpu_custom_call" | custom-call | tf_op jit(solution)/shard_map/mlp/pallas_call | solution.py:994
  225.7 5.8 %norm_gradient.2 = (f32[512,1024]{1,0:T(8,128)}, bf16[512,1024]{1,0:T(8,128)(2,1)}, f32[1,1024]{1,0:T(1,128)}) custom-call(s32[4]{0:T(128)} %pad_add_fusion.place_ref, f32[512,1024]{1,0:T(8,128)} %get-tuple-element.162.values_ref, f32[1024,1024]{1,0:T(8,128)} %get-tuple-element.174.whole_ref.part_ref, bf16[512,1024]{1,0:T(8,128)(2,1)} %copy-done.34, ...), custom_call_target="tpu_custom_call" | custom-call | tf_op jit(solution)/shard_map/norm_gradient/pallas_call | solution.py:806
  234.6 8.9 %out_back.1 = (bf16[1024,1024]{1,0:T(8,128)(2,1)}, bf16[512,1024]{1,0:T(8,128)(2,1)}, bf16[512,1024]{1,0:T(8,128)(2,1)}) custom-call(s32[4]{0:T(128)} %pad_add_fusion.place_ref, bf16[512,1024]{1,0:T(8,128)(2,1)} %get-tuple-element.177.mine_ref, bf16[512,1024]{1,0:T(8,128)(2,1)} %collective-permute-done.27.other_ref, ...), custom_call_target="tpu_custom_call" | custom-call | tf_op jit(solution)/shard_map/out_back/pallas_call | solution.py:861
  248.7 22.4 %attend_back.2 = (bf16[512,1024]{1,0:T(8,128)(2,1)}, bf16[512,1024]{1,0:T(8,128)(2,1)}, f32[2,8,128]{2,1,0:T(8,128)}, f32[1024,1024]{1,0:T(8,128)}) custom-call(bf16[1024,1024]{1,0:T(8,128)(2,1)} %get-tuple-element.169.q_ref, bf16[1024,512]{1,0:T(8,128)(2,1)} %get-tuple-element.170.k_ref, f32[1024,2048]{1,0:T(8,128)} %get-tuple-element.171.qkv_ref, ...), custom_call_target="tpu_custom_call" | custom-call | tf_op jit(solution)/shard_map/attend_back/pallas_call | solution.py:720
  279.2 23.3 %attend_back.3 = (bf16[512,1024]{1,0:T(8,128)(2,1)}, bf16[512,1024]{1,0:T(8,128)(2,1)}, f32[2,8,128]{2,1,0:T(8,128)}, f32[1024,1024]{1,0:T(8,128)}) custom-call(bf16[1024,1024]{1,0:T(8,128)(2,1)} %get-tuple-element.169.q_ref, bf16[1024,512]{1,0:T(8,128)(2,1)} %get-tuple-element.170.k_ref, f32[1024,2048]{1,0:T(8,128)} %get-tuple-element.171.qkv_ref, ...), custom_call_target="tpu_custom_call" | custom-call | tf_op jit(solution)/shard_map/attend_back/pallas_call | solution.py:720
  312.6 5.3 norm_gradient.3
  335.7 5.9 %collective-permute-done.39 = bf16[128,1536]{1,0:T(8,128)(2,1)S(1)} collective-permute-done((bf16[128,1536]{1,0:T(8,128)(2,1)S(1)}, bf16[128,1536]{1,0:T(8,128)(2,1)S(1)}, u32[]{:S(2)}, u32[]{:S(2)}) %collective-permute-start.39) | collective-permute-done | bytes 393248 | tf_op jit(solution)/shard_map/ppermute | solution.py:1225
  343.2 7.0 %collective-permute-done.38 = bf16[256,1024]{1,0:T(8,128)(2,1)S(1)} collective-permute-done((bf16[256,1024]{1,0:T(8,128)(2,1)}, bf16[256,1024]{1,0:T(8,128)(2,1)S(1)}, u32[]{:S(2)}, u32[]{:S(2)}) %collective-permute-start.38) | collective-permute-done | bytes 524320 | tf_op jit(solution)/shard_map/ppermute | solution.py:1225
  355.2 11.7 %collective-permute-done.48 = bf16[192,1024]{1,0:T(8,128)(2,1)S(1)} collective-permute-done((bf16[192,1024]{1,0:T(8,128)(2,1)S(1)}, bf16[192,1024]{1,0:T(8,128)(2,1)S(1)}, u32[]{:S(2)}, u32[]{:S(2)}) %collective-permute-start.48) | collective-permute-done | bytes 393248 | tf_op jit(solution)/shard_map/ppermute | solution.py:1225
  381.5 6.7 %collective-permute-done.42 = f32[16,128]{1,0:T(8,128)S(1)} collective-permute-done((f32[16,128]{1,0:T(8,128)S(1)}, f32[16,128]{1,0:T(8,128)S(1)}, u32[]{:S(2)}, u32[]{:S(2)}) %collective-permute-start.42) | collective-permute-done | bytes 8224 | tf_op jit(solution)/shard_map/ppermute | solution.py:1225
  392.4 7.7 %collective-permute-done.54 = bf16[128,1024]{1,0:T(8,128)(2,1)S(1)} collective-permute-done((bf16[128,1024]{1,0:T(8,128)(2,1)}, bf16[128,1024]{1,0:T(8,128)(2,1)S(1)}, u32[]{:S(2)}, u32[]{:S(2)}) %collective-permute-start.54) | collective-permute-done | bytes 262176 | tf_op jit(solution)/shard_map/ppermute | solution.py:1225
  410.6 13.9 %collective-permute-done.49 = f32[16,128]{1,0:T(8,128)S(1)} collective-permute-done((f32[16,128]{1,0:T(8,128)S(1)}, f32[16,128]{1,0:T(8,128)S(1)}, u32[]{:S(2)}, u32[]{:S(2)}) %collective-permute-start.49) | collective-permute-done | bytes 8224 | tf_op jit(solution)/shard_map/ppermute | solution.py:1225
  432.1 5.5 %collective-permute-start.56 = (f32[16,128]{1,0:T(8,128)S(1)}, f32[16,128]{1,0:T(8,128)S(1)}, u32[]{:S(2)}, u32[]{:S(2)}) collective-permute-start(f32[16,128]{1,0:T(8,128)S(1)} %add.189), channel_id=1, source_target_pairs={{0,16},{16,0},{1,17},{17,1},{2,18},{18,2},{3,19},{19,3},{4,20},{20... | collective-permute-start | bytes 24584 | tf_op jit(solution)/shard_map/ppermute | solution.py:1225
  445.3 12.5 %collective-permute-done.65 = bf16[128,1024]{1,0:T(8,128)(2,1)S(1)} collective-permute-done((bf16[128,1024]{1,0:T(8,128)(2,1)S(1)}, bf16[128,1024]{1,0:T(8,128)(2,1)S(1)}, u32[]{:S(2)}, u32[]{:S(2)}) %collective-permute-start.65) | collective-permute-done | bytes 262176 | tf_op jit(solution)/shard_map/ppermute | solution.py:1225
  490.5 5.5 %join.2 = f32[1536,1024]{1,0:T(8,128)} custom-call(s32[4]{0:T(128)} %pad_add_fusion.place_ref, bf16[768,1024]{1,0:T(8,128)(2,1)} %copy-done.4, bf16[768,1024]{1,0:T(8,128)(2,1)} %copy-done.18), custom_call_target="tpu_custom_call" | custom-call | tf_op jit(solution)/shard_map/join/pallas_call | solution.py:1103
  509.7 4.6 join.3
  518.5 5.4 %convert_element_type.50 = f32[512,3072]{1,0:T(8,128)} convert(bf16[512,3072]{1,0:T(8,128)(2,1)} %get-tuple-element.268) | non-fusion elementwise | flops 1572864 | bytes 9437184 | tf_op jit(solution)/shard_map/convert_element_type | solution.py:1500
  (398 shorter events, 244.4 us)
Async XLA Ops:
  66.4 54.0 %collective-permute-start.10 = (bf16[128,3072]{1,0:T(8,128)(2,1)}, bf16[128,3072]{1,0:T(8,128)(2,1)S(1)}, u32[]{:S(2)}, u32[]{:S(2)}) collective-permute-start(bf16[128,3072]{1,0:T(8,128)(2,1)} %get-tuple-element.153), channel_id=1, source_target_pairs={{0,1},{1,0},{2,3},{3,2},{4,5},{5,4},{6,7},{7,6},{8,9},{9,8},{10,11... | collective-permute-start | bytes 2359304 | tf_op jit(solution)/shard_map/ppermute | solution.py:1225
  67.6 52.7 %collective-permute-start.11 = (bf16[128,3072]{1,0:T(8,128)(2,1)}, bf16[128,3072]{1,0:T(8,128)(2,1)S(1)}, u32[]{:S(2)}, u32[]{:S(2)}) collective-permute-start(bf16[128,3072]{1,0:T(8,128)(2,1)} %get-tuple-element.155), channel_id=1, source_target_pairs={{0,1},{1,0},{2,3},{3,2},{4,5},{5,4},{6,7},{7,6},{8,9},{9,8},{10,11... | collective-permute-start | bytes 2359304 | tf_op jit(solution)/shard_map/ppermute | solution.py:1225
  76.6 40.1 %collective-permute-start.12 = (bf16[192,1024]{1,0:T(8,128)(2,1)}, bf16[192,1024]{1,0:T(8,128)(2,1)S(1)}, u32[]{:S(2)}, u32[]{:S(2)}) collective-permute-start(bf16[192,1024]{1,0:T(8,128)(2,1)} %get-tuple-element.156), channel_id=1, source_target_pairs={{0,1},{1,0},{2,3},{3,2},{4,5},{5,4},{6,7},{7,6},{8,9},{9,8},{10,11... | collective-permute-start | bytes 1179656 | tf_op jit(solution)/shard_map/ppermute | solution.py:1225
  77.8 42.5 %collective-permute-start.13 = (bf16[192,1024]{1,0:T(8,128)(2,1)}, bf16[192,1024]{1,0:T(8,128)(2,1)}, u32[]{:S(2)}, u32[]{:S(2)}) collective-permute-start(bf16[192,1024]{1,0:T(8,128)(2,1)} %get-tuple-element.158), channel_id=1, source_target_pairs={{0,1},{1,0},{2,3},{3,2},{4,5},{5,4},{6,7},{7,6},{8,9},{9,8},{10,11... | collective-permute-start | bytes 1179656 | tf_op jit(solution)/shard_map/ppermute | solution.py:1225
  78.7 52.6 %collective-permute-start.22 = (bf16[512,1024]{1,0:T(8,128)(2,1)S(1)}, bf16[512,1024]{1,0:T(8,128)(2,1)S(1)}, u32[]{:S(2)}, u32[]{:S(2)}) collective-permute-start(bf16[512,1024]{1,0:T(8,128)(2,1)S(1)} %copy-done.30), channel_id=1, source_target_pairs={{1,2},{2,1},{5,6},{6,5},{9,10},{10,9},{13,14},{14,13},{17,18},{18,... | collective-permute-start | bytes 3145736 | tf_op jit(solution)/shard_map/ppermute | solution.py:1291
  127.6 29.7 %collective-permute-start.17 = (bf16[128,3072]{1,0:T(8,128)(2,1)S(1)}, bf16[128,3072]{1,0:T(8,128)(2,1)S(1)}, u32[]{:S(2)}, u32[]{:S(2)}) collective-permute-start(bf16[128,3072]{1,0:T(8,128)(2,1)S(1)} %collective-permute-done.10.rest_2_), channel_id=1, source_target_pairs={{0,4},{4,0},{1,5},{5,1},{2,6},{6,2},{3,7},{7,3},{8,12},{12,8},{9,1... | collective-permute-start | bytes 2359304 | tf_op jit(solution)/shard_map/ppermute | solution.py:1225
  129.2 28.2 %collective-permute-start.18 = (bf16[128,3072]{1,0:T(8,128)(2,1)S(1)}, bf16[128,3072]{1,0:T(8,128)(2,1)S(1)}, u32[]{:S(2)}, u32[]{:S(2)}) collective-permute-start(bf16[128,3072]{1,0:T(8,128)(2,1)S(1)} %collective-permute-done.11.rest_3_), channel_id=1, source_target_pairs={{0,8},{8,0},{1,9},{9,1},{2,10},{10,2},{3,11},{11,3},{4,12},{12,4},... | collective-permute-start | bytes 2359304 | tf_op jit(solution)/shard_map/ppermute | solution.py:1225
  188.9 28.9 %collective-permute-start.24 = (bf16[384,1024]{1,0:T(8,128)(2,1)S(1)}, bf16[384,1024]{1,0:T(8,128)(2,1)S(1)}, u32[]{:S(2)}, u32[]{:S(2)}) collective-permute-start(bf16[384,1024]{1,0:T(8,128)(2,1)S(1)} %constant_dynamic-slice_fusion.23), channel_id=1, source_target_pairs={{0,4},{4,0},{1,5},{5,1},{2,6},{6,2},{3,7},{7,3},{8,12},{12,8},{9,1... | collective-permute-start | bytes 2359304 | tf_op jit(solution)/shard_map/ppermute | solution.py:1225
  189.5 42.0 %collective-permute-start.26 = (bf16[512,1536]{1,0:T(8,128)(2,1)}, bf16[512,1536]{1,0:T(8,128)(2,1)S(1)}, u32[]{:S(2)}, u32[]{:S(2)}) collective-permute-start(bf16[512,1536]{1,0:T(8,128)(2,1)} %get-tuple-element.176), channel_id=1, source_target_pairs={{0,1},{1,0},{2,3},{3,2},{4,5},{5,4},{6,7},{7,6},{8,9},{9,8},{10,11... | collective-permute-start | bytes 4718600 | tf_op jit(solution)/shard_map/ppermute | solution.py:1225
  231.7 39.4 %collective-permute-start.29 = (bf16[512,1536]{1,0:T(8,128)(2,1)}, bf16[512,1536]{1,0:T(8,128)(2,1)}, u32[]{:S(2)}, u32[]{:S(2)}) collective-permute-start(bf16[512,1536]{1,0:T(8,128)(2,1)} %get-tuple-element.185), channel_id=1, source_target_pairs={{0,1},{1,0},{2,3},{3,2},{4,5},{5,4},{6,7},{7,6},{8,9},{9,8},{10,11... | collective-permute-start | bytes 4718600 | tf_op jit(solution)/shard_map/ppermute | solution.py:1225
  233.0 38.1 %collective-permute-start.30 = (bf16[384,1024]{1,0:T(8,128)(2,1)}, bf16[384,1024]{1,0:T(8,128)(2,1)}, u32[]{:S(2)}, u32[]{:S(2)}) collective-permute-start(bf16[384,1024]{1,0:T(8,128)(2,1)} %constant_dynamic-slice_fusion.20), channel_id=1, source_target_pairs={{0,4},{4,0},{1,5},{5,1},{2,6},{6,2},{3,7},{7,3},{8,12},{12,8},{9,1... | collective-permute-start | bytes 2359304 | tf_op jit(solution)/shard_map/ppermute | solution.py:1225
  247.6 55.6 %collective-permute-start.33 = (bf16[384,1024]{1,0:T(8,128)(2,1)}, bf16[384,1024]{1,0:T(8,128)(2,1)}, u32[]{:S(2)}, u32[]{:S(2)}) collective-permute-start(bf16[384,1024]{1,0:T(8,128)(2,1)} %dynamic-slice_add_fusion), channel_id=1, source_target_pairs={{0,1},{1,0},{2,3},{3,2},{4,5},{5,4},{6,7},{7,6},{8,9},{9,8},{10,11... | collective-permute-start | bytes 2359304 | tf_op jit(solution)/shard_map/ppermute | solution.py:1225
  273.0 30.2 %collective-permute-start.32 = (bf16[256,1536]{1,0:T(8,128)(2,1)S(1)}, bf16[256,1536]{1,0:T(8,128)(2,1)S(1)}, u32[]{:S(2)}, u32[]{:S(2)}) collective-permute-start(bf16[256,1536]{1,0:T(8,128)(2,1)S(1)} %get-tuple-element.291), channel_id=1, source_target_pairs={{0,8},{8,0},{1,9},{9,1},{2,10},{10,2},{3,11},{11,3},{4,12},{12,4},... | collective-permute-start | bytes 2359304 | tf_op jit(solution)/shard_map/ppermute | solution.py:1225
  277.2 45.7 %collective-permute-start.36 = (bf16[512,1024]{1,0:T(8,128)(2,1)}, bf16[512,1024]{1,0:T(8,128)(2,1)}, u32[]{:S(2)}, u32[]{:S(2)}) collective-permute-start(bf16[512,1024]{1,0:T(8,128)(2,1)} %get-tuple-element.211), channel_id=1, source_target_pairs={{0,1},{1,0},{2,3},{3,2},{4,5},{5,4},{6,7},{7,6},{8,9},{9,8},{10,11... | collective-permute-start | bytes 3145736 | tf_op jit(solution)/shard_map/ppermute | solution.py:1225
  278.2 52.9 %collective-permute-start.40 = (bf16[512,1024]{1,0:T(8,128)(2,1)}, bf16[512,1024]{1,0:T(8,128)(2,1)}, u32[]{:S(2)}, u32[]{:S(2)}) collective-permute-start(bf16[512,1024]{1,0:T(8,128)(2,1)} %get-tuple-element.216), channel_id=1, source_target_pairs={{0,1},{1,0},{2,3},{3,2},{4,5},{5,4},{6,7},{7,6},{8,9},{9,8},{10,11... | collective-permute-start | bytes 3145736 | tf_op jit(solution)/shard_map/ppermute | solution.py:1225
  311.7 58.6 %collective-permute-start.46 = (bf16[512,1024]{1,0:T(8,128)(2,1)}, bf16[512,1024]{1,0:T(8,128)(2,1)}, u32[]{:S(2)}, u32[]{:S(2)}) collective-permute-start(bf16[512,1024]{1,0:T(8,128)(2,1)} %get-tuple-element.222), channel_id=1, source_target_pairs={{0,1},{1,0},{2,3},{3,2},{4,5},{5,4},{6,7},{7,6},{8,9},{9,8},{10,11... | collective-permute-start | bytes 3145736 | tf_op jit(solution)/shard_map/ppermute | solution.py:1225
  327.6 39.3 %collective-permute-start.48 = (bf16[192,1024]{1,0:T(8,128)(2,1)S(1)}, bf16[192,1024]{1,0:T(8,128)(2,1)S(1)}, u32[]{:S(2)}, u32[]{:S(2)}) collective-permute-start(bf16[192,1024]{1,0:T(8,128)(2,1)S(1)} %add.172), channel_id=1, source_target_pairs={{0,16},{16,0},{1,17},{17,1},{2,18},{18,2},{3,19},{19,3},{4,20},{20... | collective-permute-start | bytes 1179656 | tf_op jit(solution)/shard_map/ppermute | solution.py:1225
  333.6 33.5 %collective-permute-start.47 = (bf16[256,1024]{1,0:T(8,128)(2,1)}, bf16[256,1024]{1,0:T(8,128)(2,1)}, u32[]{:S(2)}, u32[]{:S(2)}) collective-permute-start(bf16[256,1024]{1,0:T(8,128)(2,1)} %get-tuple-element.313), channel_id=1, source_target_pairs={{0,4},{4,0},{1,5},{5,1},{2,6},{6,2},{3,7},{7,3},{8,12},{12,8},{9,1... | collective-permute-start | bytes 1572872 | tf_op jit(solution)/shard_map/ppermute | solution.py:1225
  341.6 33.2 %collective-permute-start.45 = (bf16[128,1536]{1,0:T(8,128)(2,1)S(1)}, bf16[128,1536]{1,0:T(8,128)(2,1)}, u32[]{:S(2)}, u32[]{:S(2)}) collective-permute-start(bf16[128,1536]{1,0:T(8,128)(2,1)S(1)} %add.175), channel_id=1, source_target_pairs={{0,16},{16,0},{1,17},{17,1},{2,18},{18,2},{3,19},{19,3},{4,20},{20... | collective-permute-start | bytes 1179656 | tf_op jit(solution)/shard_map/ppermute | solution.py:1225
  428.8 52.0 %collective-permute-start.76 = (bf16[512,1536]{1,0:T(8,128)(2,1)S(1)}, bf16[512,1536]{1,0:T(8,128)(2,1)}, u32[]{:S(2)}, u32[]{:S(2)}) collective-permute-start(bf16[512,1536]{1,0:T(8,128)(2,1)S(1)} %maximum_select_fusion), channel_id=1, source_target_pairs={{0,2},{2,0},{1,3},{3,1},{4,6},{6,4},{5,7},{7,5},{8,10},{10,8},{9,1... | collective-permute-start | bytes 4718600 | tf_op jit(solution)/shard_map/ppermute | solution.py:1225
  429.5 51.6 %collective-permute-start.77 = (bf16[512,1536]{1,0:T(8,128)(2,1)S(1)}, bf16[512,1536]{1,0:T(8,128)(2,1)}, u32[]{:S(2)}, u32[]{:S(2)}) collective-permute-start(bf16[512,1536]{1,0:T(8,128)(2,1)S(1)} %maximum_select_fusion.1), channel_id=1, source_target_pairs={{0,2},{2,0},{1,3},{3,1},{4,6},{6,4},{5,7},{7,5},{8,10},{10,8},{9,1... | collective-permute-start | bytes 4718600 | tf_op jit(solution)/shard_map/ppermute | solution.py:1225
  431.2 38.0 %collective-permute-start.63 = (bf16[384,1024]{1,0:T(8,128)(2,1)}, bf16[384,1024]{1,0:T(8,128)(2,1)}, u32[]{:S(2)}, u32[]{:S(2)}) collective-permute-start(bf16[384,1024]{1,0:T(8,128)(2,1)} %maximum_select_fusion.7), channel_id=1, source_target_pairs={{0,4},{4,0},{1,5},{5,1},{2,6},{6,2},{3,7},{7,3},{8,12},{12,8},{9,1... | collective-permute-start | bytes 2359304 | tf_op jit(solution)/shard_map/ppermute | solution.py:1225
  442.3 34.8 %collective-permute-start.61 = (bf16[512,1024]{1,0:T(8,128)(2,1)}, bf16[512,1024]{1,0:T(8,128)(2,1)}, u32[]{:S(2)}, u32[]{:S(2)}) collective-permute-start(bf16[512,1024]{1,0:T(8,128)(2,1)} %other_half.5), channel_id=1, source_target_pairs={{0,2},{2,0},{1,3},{3,1},{4,6},{6,4},{5,7},{7,5},{8,10},{10,8},{9,1... | collective-permute-start | bytes 3145736 | tf_op jit(solution)/shard_map/ppermute | solution.py:1225
  469.3 30.8 %collective-permute-start.72 = (bf16[256,1024]{1,0:T(8,128)(2,1)}, bf16[256,1024]{1,0:T(8,128)(2,1)}, u32[]{:S(2)}, u32[]{:S(2)}) collective-permute-start(bf16[256,1024]{1,0:T(8,128)(2,1)} %maximum_select_fusion.10), channel_id=1, source_target_pairs={{0,8},{8,0},{1,9},{9,1},{2,10},{10,2},{3,11},{11,3},{4,12},{12,4},... | collective-permute-start | bytes 1572872 | tf_op jit(solution)/shard_map/ppermute | solution.py:1225
  (114 other events, 1625.7 us)

commit v4 on v3

--- a/solution.py
+++ b/solution.py
@@ -1118,6 +1118,44 @@
     )(place, mine, other)
 
 
+def unmix_kernel(widths, groups, place_ref, *refs):
+    x, c = place_ref[0], place_ref[1]
+    sources, outs = refs[:4], refs[4:]
+    at = pl.program_id(0)
+    block, core, group = at // (2 * groups), at // groups % 2, at % groups
+    chosen = jnp.where(block == x, 0, 1) + jnp.where(core == c, 0, 2)
+    step = sum(widths)
+    for index, source in enumerate(sources):
+
+        @pl.when(chosen == index)
+        def _(source=source):
+            first = 0
+            for out, count in zip(outs, widths):
+                start = pl.multiple_of(group * step + first, math.gcd(step, count))
+                out[...] = source[:, pl.ds(start, count)].astype(jnp.float32)
+                first += count
+
+
+def unmix(place, near, far, near_other, far_other, widths, groups):
+    rows = near.shape[0]
+    whole = pl.BlockSpec(near.shape, lambda i, place: (0, 0), pipeline_mode=pl.Buffered(1))
+    return pl.pallas_call(
+        functools.partial(unmix_kernel, widths, groups),
+        grid_spec=pltpu.PrefetchScalarGridSpec(
+            num_scalar_prefetch=1,
+            grid=(4 * groups,),
+            in_specs=[whole] * 4,
+            out_specs=[pl.BlockSpec((rows, count), lambda i, place: (0, i)) for count in widths],
+        ),
+        out_shape=[
+            jax.ShapeDtypeStruct((rows, 4 * groups * count), jnp.float32) for count in widths
+        ],
+        compiler_params=pltpu.CompilerParams(vmem_limit_bytes=VMEM_BYTES),
+        cost_estimate=NO_COST,
+        name="unmix",
+    )(place, near, far, near_other, far_other)
+
+
 def copy_kernel(plan, place_ref, *refs):
     sems = refs[-1]
     copies = [
@@ -1462,9 +1500,9 @@
 
     dh_sent = other_half(place, dh_part)
     dh_got = swap(dh_sent, "c")
-    mark = down_piece.step(dh_sent)
+    mark = near_piece.step(dh_sent)
+    mark = down_piece.step(mark)
     mark = far_piece.step(mark)
-    mark = near_piece.step(mark)
     input_sum, gain_one_sum = norm_gradient(
         place, own_tokens, dh_part, hold(dh_got, mark), grad_resid, gain_one, False
     )
@@ -1482,6 +1520,10 @@
 
     def rows_result(piece):
         return piece.step(mark)
+
+    def unmixed(near, far, widths, groups):
+        others = [hold(piece.got, mark) for piece in (near, far)]
+        return unmix(place, near.kept, far.kept, *others, widths, groups)
 
     def columns_result(near, far, widths, groups):
         others = [hold(piece.got, mark) for piece in (near, far)]
@@ -1522,45 +1564,45 @@
     mark = far_piece.step(mark)
     mark = qkv_near_piece.step(mark)
     mark = near_piece.step(mark)
+    mark = gain_step("y", mark)
+    mark = qkv_near_piece.step(mark)
     mark = out_piece.step(mark)
-    mark = gain_step("y", mark)
     input_turned = turn(hold(input_sum, mark))
+    mark = qkv_far_piece.step(mark)
+    mark = qkv_near_piece.step(mark)
     mark = down_piece.step(mark)
-    mark = qkv_near_piece.step(mark)
+    mark = out_piece.step(mark)
+    mark = near_piece.step(mark)
     mark = qkv_far_piece.step(mark)
     mark = far_piece.step(mark)
-    mark = out_piece.step(mark)
-    mark = near_piece.step(mark)
     mark = gain_step("za", mark)
     mark = qkv_far_piece.step(mark)
     mark = qkv_near_piece.step(mark)
     mark = down_piece.step(mark)
+    mark = grad_input = hold(input_turned, mark).astype(f32)
+    mark = out_piece.step(mark)
     mark = far_piece.step(mark)
-    mark = out_piece.step(mark)
-    mark = grad_input = hold(input_turned, mark).astype(f32)
     mark = gain_step("zb", mark)
+    mark = near_piece.step(mark)
     mark = qkv_far_piece.step(mark)
     mark = qkv_near_piece.step(mark)
-    mark = near_piece.step(mark)
+    result_turned = turn(result_start(mark))
     mark = far_piece.step(mark)
-    mark = gain_step("c", mark)
-    result_turned = turn(result_start(mark))
+    mark = down_piece.step(mark)
+    grad_gate_w, grad_up_w = lax.optimization_barrier(
+        unmixed(near_piece, far_piece, [unit_block, unit_block], unit_groups)
+    )
+    mark = grad_up_w
+    mark = out_piece.step(mark)
+    mark = grad_down_w = rows_result(down_piece)
     mark = qkv_far_piece.step(mark)
     mark = qkv_near_piece.step(mark)
-    mark = down_piece.step(mark)
-    grad_gate_w, grad_up_w = columns_result(
-        near_piece, far_piece, [unit_block, unit_block], unit_groups
-    )
-    mark = hold(grad_up_w, grad_gate_w)
+    mark = gain_step("c", mark)
     mark = out_piece.step(mark)
+    mark = result = hold(result_turned, mark)
     mark = qkv_far_piece.step(mark)
-    mark = grad_down_w = rows_result(down_piece)
-    mark = result = hold(result_turned, mark)
+    mark = grad_out_w = rows_result(out_piece)
     mark = gain_step(None, mark)
-    mark = qkv_near_piece.step(mark)
-    mark = out_piece.step(mark)
-    mark = grad_out_w = rows_result(out_piece)
-    mark = qkv_far_piece.step(mark)
     grad_query_w, grad_key_w, grad_value_w = columns_result(
         qkv_near_piece, qkv_far_piece, [group * head_dim, head_dim, head_dim], head_groups
     )

time: 543 us -> 537 us (0.989)
  waiting for transfers between devices: 153 us -> 185 us
  other arithmetic: 68.2 us -> 50.6 us
  starting transfers between devices: 84.6 us -> 69.9 us
  local copies, waits for them, and re-layouts: 33.6 us -> 19 us
  Pallas kernels: 196 us -> 206 us
    ppermute x74, waiting for transfers between devices: 153 us -> 185 us  [swap(): return lax.ppermute(values, axis, [(0, 1), (1, 0)])]
    ppermute x74, starting transfers between devices: 80.6 us -> 65.9 us  [swap(): return lax.ppermute(values, axis, [(0, 1), (1, 0)])]
    unnamed x145 -> x110, local copies, waits for them, and re-layouts: 17.7 us -> 6.69 us
    pallas_call x0 -> x1, Pallas kernels: none -> 10.3 us  [unmix(): pl.pallas_call(functools.partial(unmix_kernel, widths, groups), grid_spec...]
    convert_element_type x5 -> x3, other arithmetic: 14.6 us -> 5.67 us  [columns_result(): results.append(jnp.concatenate(pieces, axis=1).astype(f32))]
    select_n x14, other arithmetic: 17.6 us -> 10.8 us  [ordered(): jnp.where(first, jnp.concatenate([mine, other], axis=axis), jnp.concatena...]
  transfers between devices with their start and end apart: 78 -> 78, of which waited for: 28 -> 29; matrix products, arithmetic and copies ran while one was open for 15% -> 9% of each run, Pallas kernels for 32% -> 34%
where the time goes in v4:
time: 537 us; the launch traced here: 532 us
  Pallas kernels  206 us (38%)
  waiting for transfers between devices  185 us (34%)
  starting transfers between devices  69.9 us (13%)
  other arithmetic  50.6 us (9%)
  local copies, waits for them, and re-layouts  19 us (4%)
    ppermute x74, waiting for transfers between devices, swap(): return lax.ppermute(values, axis, [(0, 1), (1, 0)])  185 us
    ppermute x74, starting transfers between devices, swap(): return lax.ppermute(values, axis, [(0, 1), (1, 0)])  65.9 us
    pallas_call x2, Pallas kernels, mlp(): pl.pallas_call(functools.partial(mlp_kernel, block=block, first=first), g...  51.4 us
    pallas_call x2, Pallas kernels, attend_back(): pl.pallas_call(functools.partial(attend_back_kernel, first=first), grid=(...  45.7 us
    pallas_call x1, Pallas kernels, attend(): pl.pallas_call(attend_kernel, grid_spec=pltpu.PrefetchScalarGridSpec(num_...  28.3 us
    add x23, other arithmetic, step(): values = self.kept + got  17.7 us
    pallas_call x5, Pallas kernels, copied(): pl.pallas_call(functools.partial(copy_kernel, plan), in_specs=[pl.BlockSp...  15.4 us
    pallas_call x2, Pallas kernels, norm_gradient(): pl.pallas_call(norm_back_kernel, grid_spec=pltpu.PrefetchScalarGridSpec(n...  11.1 us
  transfers between devices with their start and end apart: 78, of which 29 were waited for; matrix products, arithmetic and copies ran while one was open for 9% of the time, Pallas kernels for 34%

profile of v4, /device:TPU:0, one launch (start us, length us, event | category | flops | bytes accessed | tf_op | source)
XLA Modules:
  0.0 531.8 jit_solution(15218933484178351434)
XLA Ops:
  27.5 11.0 %collective-permute-done.2.near_z = bf16[128,2048]{1,0:T(8,128)(2,1)S(1)} collective-permute-done((bf16[128,2048]{1,0:T(8,128)(2,1)S(1)}, bf16[128,2048]{1,0:T(8,128)(2,1)S(1)}, u32[]{:S(2)}, u32[]{:S(2)}) %collective-permute-start.2) | collective-permute-done | bytes 524320 | tf_op jit(solution)/shard_map/ppermute | solution.py:1263
  45.6 17.8 %collective-permute-done.5.refs_1_ = bf16[128,1024]{1,0:T(8,128)(2,1)S(1)} collective-permute-done((bf16[128,1024]{1,0:T(8,128)(2,1)S(1)}, bf16[128,1024]{1,0:T(8,128)(2,1)S(1)}, u32[]{:S(2)}, u32[]{:S(2)}) %collective-permute-start.5) | collective-permute-done | bytes 262176 | tf_op jit(solution)/shard_map/ppermute | solution.py:1263
  88.3 28.3 %attend.1 = (bf16[1024,1024]{1,0:T(8,128)(2,1)}, bf16[1024,1024]{1,0:T(8,128)(2,1)}, bf16[1024,512]{1,0:T(8,128)(2,1)}, f32[4,2,1024]{2,1,0:T(2,128)}, f32[1024,2048]{1,0:T(8,128)}, /*index=5*/bf16[1024,2048]{1,0:T(8,128)(2,1)}) custom-call(s32[4]{0:T(128)} %pad_add_fusion.place_ref, bf16[1024,1024]{1,0:T(8,128)(2,1)} %norm_first.1.h_ref, ...), custom_call_target="tpu_custom_call" | custom-call | tf_op jit(solution)/shard_map/attend/pallas_call | solution.py:575
  120.3 7.2 %out_forward.1 = (bf16[512,1024]{1,0:T(8,128)(2,1)}, f32[512,1024]{1,0:T(8,128)}) custom-call(s32[4]{0:T(128)} %pad_add_fusion.place_ref, bf16[1024,1024]{1,0:T(8,128)(2,1)} %get-tuple-element.162.o_ref, bf16[1024,1024]{1,0:T(8,128)(2,1)} %join_rows.1.w_ref), custom_call_target="tpu_custom_call" | custom-call | tf_op jit(solution)/shard_map/out_forward/pallas_call | solution.py:651
  138.1 17.9 %collective-permute-done.19.rest_8_ = bf16[192,1024]{1,0:T(8,128)(2,1)} collective-permute-done((bf16[192,1024]{1,0:T(8,128)(2,1)S(1)}, bf16[192,1024]{1,0:T(8,128)(2,1)}, u32[]{:S(2)}, u32[]{:S(2)}) %collective-permute-start.19) | collective-permute-done | bytes 393248 | tf_op jit(solution)/shard_map/ppermute | solution.py:1263
  162.8 24.7 %mlp.2 = (bf16[512,1536]{1,0:T(8,128)(2,1)}, bf16[512,1536]{1,0:T(8,128)(2,1)}, bf16[768,1024]{1,0:T(8,128)(2,1)}, f32[1024,1024]{1,0:T(8,128)}, f32[1024,1024]{1,0:T(8,128)}) custom-call(s32[4]{0:T(128)} %pad_add_fusion.place_ref, bf16[512,1024]{1,0:T(8,128)(2,1)} %get-tuple-element.167.hm_ref, bf16[512,1024]{1,0:T(8,128)(2,1)} %copy-done.4, ...), custom_call_target="tpu_custom_call" | custom-call | tf_op jit(solution)/shard_map/mlp/pallas_call | solution.py:994
  191.0 26.7 %mlp.3 = (bf16[512,1536]{1,0:T(8,128)(2,1)}, bf16[512,1536]{1,0:T(8,128)(2,1)}, bf16[768,1024]{1,0:T(8,128)(2,1)}, f32[1024,1024]{1,0:T(8,128)}, f32[1024,1024]{1,0:T(8,128)}) custom-call(s32[4]{0:T(128)} %pad_add_fusion.place_ref, bf16[512,1024]{1,0:T(8,128)(2,1)} %get-tuple-element.167.hm_ref, bf16[512,1024]{1,0:T(8,128)(2,1)} %copy-done.4, ...), custom_call_target="tpu_custom_call" | custom-call | tf_op jit(solution)/shard_map/mlp/pallas_call | solution.py:994
  225.5 5.8 %norm_gradient.2 = (f32[512,1024]{1,0:T(8,128)}, bf16[512,1024]{1,0:T(8,128)(2,1)}, f32[1,1024]{1,0:T(1,128)}) custom-call(s32[4]{0:T(128)} %pad_add_fusion.place_ref, f32[512,1024]{1,0:T(8,128)} %get-tuple-element.165.values_ref, f32[1024,1024]{1,0:T(8,128)} %get-tuple-element.177.whole_ref.part_ref, bf16[512,1024]{1,0:T(8,128)(2,1)} %copy-done.23, ...), custom_call_target="tpu_custom_call" | custom-call | tf_op jit(solution)/shard_map/norm_gradient/pallas_call | solution.py:806
  234.4 8.9 %out_back.1 = (bf16[1024,1024]{1,0:T(8,128)(2,1)}, bf16[512,1024]{1,0:T(8,128)(2,1)}, bf16[512,1024]{1,0:T(8,128)(2,1)}) custom-call(s32[4]{0:T(128)} %pad_add_fusion.place_ref, bf16[512,1024]{1,0:T(8,128)(2,1)} %get-tuple-element.180.mine_ref, bf16[512,1024]{1,0:T(8,128)(2,1)} %collective-permute-done.27.other_ref, ...), custom_call_target="tpu_custom_call" | custom-call | tf_op jit(solution)/shard_map/out_back/pallas_call | solution.py:861
  248.4 22.4 %attend_back.2 = (bf16[512,1024]{1,0:T(8,128)(2,1)}, bf16[512,1024]{1,0:T(8,128)(2,1)}, f32[2,8,128]{2,1,0:T(8,128)}, f32[1024,1024]{1,0:T(8,128)}) custom-call(bf16[1024,1024]{1,0:T(8,128)(2,1)} %get-tuple-element.172.q_ref, bf16[1024,512]{1,0:T(8,128)(2,1)} %get-tuple-element.173.k_ref, f32[1024,2048]{1,0:T(8,128)} %get-tuple-element.174.qkv_ref, ...), custom_call_target="tpu_custom_call" | custom-call | tf_op jit(solution)/shard_map/attend_back/pallas_call | solution.py:720
  279.8 23.3 %attend_back.3 = (bf16[512,1024]{1,0:T(8,128)(2,1)}, bf16[512,1024]{1,0:T(8,128)(2,1)}, f32[2,8,128]{2,1,0:T(8,128)}, f32[1024,1024]{1,0:T(8,128)}) custom-call(bf16[1024,1024]{1,0:T(8,128)(2,1)} %get-tuple-element.172.q_ref, bf16[1024,512]{1,0:T(8,128)(2,1)} %get-tuple-element.173.k_ref, f32[1024,2048]{1,0:T(8,128)} %get-tuple-element.174.qkv_ref, ...), custom_call_target="tpu_custom_call" | custom-call | tf_op jit(solution)/shard_map/attend_back/pallas_call | solution.py:720
  313.4 5.3 norm_gradient.3
  335.6 5.6 %collective-permute-done.41 = bf16[128,1536]{1,0:T(8,128)(2,1)} collective-permute-done((bf16[128,1536]{1,0:T(8,128)(2,1)S(1)}, bf16[128,1536]{1,0:T(8,128)(2,1)}, u32[]{:S(2)}, u32[]{:S(2)}) %collective-permute-start.41) | collective-permute-done | bytes 393248 | tf_op jit(solution)/shard_map/ppermute | solution.py:1263
  342.4 10.4 %collective-permute-done.40 = f32[16,128]{1,0:T(8,128)S(1)} collective-permute-done((f32[16,128]{1,0:T(8,128)S(1)}, f32[16,128]{1,0:T(8,128)S(1)}, u32[]{:S(2)}, u32[]{:S(2)}) %collective-permute-start.40) | collective-permute-done | bytes 8224 | tf_op jit(solution)/shard_map/ppermute | solution.py:1263
  354.7 6.2 %collective-permute-done.44 = bf16[256,1024]{1,0:T(8,128)(2,1)} collective-permute-done((bf16[256,1024]{1,0:T(8,128)(2,1)}, bf16[256,1024]{1,0:T(8,128)(2,1)}, u32[]{:S(2)}, u32[]{:S(2)}) %collective-permute-start.44) | collective-permute-done | bytes 524320 | tf_op jit(solution)/shard_map/ppermute | solution.py:1263
  367.6 7.2 %collective-permute-done.42 = bf16[128,1024]{1,0:T(8,128)(2,1)S(1)} collective-permute-done((bf16[128,1024]{1,0:T(8,128)(2,1)S(1)}, bf16[128,1024]{1,0:T(8,128)(2,1)S(1)}, u32[]{:S(2)}, u32[]{:S(2)}) %collective-permute-start.42) | collective-permute-done | bytes 262176 | tf_op jit(solution)/shard_map/ppermute | solution.py:1263
  379.0 7.8 %collective-permute-done.48 = bf16[128,1024]{1,0:T(8,128)(2,1)} collective-permute-done((bf16[128,1024]{1,0:T(8,128)(2,1)S(1)}, bf16[128,1024]{1,0:T(8,128)(2,1)}, u32[]{:S(2)}, u32[]{:S(2)}) %collective-permute-start.48) | collective-permute-done | bytes 262176 | tf_op jit(solution)/shard_map/ppermute | solution.py:1263
  401.6 14.3 %collective-permute-done.50 = bf16[128,1024]{1,0:T(8,128)(2,1)S(1)} collective-permute-done((bf16[128,1024]{1,0:T(8,128)(2,1)S(1)}, bf16[128,1024]{1,0:T(8,128)(2,1)S(1)}, u32[]{:S(2)}, u32[]{:S(2)}) %collective-permute-start.50) | collective-permute-done | bytes 262176 | tf_op jit(solution)/shard_map/ppermute | solution.py:1263
  422.3 7.4 %collective-permute-done.58 = bf16[128,1024]{1,0:T(8,128)(2,1)S(1)} collective-permute-done((bf16[128,1024]{1,0:T(8,128)(2,1)S(1)}, bf16[128,1024]{1,0:T(8,128)(2,1)S(1)}, u32[]{:S(2)}, u32[]{:S(2)}) %collective-permute-start.58) | collective-permute-done | bytes 262176 | tf_op jit(solution)/shard_map/ppermute | solution.py:1263
  433.3 22.9 %collective-permute-done.56 = f32[16,128]{1,0:T(8,128)S(1)} collective-permute-done((f32[16,128]{1,0:T(8,128)S(1)}, f32[16,128]{1,0:T(8,128)S(1)}, u32[]{:S(2)}, u32[]{:S(2)}) %collective-permute-start.56) | collective-permute-done | bytes 8224 | tf_op jit(solution)/shard_map/ppermute | solution.py:1263
  466.4 7.5 %collective-permute-done.66 = bf16[384,1024]{1,0:T(8,128)(2,1)S(1)} collective-permute-done((bf16[384,1024]{1,0:T(8,128)(2,1)S(1)}, bf16[384,1024]{1,0:T(8,128)(2,1)S(1)}, u32[]{:S(2)}, u32[]{:S(2)}) %collective-permute-start.66) | collective-permute-done | bytes 786464 | tf_op jit(solution)/shard_map/ppermute | solution.py:1263
  480.0 10.3 %unmix.1 = (f32[512,3072]{1,0:T(8,128)}, f32[512,3072]{1,0:T(8,128)}) custom-call(s32[4]{0:T(128)} %pad_add_fusion.place_ref, bf16[512,1536]{1,0:T(8,128)(2,1)} %maximum_select_fusion.refs_0_, bf16[512,1536]{1,0:T(8,128)(2,1)} %maximum_select_fusion.1.refs_1_, bf16[512,1536]{1,0:T(8,128)(2,1)} %collective-permute-done.65.refs_2_, ...), custom_call_target="tpu_custom_call" | custom-call | tf_op jit(solution)/shard_map/unmix/pallas_call | solution.py:1142
  493.6 5.5 %join.2 = f32[1536,1024]{1,0:T(8,128)} custom-call(s32[4]{0:T(128)} %pad_add_fusion.place_ref, bf16[768,1024]{1,0:T(8,128)(2,1)} %maximum_select_fusion.2.mine_ref, bf16[768,1024]{1,0:T(8,128)(2,1)} %collective-permute-done.72.other_ref), custom_call_target="tpu_custom_call" | custom-call | tf_op jit(solution)/shard_map/join/pallas_call | solution.py:1103
  507.1 8.8 %collective-permute-done.75 = bf16[256,1024]{1,0:T(8,128)(2,1)S(1)} collective-permute-done((bf16[256,1024]{1,0:T(8,128)(2,1)S(1)}, bf16[256,1024]{1,0:T(8,128)(2,1)S(1)}, u32[]{:S(2)}, u32[]{:S(2)}) %collective-permute-start.75) | collective-permute-done | bytes 524320 | tf_op jit(solution)/shard_map/ppermute | solution.py:1263
  (360 shorter events, 216.7 us)
Async XLA Ops:
  66.3 54.0 %collective-permute-start.10 = (bf16[128,3072]{1,0:T(8,128)(2,1)}, bf16[128,3072]{1,0:T(8,128)(2,1)S(1)}, u32[]{:S(2)}, u32[]{:S(2)}) collective-permute-start(bf16[128,3072]{1,0:T(8,128)(2,1)} %get-tuple-element.156), channel_id=1, source_target_pairs={{0,1},{1,0},{2,3},{3,2},{4,5},{5,4},{6,7},{7,6},{8,9},{9,8},{10,11... | collective-permute-start | bytes 2359304 | tf_op jit(solution)/shard_map/ppermute | solution.py:1263
  67.6 52.7 %collective-permute-start.11 = (bf16[128,3072]{1,0:T(8,128)(2,1)}, bf16[128,3072]{1,0:T(8,128)(2,1)S(1)}, u32[]{:S(2)}, u32[]{:S(2)}) collective-permute-start(bf16[128,3072]{1,0:T(8,128)(2,1)} %get-tuple-element.158), channel_id=1, source_target_pairs={{0,1},{1,0},{2,3},{3,2},{4,5},{5,4},{6,7},{7,6},{8,9},{9,8},{10,11... | collective-permute-start | bytes 2359304 | tf_op jit(solution)/shard_map/ppermute | solution.py:1263
  76.5 40.1 %collective-permute-start.12 = (bf16[192,1024]{1,0:T(8,128)(2,1)}, bf16[192,1024]{1,0:T(8,128)(2,1)S(1)}, u32[]{:S(2)}, u32[]{:S(2)}) collective-permute-start(bf16[192,1024]{1,0:T(8,128)(2,1)} %get-tuple-element.159), channel_id=1, source_target_pairs={{0,1},{1,0},{2,3},{3,2},{4,5},{5,4},{6,7},{7,6},{8,9},{9,8},{10,11... | collective-permute-start | bytes 1179656 | tf_op jit(solution)/shard_map/ppermute | solution.py:1263
  77.7 42.5 %collective-permute-start.13 = (bf16[192,1024]{1,0:T(8,128)(2,1)}, bf16[192,1024]{1,0:T(8,128)(2,1)}, u32[]{:S(2)}, u32[]{:S(2)}) collective-permute-start(bf16[192,1024]{1,0:T(8,128)(2,1)} %get-tuple-element.161), channel_id=1, source_target_pairs={{0,1},{1,0},{2,3},{3,2},{4,5},{5,4},{6,7},{7,6},{8,9},{9,8},{10,11... | collective-permute-start | bytes 1179656 | tf_op jit(solution)/shard_map/ppermute | solution.py:1263
  78.6 52.6 %collective-permute-start.22 = (bf16[512,1024]{1,0:T(8,128)(2,1)S(1)}, bf16[512,1024]{1,0:T(8,128)(2,1)S(1)}, u32[]{:S(2)}, u32[]{:S(2)}) collective-permute-start(bf16[512,1024]{1,0:T(8,128)(2,1)S(1)} %copy-done.21), channel_id=1, source_target_pairs={{1,2},{2,1},{5,6},{6,5},{9,10},{10,9},{13,14},{14,13},{17,18},{18,... | collective-permute-start | bytes 3145736 | tf_op jit(solution)/shard_map/ppermute | solution.py:1329
  127.5 29.7 %collective-permute-start.17 = (bf16[128,3072]{1,0:T(8,128)(2,1)S(1)}, bf16[128,3072]{1,0:T(8,128)(2,1)S(1)}, u32[]{:S(2)}, u32[]{:S(2)}) collective-permute-start(bf16[128,3072]{1,0:T(8,128)(2,1)S(1)} %collective-permute-done.10.rest_2_), channel_id=1, source_target_pairs={{0,4},{4,0},{1,5},{5,1},{2,6},{6,2},{3,7},{7,3},{8,12},{12,8},{9,1... | collective-permute-start | bytes 2359304 | tf_op jit(solution)/shard_map/ppermute | solution.py:1263
  129.1 28.2 %collective-permute-start.18 = (bf16[128,3072]{1,0:T(8,128)(2,1)S(1)}, bf16[128,3072]{1,0:T(8,128)(2,1)S(1)}, u32[]{:S(2)}, u32[]{:S(2)}) collective-permute-start(bf16[128,3072]{1,0:T(8,128)(2,1)S(1)} %collective-permute-done.11.rest_3_), channel_id=1, source_target_pairs={{0,8},{8,0},{1,9},{9,1},{2,10},{10,2},{3,11},{11,3},{4,12},{12,4},... | collective-permute-start | bytes 2359304 | tf_op jit(solution)/shard_map/ppermute | solution.py:1263
  188.7 28.9 %collective-permute-start.24 = (bf16[384,1024]{1,0:T(8,128)(2,1)S(1)}, bf16[384,1024]{1,0:T(8,128)(2,1)S(1)}, u32[]{:S(2)}, u32[]{:S(2)}) collective-permute-start(bf16[384,1024]{1,0:T(8,128)(2,1)S(1)} %constant_dynamic-slice_fusion.23), channel_id=1, source_target_pairs={{0,4},{4,0},{1,5},{5,1},{2,6},{6,2},{3,7},{7,3},{8,12},{12,8},{9,1... | collective-permute-start | bytes 2359304 | tf_op jit(solution)/shard_map/ppermute | solution.py:1263
  189.3 42.0 %collective-permute-start.26 = (bf16[512,1536]{1,0:T(8,128)(2,1)}, bf16[512,1536]{1,0:T(8,128)(2,1)S(1)}, u32[]{:S(2)}, u32[]{:S(2)}) collective-permute-start(bf16[512,1536]{1,0:T(8,128)(2,1)} %get-tuple-element.179), channel_id=1, source_target_pairs={{0,1},{1,0},{2,3},{3,2},{4,5},{5,4},{6,7},{7,6},{8,9},{9,8},{10,11... | collective-permute-start | bytes 4718600 | tf_op jit(solution)/shard_map/ppermute | solution.py:1263
  231.5 39.3 %collective-permute-start.29 = (bf16[512,1536]{1,0:T(8,128)(2,1)}, bf16[512,1536]{1,0:T(8,128)(2,1)}, u32[]{:S(2)}, u32[]{:S(2)}) collective-permute-start(bf16[512,1536]{1,0:T(8,128)(2,1)} %get-tuple-element.188), channel_id=1, source_target_pairs={{0,1},{1,0},{2,3},{3,2},{4,5},{5,4},{6,7},{7,6},{8,9},{9,8},{10,11... | collective-permute-start | bytes 4718600 | tf_op jit(solution)/shard_map/ppermute | solution.py:1263
  232.8 38.0 %collective-permute-start.30 = (bf16[384,1024]{1,0:T(8,128)(2,1)}, bf16[384,1024]{1,0:T(8,128)(2,1)}, u32[]{:S(2)}, u32[]{:S(2)}) collective-permute-start(bf16[384,1024]{1,0:T(8,128)(2,1)} %constant_dynamic-slice_fusion.20), channel_id=1, source_target_pairs={{0,4},{4,0},{1,5},{5,1},{2,6},{6,2},{3,7},{7,3},{8,12},{12,8},{9,1... | collective-permute-start | bytes 2359304 | tf_op jit(solution)/shard_map/ppermute | solution.py:1263
  247.4 56.5 %collective-permute-start.34 = (bf16[384,1024]{1,0:T(8,128)(2,1)}, bf16[384,1024]{1,0:T(8,128)(2,1)}, u32[]{:S(2)}, u32[]{:S(2)}) collective-permute-start(bf16[384,1024]{1,0:T(8,128)(2,1)} %dynamic-slice_add_fusion), channel_id=1, source_target_pairs={{0,1},{1,0},{2,3},{3,2},{4,5},{5,4},{6,7},{7,6},{8,9},{9,8},{10,11... | collective-permute-start | bytes 2359304 | tf_op jit(solution)/shard_map/ppermute | solution.py:1263
  273.6 30.2 %collective-permute-start.33 = (bf16[256,1536]{1,0:T(8,128)(2,1)}, bf16[256,1536]{1,0:T(8,128)(2,1)S(1)}, u32[]{:S(2)}, u32[]{:S(2)}) collective-permute-start(bf16[256,1536]{1,0:T(8,128)(2,1)} %get-tuple-element.269), channel_id=1, source_target_pairs={{0,8},{8,0},{1,9},{9,1},{2,10},{10,2},{3,11},{11,3},{4,12},{12,4},... | collective-permute-start | bytes 2359304 | tf_op jit(solution)/shard_map/ppermute | solution.py:1263
  277.8 45.9 %collective-permute-start.36 = (bf16[512,1024]{1,0:T(8,128)(2,1)}, bf16[512,1024]{1,0:T(8,128)(2,1)}, u32[]{:S(2)}, u32[]{:S(2)}) collective-permute-start(bf16[512,1024]{1,0:T(8,128)(2,1)} %get-tuple-element.210), channel_id=1, source_target_pairs={{0,1},{1,0},{2,3},{3,2},{4,5},{5,4},{6,7},{7,6},{8,9},{9,8},{10,11... | collective-permute-start | bytes 3145736 | tf_op jit(solution)/shard_map/ppermute | solution.py:1263
  278.8 51.9 %collective-permute-start.31 = (bf16[512,1024]{1,0:T(8,128)(2,1)}, bf16[512,1024]{1,0:T(8,128)(2,1)S(1)}, u32[]{:S(2)}, u32[]{:S(2)}) collective-permute-start(bf16[512,1024]{1,0:T(8,128)(2,1)} %get-tuple-element.199), channel_id=1, source_target_pairs={{0,1},{1,0},{2,3},{3,2},{4,5},{5,4},{6,7},{7,6},{8,9},{9,8},{10,11... | collective-permute-start | bytes 3145736 | tf_op jit(solution)/shard_map/ppermute | solution.py:1263
  312.4 49.8 %collective-permute-start.43 = (bf16[512,1024]{1,0:T(8,128)(2,1)}, bf16[512,1024]{1,0:T(8,128)(2,1)}, u32[]{:S(2)}, u32[]{:S(2)}) collective-permute-start(bf16[512,1024]{1,0:T(8,128)(2,1)} %get-tuple-element.225), channel_id=1, source_target_pairs={{0,1},{1,0},{2,3},{3,2},{4,5},{5,4},{6,7},{7,6},{8,9},{9,8},{10,11... | collective-permute-start | bytes 3145736 | tf_op jit(solution)/shard_map/ppermute | solution.py:1263
  333.6 27.3 %collective-permute-start.44 = (bf16[256,1024]{1,0:T(8,128)(2,1)}, bf16[256,1024]{1,0:T(8,128)(2,1)}, u32[]{:S(2)}, u32[]{:S(2)}) collective-permute-start(bf16[256,1024]{1,0:T(8,128)(2,1)} %get-tuple-element.291), channel_id=1, source_target_pairs={{0,8},{8,0},{1,9},{9,1},{2,10},{10,2},{3,11},{11,3},{4,12},{12,4},... | collective-permute-start | bytes 1572872 | tf_op jit(solution)/shard_map/ppermute | solution.py:1263
  341.2 34.7 %collective-permute-start.49 = (bf16[192,1024]{1,0:T(8,128)(2,1)S(1)}, bf16[192,1024]{1,0:T(8,128)(2,1)}, u32[]{:S(2)}, u32[]{:S(2)}) collective-permute-start(bf16[192,1024]{1,0:T(8,128)(2,1)S(1)} %add.172), channel_id=1, source_target_pairs={{0,16},{16,0},{1,17},{17,1},{2,18},{18,2},{3,19},{19,3},{4,20},{20... | collective-permute-start | bytes 1179656 | tf_op jit(solution)/shard_map/ppermute | solution.py:1263
  352.8 37.0 %collective-permute-start.47 = (bf16[128,1536]{1,0:T(8,128)(2,1)S(1)}, bf16[128,1536]{1,0:T(8,128)(2,1)}, u32[]{:S(2)}, u32[]{:S(2)}) collective-permute-start(bf16[128,1536]{1,0:T(8,128)(2,1)S(1)} %add.177), channel_id=1, source_target_pairs={{0,8},{8,0},{1,9},{9,1},{2,10},{10,2},{3,11},{11,3},{4,12},{12,4},... | collective-permute-start | bytes 1179656 | tf_op jit(solution)/shard_map/ppermute | solution.py:1263
  363.9 55.5 %collective-permute-start.59 = (bf16[512,1024]{1,0:T(8,128)(2,1)}, bf16[512,1024]{1,0:T(8,128)(2,1)}, u32[]{:S(2)}, u32[]{:S(2)}) collective-permute-start(bf16[512,1024]{1,0:T(8,128)(2,1)} %get-tuple-element.237), channel_id=1, source_target_pairs={{1,2},{2,1},{5,6},{6,5},{9,10},{10,9},{13,14},{14,13},{17,18},{18,... | collective-permute-start | bytes 3145736 | tf_op jit(solution)/shard_map/ppermute | solution.py:1329
  386.8 31.1 %collective-permute-start.60 = (bf16[192,1024]{1,0:T(8,128)(2,1)S(1)}, bf16[192,1024]{1,0:T(8,128)(2,1)}, u32[]{:S(2)}, u32[]{:S(2)}) collective-permute-start(bf16[192,1024]{1,0:T(8,128)(2,1)S(1)} %add.183), channel_id=1, source_target_pairs={{0,8},{8,0},{1,9},{9,1},{2,10},{10,2},{3,11},{11,3},{4,12},{12,4},... | collective-permute-start | bytes 1179656 | tf_op jit(solution)/shard_map/ppermute | solution.py:1263
  400.7 56.3 %collective-permute-start.55 = (bf16[256,1536]{1,0:T(8,128)(2,1)S(1)}, bf16[256,1536]{1,0:T(8,128)(2,1)S(1)}, u32[]{:S(2)}, u32[]{:S(2)}) collective-permute-start(bf16[256,1536]{1,0:T(8,128)(2,1)S(1)} %maximum_select_fusion.6), channel_id=1, source_target_pairs={{0,4},{4,0},{1,5},{5,1},{2,6},{6,2},{3,7},{7,3},{8,12},{12,8},{9,1... | collective-permute-start | bytes 2359304 | tf_op jit(solution)/shard_map/ppermute | solution.py:1263
  429.9 34.7 %collective-permute-start.64 = (bf16[256,1536]{1,0:T(8,128)(2,1)S(1)}, bf16[256,1536]{1,0:T(8,128)(2,1)S(1)}, u32[]{:S(2)}, u32[]{:S(2)}) collective-permute-start(bf16[256,1536]{1,0:T(8,128)(2,1)S(1)} %maximum_select_fusion.8), channel_id=1, source_target_pairs={{0,8},{8,0},{1,9},{9,1},{2,10},{10,2},{3,11},{11,3},{4,12},{12,4},... | collective-permute-start | bytes 2359304 | tf_op jit(solution)/shard_map/ppermute | solution.py:1263
  432.0 28.8 %collective-permute-start.53 = (bf16[128,1024]{1,0:T(8,128)(2,1)S(1)}, bf16[128,1024]{1,0:T(8,128)(2,1)S(1)}, u32[]{:S(2)}, u32[]{:S(2)}) collective-permute-start(bf16[128,1024]{1,0:T(8,128)(2,1)S(1)} %add.189), channel_id=1, source_target_pairs={{0,8},{8,0},{1,9},{9,1},{2,10},{10,2},{3,11},{11,3},{4,12},{12,4},... | collective-permute-start | bytes 786440 | tf_op jit(solution)/shard_map/ppermute | solution.py:1263
  (102 other events, 1469.9 us)
